TPU v7x, 512 devices: a whole 4x8x8 slice. The times are simulated.
512 devices in a mesh: section: 64 (over x, z, y_hi), tp: 8 (over y_lo, core).
Axes of the slice: x: 4, y: 8 (y_hi: 2, y_lo: 4; y = y_hi * 4 + y_lo), z: 8, core: 2. Of those that a mesh axis runs over, the one named last changes fastest.
Arguments:
- hidden_in: bfloat16 [8192, 8192], P('section', 'tp')
- grad_sent: bfloat16 [8192, 8192], P('section', 'tp'), may hold values from -1.25 to 1.25
- value_grad: bfloat16 [8192, 1024], P('section', 'tp'), may hold values from -4 to 4
- value_weight: bfloat16 [524288, 1024], P('section', 'tp'), may hold values from -0.0625 to 0.0625
- rotation: bfloat16 [8192, 1024], P('section', 'tp'), may hold values from -0.5 to 0.5
- act_scale: float32 [64, 8192], P('section', 'tp'), may hold values from 0.1 to 0.6
- outliers: int32 [64, 128], P('section'), may hold values from 0 to 8191, as said below
Outputs:
- emitted: bfloat16 [8192, 8192], P('section', 'tp')
- r1_grad: float32 [4096, 8192], P('tp', 'section')
- r2_grad: float32 [8192, 1024], P('section', 'tp')
Inputs may be any that keep to these rules, and one draw needn't show every extreme that they name: `outliers`: each row holds 128 distinct column indices.
All inputs are finite; a program needn't handle non-finite values.
Results may differ from a plain program's by a relative error of at most 0.019.
Values may be sent and summed in bfloat16 or wider, within the bound.
No kernel may reach another device: no remote copies, remote signals or barrier semaphores. Data moves between devices by JAX's collectives and lax.ppermute only.
A program may use at most 64 MiB of HBM per device.

v0:
```python
import math

import jax
import jax.numpy as jnp
from jax import lax
from jax.sharding import PartitionSpec as P

ROWS_OUT = 4096


NORM_EPS = 1e-05
SCALE_FLOOR = 1e-06
TWO_PI = 2.0 * math.pi


def passed_along(value, axis, steps):
    count = lax.axis_size(axis)
    pairs = [(source, (source + steps) % count) for source in range(count)]
    return lax.ppermute(value, axis, pairs)


def soft_quant(values, step_size):
    scaled = values / step_size
    shifted = scaled - jnp.sin(TWO_PI * scaled) / TWO_PI
    return step_size * 7.0 * jnp.tanh(shifted / 7.0)


def clip_slope(values, step_size):
    bounded = jnp.tanh(values / (7.0 * step_size))
    return 1.0 - bounded * bounded


def local(hidden_in, grad_sent, value_grad, value_weight, rotation, act_scale, outliers):
    token_count, local_width = hidden_in.shape
    full_width = value_weight.shape[0]
    head_dim = rotation.shape[0]
    local_cols = rotation.shape[1]
    heads_dev = local_cols // head_dim
    incoming = passed_along(grad_sent, "section", -1)
    offset = lax.axis_index("tp") * local_width
    outlier_cols = outliers[0]
    local_ids = offset + jnp.arange(local_width, dtype=jnp.int32)
    outlier_mask = jnp.any(local_ids[:, None] == outlier_cols[None, :], axis=1)[None, :]
    stream_f = hidden_in.astype(jnp.float32)
    squares = lax.psum(jnp.sum(stream_f * stream_f, axis=1), "tp")
    inverse = lax.rsqrt(squares[:, None] / full_width + NORM_EPS)
    normed = stream_f * inverse
    quant_local = jnp.where(outlier_mask, normed, soft_quant(normed, act_scale)).astype(
        jnp.bfloat16
    )
    quant_all = lax.all_gather(quant_local, "tp", axis=1, tiled=True)
    weight_heads = value_weight.reshape(full_width, heads_dev, head_dim)
    rotor_heads = rotation.reshape(head_dim, heads_dev, head_dim)
    rotated = jnp.einsum(
        "dhk,khj->dhj", weight_heads, rotor_heads, preferred_element_type=jnp.float32
    ).astype(jnp.bfloat16)
    wstep = jnp.max(jnp.abs(rotated.astype(jnp.float32)), axis=0) / 7.0 + SCALE_FLOOR
    wquant = soft_quant(rotated.astype(jnp.float32), wstep).astype(jnp.bfloat16)
    value_heads = value_grad.reshape(token_count, heads_dev, head_dim)
    weight_block = wquant
    summed = lax.psum_scatter(
        jnp.einsum(
            "dhj,nhj->dn", weight_block, value_heads, preferred_element_type=jnp.float32
        ).astype(jnp.bfloat16),
        "tp",
        scatter_dimension=0,
        tiled=True,
    ).astype(jnp.float32)
    quant_grad = summed.T
    normed_grad = jnp.where(outlier_mask, quant_grad, quant_grad * clip_slope(normed, act_scale))
    emitted = (incoming.astype(jnp.float32) + inverse * normed_grad).astype(jnp.bfloat16)
    rows_local = ROWS_OUT // lax.axis_size("tp")
    weight_block = lax.slice_in_dim(rotated, 0, rows_local * lax.axis_size("tp"), axis=0)
    frame_local = lax.psum_scatter(
        jnp.einsum(
            "dhj,nhj->dn", weight_block, value_heads, preferred_element_type=jnp.float32
        ).astype(jnp.bfloat16),
        "tp",
        scatter_dimension=0,
        tiled=True,
    )
    projected = jnp.dot(quant_all, value_weight, preferred_element_type=jnp.float32).reshape(
        token_count, heads_dev, head_dim
    )
    rotation_grad = jnp.einsum(
        "nhk,nhj->khj",
        projected,
        value_grad.astype(jnp.float32).reshape(token_count, heads_dev, head_dim),
        precision=lax.Precision.HIGHEST,
    ).reshape(head_dim, local_cols)
    columns = lax.all_to_all(quant_all, "section", split_axis=1, concat_axis=0, tiled=True)
    frame_grad = jnp.dot(
        lax.all_gather(frame_local, "section", axis=1, tiled=True),
        columns,
        preferred_element_type=jnp.float32,
    )
    return (emitted, frame_grad, rotation_grad)


def solution(mesh):
    in_specs = (
        P("section", "tp"),
        P("section", "tp"),
        P("section", "tp"),
        P("section", "tp"),
        P("section", "tp"),
        P("section", "tp"),
        P("section", None),
    )
    out_specs = (P("section", "tp"), P("tp", "section"), P("section", "tp"))
    return jax.shard_map(local, mesh=mesh, in_specs=in_specs, out_specs=out_specs, check_vma=False)
```

profile of v0, /device:TPU:8, one launch (start us, length us, event | category | flops | bytes accessed | tf_op | source)
XLA Modules:
  0.0 349.1 jit_solution(7523503010798542142)
XLA Ops:
  7.2 0.0 copy-start
  7.2 0.0 copy-start.4
  7.2 0.0 reduce-scatter.3.cloned.1.call-start
  7.2 1.5 copy-done
  8.8 1.6 fusion.1
  10.3 0.0 copy-start.1
  10.4 1.3 copy-done.1
  11.7 0.0 copy-done.4
  11.7 16.7 %convolution_convert_fusion = bf16[8192,128]{1,0:T(8,128)(2,1)} fusion(bf16[128,128]{1,0:T(8,128)(2,1)S(1)} %copy-done.4, bf16[8192,1,128]{0,2,1:T(8,128)(2,1)S(1)} %get-tuple-element.17, f32[128]{0:T(128)S(1)} %get-tuple-element.15, f32[128]{0:T(128)S(1)} %get-tuple-element.14), kind=kOutput, calls=%fused_computation | convolution fusion | flops 277872640 | bytes 4228096 | tf_op jit(solution)/shard_map/dhj,nhj->dn/dot_general | solution.py:62
  28.3 0.0 reduce-scatter.3.cloned.1.call-update
  28.3 0.0 copy-start.2
  28.3 0.0 copy-start.3
  28.4 0.0 copy-start.6
  28.4 0.0 copy-start.5
  28.4 0.0 reduce-scatter.5.cloned.1.call-start
  28.4 2.7 convolution_convert_fusion.2
  31.1 0.0 reduce-scatter.5.cloned.1.call-update
  31.2 0.0 all-gather.5.cloned.1.call-start
  31.2 0.0 copy-done.2
  31.2 0.2 copy.17
  31.4 17.5 %collective-permute-start = (bf16[128,1024]{0,1:T(8,128)(2,1)S(1)}, bf16[128,1024]{0,1:T(8,128)(2,1)S(1)}, u32[]{:S(2)}, u32[]{:S(2)}) collective-permute-start(bf16[128,1024]{0,1:T(8,128)(2,1)S(1)} %copy.17), channel_id=1, source_target_pairs={{0,504},{8,0},{16,8},{24,16},{32,24},{40,32},{48,40},{56,48},{64,5... | collective-permute-start | bytes 786440 | tf_op jit(solution)/shard_map/ppermute | solution.py:19
  48.9 0.0 copy-done.3
  48.9 0.2 copy.18
  49.1 0.2 fusion.16
  49.3 27.8 %psum.7 = f32[128]{0:T(128)S(1)} all-reduce(f32[128]{0:T(128)S(1)} %fusion.16), channel_id=1, replica_groups=mesh['section'=64,'tp'=8] {'tp'}, use_global_device_ids=true, to_apply=%region_1.0 | all-reduce | flops 128 | bytes 1024 | tf_op jit(solution)/shard_map/psum | solution.py:45
  77.1 0.0 copy-done.6
  77.1 0.4 compare_reduce_fusion
  77.5 0.0 copy-done.5
  77.5 0.0 collective-permute-done
  77.5 4.1 %reduce-scatter.3.cloned.1.call-done = bf16[1024,128]{1,0:T(8,128)(2,1)} async-done(((bf16[8192,128]{1,0:T(8,128)(2,1)}), bf16[1024,128]{1,0:T(8,128)(2,1)}) %reduce-scatter.3.cloned.1.call-update) | async-done | bytes 262160 | tf_op jit(solution)/shard_map/reduce_scatter | solution.py:61
  81.6 4.5 %fusion.15 = (bf16[128,1024]{0,1:T(8,128)(2,1)}, bf16[128,1024]{0,1:T(8,128)(2,1)S(1)}) fusion(bf16[128,1024]{0,1:T(8,128)(2,1)S(1)} %copy.18, f32[1024]{0:T(1024)S(1)} %bitcast.32, f32[1024]{0:T(1024)S(1)} %bitcast.33, f32[128]{0:T(128)S(1)} %add_rsqrt_fusion, pred[1024]{0:T(1024)(128)(4,1)S(1)} %compare_reduce_fusion, ...), kind=kLoop, calls=%fused_computation.24 | loop fusion | flops 2621440 | bytes 1320448 | tf_op jit(solution)/shard_map/convert_element_type | solution.py:48
  86.1 0.0 all-gather.5.cloned.1.call-update
  86.1 0.0 all-gather.3.cloned.1.call-start
  86.2 32.2 %reduce-scatter.5.cloned.1.call-done = bf16[512,128]{1,0:T(8,128)(2,1)} async-done(((bf16[4096,128]{1,0:T(8,128)(2,1)}), bf16[512,128]{1,0:T(8,128)(2,1)}) %reduce-scatter.5.cloned.1.call-update) | async-done | bytes 131088 | tf_op jit(solution)/shard_map/reduce_scatter | solution.py:74
  118.4 0.0 all-gather.3.cloned.1.call-update
  118.4 44.1 %all-gather.5.cloned.1.call-done = bf16[128,8192]{0,1:T(8,128)(2,1)} async-done(((bf16[128,1024]{0,1:T(8,128)(2,1)}), bf16[128,8192]{0,1:T(8,128)(2,1)}) %all-gather.5.cloned.1.call-update) | async-done | bytes 2097168 | tf_op jit(solution)/shard_map/all_gather | solution.py:51
  162.5 4.1 %copy.19 = bf16[128,64,128]{2,0,1:T(8,128)(2,1)} copy(bf16[128,64,128]{0,2,1:T(8,128)(2,1)} %bitcast.31) | data formatting | bytes 4194304 | tf_op jit(solution)/shard_map/all_to_all | solution.py:91
  166.6 13.9 %all-to-all-start = ((bf16[128,64,128]{2,0,1:T(8,128)(2,1)}), bf16[128,64,128]{2,0,1:T(8,128)(2,1)}, u32[]{:S(2)}, u32[]{:S(2)}) async-start(bf16[128,64,128]{2,0,1:T(8,128)(2,1)} %copy.19), calls=%async_computation.2 | async-start | bytes 4194304 | tf_op jit(solution)/shard_map/all_to_all | solution.py:91
  180.4 0.9 copy.20
  181.3 2.3 fusion.24
  183.6 0.9 fusion.25
  184.5 45.0 %all-to-all-done = bf16[128,64,128]{2,0,1:T(8,128)(2,1)} async-done(((bf16[128,64,128]{2,0,1:T(8,128)(2,1)}), bf16[128,64,128]{2,0,1:T(8,128)(2,1)}, u32[]{:S(2)}, u32[]{:S(2)}) %all-to-all-start) | async-done | bytes 2097184 | tf_op jit(solution)/shard_map/all_to_all | solution.py:91
  229.5 106.0 %all-gather.3.cloned.1.call-done = bf16[512,8192]{1,0:T(8,128)(2,1)} async-done(((bf16[512,128]{1,0:T(8,128)(2,1)}), bf16[512,8192]{1,0:T(8,128)(2,1)}) %all-gather.3.cloned.1.call-update) | async-done | bytes 8388624 | tf_op jit(solution)/shard_map/all_gather | solution.py:93
  335.5 7.0 %fusion.23 = f32[512,128]{1,0:T(8,128)} fusion(bf16[512,8192]{1,0:T(8,128)(2,1)} %all-gather.3.cloned.1.call-done, bf16[8192,128]{1,0:T(8,128)(2,1)} %bitcast.11), kind=kOutput, calls=%fused_computation.38 | convolution fusion | flops 1073741824 | bytes 10747904 | tf_op jit(solution)/shard_map/dot_general | solution.py:92
  (4 shorter events, 0.0 us)
Async XLA Ops:
  7.2 1.6 copy-start
  7.2 4.5 %copy-start.4 = (bf16[128,128]{1,0:T(8,128)(2,1)S(1)}, bf16[128,128]{1,0:T(8,128)(2,1)}, u32[]{:S(2)}) copy-start(bf16[128,128]{1,0:T(8,128)(2,1)} %param.9) | copy-start | bytes 98308
  7.2 74.4 %reduce-scatter.3.cloned.1.call-start = ((), (), s32[]{:S(2)}) async-start(), calls=%async_computation.3 | async-start | bytes 2359296 | tf_op jit(solution)/shard_map/reduce_scatter | solution.py:61
  10.3 1.3 copy-start.1
  28.3 2.9 copy-start.2
  28.3 20.6 %copy-start.3 = (bf16[128,1024]{1,0:T(8,128)(2,1)S(1)}, bf16[128,1024]{1,0:T(8,128)(2,1)}, u32[]{:S(2)}) copy-start(bf16[128,1024]{1,0:T(8,128)(2,1)} %param.7) | copy-start | bytes 786436
  28.4 48.7 %copy-start.6 = (s32[1,128]{1,0:T(1,128)S(1)}, s32[1,128]{1,0:T(1,128)}, u32[]{:S(2)}) copy-start(s32[1,128]{1,0:T(1,128)} %param.13) | copy-start | bytes 1540
  28.4 49.1 %copy-start.5 = (f32[1,1024]{1,0:T(1,128)S(1)}, f32[1,1024]{1,0:T(1,128)}, u32[]{:S(2)}) copy-start(f32[1,1024]{1,0:T(1,128)} %param.12) | copy-start | bytes 12292
  28.4 90.0 %reduce-scatter.5.cloned.1.call-start = ((), (), s32[]{:S(2)}) async-start(), calls=%async_computation.4 | async-start | bytes 1179648 | tf_op jit(solution)/shard_map/reduce_scatter | solution.py:74
  31.2 131.3 %all-gather.5.cloned.1.call-start = ((), (), s32[]{:S(2)}) async-start(), calls=%async_computation.6 | async-start | bytes 2359296 | tf_op jit(solution)/shard_map/all_gather | solution.py:51
  31.4 46.1 %collective-permute-start = (bf16[128,1024]{0,1:T(8,128)(2,1)S(1)}, bf16[128,1024]{0,1:T(8,128)(2,1)S(1)}, u32[]{:S(2)}, u32[]{:S(2)}) collective-permute-start(bf16[128,1024]{0,1:T(8,128)(2,1)S(1)} %copy.17), channel_id=1, source_target_pairs={{0,504},{8,0},{16,8},{24,16},{32,24},{40,32},{48,40},{56,48},{64,5... | collective-permute-start | bytes 786440 | tf_op jit(solution)/shard_map/ppermute | solution.py:19
  86.1 249.4 %all-gather.3.cloned.1.call-start = ((), (), s32[]{:S(2)}) async-start(), calls=%async_computation.5 | async-start | bytes 8519680 | tf_op jit(solution)/shard_map/all_gather | solution.py:93
  166.6 62.9 %all-to-all-start = ((bf16[128,64,128]{2,0,1:T(8,128)(2,1)}), bf16[128,64,128]{2,0,1:T(8,128)(2,1)}, u32[]{:S(2)}, u32[]{:S(2)}) async-start(bf16[128,64,128]{2,0,1:T(8,128)(2,1)} %copy.19), calls=%async_computation.2 | async-start | bytes 4194304 | tf_op jit(solution)/shard_map/all_to_all | solution.py:91
Sparse Core Ops, SparseCore 0:
  28.5 53.0 reduce-scatter.2
  84.4 33.8 reduce-scatter.4
  121.0 41.4 all-gather.4
  166.7 168.8 all-gather.2
where the time goes:
time: 350 us; the launch traced here: 349 us
  waiting for transfers between devices  232 us (66%)
  starting transfers between devices  31.5 us (9%)
  matrix products  31.2 us (9%)
  blocking collectives  27.8 us (8%)
  between operations  13.9 us (4%)
  local copies, waits for them, and re-layouts  8.11 us (2%)
  other arithmetic  5.03 us (1%)
    all_gather x1, waiting for transfers between devices, local(): lax.all_gather(frame_local, 'section', axis=1, tiled=True)  106 us
    all_to_all x1, waiting for transfers between devices, local(): lax.all_to_all(quant_all, 'section', split_axis=1, concat_axis=0, tiled=T...  45 us
    all_gather x1, waiting for transfers between devices, local(): quant_all = lax.all_gather(quant_local, 'tp', axis=1, tiled=True)  44.1 us
    reduce_scatter x2, waiting for transfers between devices, local(): lax.psum_scatter(jnp.einsum('dhj,nhj->dn', weight_block, value_heads, pre...  36.3 us
    psum x1, blocking collectives, local(): squares = lax.psum(jnp.sum(stream_f * stream_f, axis=1), 'tp')  27.8 us
    dot_general x2, matrix products, local(): jnp.einsum('dhj,nhj->dn', weight_block, value_heads, preferred_element_ty...  19.4 us
    ppermute x1, starting transfers between devices, passed_along(): return lax.ppermute(value, axis, pairs)  17.5 us
    all_to_all x1, starting transfers between devices, local(): lax.all_to_all(quant_all, 'section', split_axis=1, concat_axis=0, tiled=T...  13.9 us
  transfers between devices with their start and end apart: 6, of which 5 were waited for; matrix products, arithmetic and copies ran while one was open for 5% of the time, Pallas kernels for 0%

commit v1 on v0

v1 whole, which is shorter than its diff:
```python
import math

import jax
import jax.numpy as jnp
from jax import lax
from jax.experimental import pallas as pl
from jax.experimental.pallas import tpu as pltpu
from jax.sharding import Mesh
from jax.sharding import PartitionSpec as P

ROWS_OUT = 4096
NORM_EPS = 1e-05
SCALE_FLOOR = 1e-06
TP = 8
BIG = 32 << 20
CHEAP = pl.CostEstimate(flops=1, bytes_accessed=1, transcendentals=0)
LONG = pl.CostEstimate(flops=9_000_000_000, bytes_accessed=1, transcendentals=0)
SEC = ("x", "zh", "zl", "yh")
TPA = ("yl", "c")
NEAR = ("x", "zl")
FAR = ("zh", "yh")
SIN_POLY = (
    0.9999995827674866,
    -6.579691410064697,
    12.986435890197754,
    -12.188101768493652,
    6.558041572570801,
    -1.9530311822891235,
)


def soft_quant(values, inv_step, step7):
    scaled = values * inv_step
    turn = scaled - jnp.round(scaled)
    square = turn * turn
    poly = SIN_POLY[-1]
    for coef in SIN_POLY[-2::-1]:
        poly = poly * square + coef
    shifted = scaled - turn * poly
    return step7 * jnp.tanh(shifted * (1.0 / 7.0))


def dot_nt(left, right):
    return lax.dot_general(
        left, right, (((1,), (1,)), ((), ())), preferred_element_type=jnp.float32
    )


def three_terms(value):
    top = value.astype(jnp.bfloat16).astype(jnp.float32)
    rest = value - top
    mid = rest.astype(jnp.bfloat16).astype(jnp.float32)
    return top, mid, rest - mid


def prepare_kernel(x_ref, scale_ref, out_ref):
    squares = jnp.zeros((128, 128), jnp.float32)
    for lane in range(8):
        x = x_ref[:, lane * 128 : (lane + 1) * 128].astype(jnp.float32)
        squares += x * x
    squares = jnp.sum(jnp.transpose(squares), axis=0, keepdims=True)
    squares = jnp.concatenate([squares] + [jnp.zeros((1, 896), jnp.float32)], axis=1)
    row = lax.broadcasted_iota(jnp.int32, (16, 1024), 0)
    extra = jnp.zeros((16, 1024), jnp.float32)
    for index, term in enumerate(three_terms(scale_ref[...]) + three_terms(squares)):
        extra = jnp.where(row == index, term, extra)
    extra = extra.astype(jnp.bfloat16)
    for copy in range(4):
        out_ref[copy, 0:128, :] = x_ref[...]
        out_ref[copy, 128:144, :] = extra


def prepare(hidden, scale):
    return pl.pallas_call(
        prepare_kernel,
        out_shape=jax.ShapeDtypeStruct((4, 144, 1024), jnp.bfloat16),
        compiler_params=pltpu.CompilerParams(vmem_limit_bytes=BIG),
        cost_estimate=CHEAP,
        name="prepare",
    )(hidden, scale)


def rotate_kernel(core_ref, w_ref, r2_ref, dv_ref, rot_ref, top_ref, keep_ref, send_ref):
    step = pl.program_id(0)
    core = core_ref[0]
    rot = jnp.dot(w_ref[...], r2_ref[...], preferred_element_type=jnp.float32).astype(jnp.bfloat16)
    rot_ref[...] = rot
    top = jnp.max(jnp.abs(rot.astype(jnp.float32)), axis=0, keepdims=True)

    @pl.when(step == 0)
    def _():
        top_ref[...] = top

    @pl.when(step > 0)
    def _():
        top_ref[...] = jnp.maximum(top_ref[...], top)

    @pl.when(step < 2)
    def _():
        for part in range(4):
            prod = dot_nt(dv_ref[...], rot[part * 512 : (part + 1) * 512]).astype(jnp.bfloat16)
            chip = (step * 2 + part // 2 + 4 - core_ref[1]) % 4

            @pl.when(core == part % 2)
            def _():
                keep_ref[chip] = prod

            @pl.when(core != part % 2)
            def _():
                send_ref[chip] = prod


def rotate(core, weight, rotor, value_grad):
    whole = lambda i, core: (0, 0)
    block = lambda i, core: (i, 0)
    half = jax.ShapeDtypeStruct((4, 128, 512), jnp.bfloat16)
    return pl.pallas_call(
        rotate_kernel,
        grid_spec=pltpu.PrefetchScalarGridSpec(
            num_scalar_prefetch=1,
            grid=(4,),
            in_specs=[
                pl.BlockSpec((2048, 128), block),
                pl.BlockSpec((128, 128), whole),
                pl.BlockSpec((128, 128), whole),
            ],
            out_specs=[
                pl.BlockSpec((2048, 128), block),
                pl.BlockSpec((1, 128), whole),
                pl.BlockSpec((4, 128, 512), lambda i, core: (0, 0, 0)),
                pl.BlockSpec((4, 128, 512), lambda i, core: (0, 0, 0)),
            ],
        ),
        out_shape=[
            jax.ShapeDtypeStruct((8192, 128), jnp.bfloat16),
            jax.ShapeDtypeStruct((1, 128), jnp.float32),
            half,
            half,
        ],
        compiler_params=pltpu.CompilerParams(vmem_limit_bytes=BIG),
        cost_estimate=pl.CostEstimate(flops=23000000000, bytes_accessed=1, transcendentals=0),
        name="rotate",
    )(core, weight, rotor, value_grad)


def weight_grad_kernel(core_ref, rot_ref, top_ref, dv_ref, send_ref, keep_ref):
    index = pl.program_id(0)
    step = top_ref[...] / 7.0 + SCALE_FLOOR
    quant = soft_quant(rot_ref[...].astype(jnp.float32), 1.0 / step, step * 7.0)
    prod = dot_nt(dv_ref[...], quant.astype(jnp.bfloat16)).astype(jnp.bfloat16)

    @pl.when(index < 4)
    def _():
        send_ref[0] = prod

    @pl.when(index >= 4)
    def _():
        keep_ref[0] = prod


def weight_grad(core, rot, top, value_grad):
    half = jax.ShapeDtypeStruct((4, 128, 1024), jnp.bfloat16)
    return pl.pallas_call(
        weight_grad_kernel,
        grid_spec=pltpu.PrefetchScalarGridSpec(
            num_scalar_prefetch=1,
            grid=(8,),
            in_specs=[
                pl.BlockSpec(
                    (1024, 128),
                    lambda i, core: (
                        ((i + core[1]) % 4) * 2 + jnp.where(i < 4, 1 - core[0], core[0]),
                        0,
                    ),
                ),
                pl.BlockSpec((1, 128), lambda i, core: (0, 0)),
                pl.BlockSpec((128, 128), lambda i, core: (0, 0)),
            ],
            out_specs=[
                pl.BlockSpec((1, 128, 1024), lambda i, core: (jnp.minimum(i, 3), 0, 0)),
                pl.BlockSpec((1, 128, 1024), lambda i, core: (jnp.maximum(i - 4, 0), 0, 0)),
            ],
        ),
        out_shape=[half, half],
        compiler_params=pltpu.CompilerParams(vmem_limit_bytes=BIG),
        cost_estimate=pl.CostEstimate(flops=10350000000, bytes_accessed=1, transcendentals=0),
        name="weight_grad",
    )(core, rot, top, value_grad)


def quant_kernel(core_ref, all_ref, mask_ref, inv_ref, quant_ref):
    inverse = jnp.transpose(jnp.broadcast_to(inv_ref[...], (128, 128)))
    mask = mask_ref[0]
    scale = all_ref[0, 128:144, :].astype(jnp.float32)
    scale = scale[0:1] + scale[1:2] + scale[2:3]
    recip = 1.0 / scale
    scale7 = scale * 7.0
    for lane in range(8):
        cols = slice(lane * 128, (lane + 1) * 128)
        normed = all_ref[0, 0:128, cols].astype(jnp.float32) * inverse
        soft = soft_quant(normed, recip[:, cols], scale7[:, cols])
        quant = jnp.where(mask[:, cols] > 0.0, normed, soft).astype(jnp.bfloat16)
        zh, zl, yh = lane // 4, (lane // 2) % 2, lane % 2
        place = zh * 2 + yh
        quant_ref[zl, :, place * 128 : (place + 1) * 128] = quant


def quantize(core, hidden_all, mask, inverse):
    return pl.pallas_call(
        quant_kernel,
        grid_spec=pltpu.PrefetchScalarGridSpec(
            num_scalar_prefetch=1,
            grid=(4,),
            in_specs=[
                pl.BlockSpec((1, 144, 1024), lambda i, core: (i, 0, 0)),
                pl.BlockSpec((1, 1, 1024), lambda i, core: (i * 2 + core[0], 0, 0)),
                pl.BlockSpec((1, 128), lambda i, core: (0, 0)),
            ],
            out_specs=pl.BlockSpec((2, 128, 512), lambda i, core: (i, 0, 0)),
        ),
        out_shape=jax.ShapeDtypeStruct((8, 128, 512), jnp.bfloat16),
        compiler_params=pltpu.CompilerParams(vmem_limit_bytes=BIG),
        cost_estimate=CHEAP,
        name="quantize",
    )(core, hidden_all, mask, inverse)


def rotor_grad_kernel(core_ref, mine_ref, other_ref, wm_ref, wo_ref, dv_ref, r2_ref, total_ref):
    step = pl.program_id(0)
    total = jnp.zeros((128, 128), jnp.float32)
    for quant_ref, weight_ref in ((mine_ref, wm_ref), (other_ref, wo_ref)):
        for lane in range(8):
            zh, zl, yh = lane // 4, (lane // 2) % 2, lane % 2
            place = zh * 2 + yh
            total += jnp.dot(
                quant_ref[zl, :, place * 128 : (place + 1) * 128],
                weight_ref[0, lane * 128 : (lane + 1) * 128, :],
                preferred_element_type=jnp.float32,
            )

    @pl.when(step == 0)
    def _():
        total_ref[...] = total

    @pl.when(step > 0)
    def _():
        total_ref[...] += total

    @pl.when(step == 3)
    def _():
        r2_ref[...] = lax.dot_general(
            total_ref[...],
            dv_ref[...].astype(jnp.float32),
            (((0,), (0,)), ((), ())),
            precision=lax.Precision.HIGHEST,
            preferred_element_type=jnp.float32,
        )


def rotor_grad(core, mine, other, weight, value_grad):
    weight = weight.reshape(8, 1024, 128)
    quant_spec = pl.BlockSpec((2, 128, 512), lambda i, core: (i, 0, 0))
    return pl.pallas_call(
        rotor_grad_kernel,
        grid_spec=pltpu.PrefetchScalarGridSpec(
            num_scalar_prefetch=1,
            grid=(4,),
            in_specs=[
                quant_spec,
                quant_spec,
                pl.BlockSpec((1, 1024, 128), lambda i, core: (i * 2 + core[0], 0, 0)),
                pl.BlockSpec((1, 1024, 128), lambda i, core: (i * 2 + 1 - core[0], 0, 0)),
                pl.BlockSpec((128, 128), lambda i, core: (0, 0)),
            ],
            out_specs=pl.BlockSpec((128, 128), lambda i, core: (0, 0)),
            scratch_shapes=[pltpu.VMEM((128, 128), jnp.float32)],
        ),
        out_shape=jax.ShapeDtypeStruct((128, 128), jnp.float32),
        compiler_params=pltpu.CompilerParams(vmem_limit_bytes=BIG),
        cost_estimate=CHEAP,
        name="rotor_grad",
    )(core, mine, other, weight, weight, value_grad)


def outer_kernel(place_ref, frame_ref, mine_ref, other_ref, out_ref, left_ref):
    x, zl, yh = place_ref[2], place_ref[3], place_ref[4]

    @pl.when(pl.program_id(0) == 0)
    def _():
        for near in range(8):
            turn = (near // 2 + 4 - x) % 4
            flip = (near % 2 + zl) % 2
            left_ref[near * 128 : (near + 1) * 128, :] = frame_ref[turn * 2 + flip]

    def product(quant_ref):
        prod = lax.dot_general(
            left_ref[...],
            quant_ref[...],
            (((0,), (0,)), ((), ())),
            preferred_element_type=jnp.float32,
        ).astype(jnp.bfloat16)
        for part in range(2):
            out_ref[(part + yh) % 2] = prod[:, part * 128 : (part + 1) * 128]

    @pl.when(pl.program_id(0) < 2)
    def _():
        product(mine_ref)

    @pl.when(pl.program_id(0) >= 2)
    def _():
        product(other_ref)


def outer(place, frames, mine, other):
    return pl.pallas_call(
        outer_kernel,
        grid_spec=pltpu.PrefetchScalarGridSpec(
            num_scalar_prefetch=1,
            grid=(4,),
            in_specs=[
                pl.BlockSpec((8, 128, 512), lambda i, place: (0, 0, 0)),
                pl.BlockSpec((1024, 256), lambda i, place: (0, jnp.minimum(i, 1))),
                pl.BlockSpec((1024, 256), lambda i, place: (0, jnp.maximum(i - 2, 0))),
            ],
            out_specs=pl.BlockSpec(
                (2, 512, 128),
                lambda i, place: (jnp.where(i < 2, place[0], 1 - place[0]) * 2 + i % 2, 0, 0),
            ),
            scratch_shapes=[pltpu.VMEM((1024, 512), jnp.bfloat16)],
        ),
        out_shape=jax.ShapeDtypeStruct((8, 512, 128), jnp.bfloat16),
        compiler_params=pltpu.CompilerParams(vmem_limit_bytes=BIG),
        cost_estimate=CHEAP,
        name="outer",
    )(place, frames, mine, other)


def exchange(value, axes):
    return lax.all_to_all(value, axes, split_axis=0, concat_axis=0, tiled=True)


def shifted(value, axis, turn):
    count = lax.axis_size(axis)
    return lax.ppermute(value, axis, [(chip, (chip + turn) % count) for chip in range(count)])


def swap_core(value):
    return shifted(value, "c", 1)


def local(hidden_in, grad_sent, value_grad, value_weight, rotation, act_scale, outliers):
    sections = 64
    pairs = [(source, (source - 1) % sections) for source in range(sections)]
    place = jnp.stack([lax.axis_index(axis) for axis in ("c", "yl", "x", "zl", "yh")])
    place = place.astype(jnp.int32)
    wide = lambda value: value.astype(jnp.float32)
    tie = lax.optimization_barrier

    def chip_sum(pair):
        total = pair[0]
        for turn in (1, 2, 3):
            total = total + wide(shifted(pair[turn].astype(jnp.bfloat16), "yl", turn))
        return total

    hidden_all = exchange(prepare(hidden_in, act_scale), "yl")

    rot, peak, frame_keep, frame_send = rotate(place, value_weight, rotation, value_grad)
    frame_recv = swap_core(frame_send)
    frame = chip_sum([wide(frame_keep[turn]) + wide(frame_recv[turn]) for turn in range(4)])
    frame = frame.astype(jnp.bfloat16)
    grad_send, grad_keep = weight_grad(place, rot, peak, value_grad)
    hidden_all, frame, grad_send, grad_keep, grad_sent = tie(
        (hidden_all, frame, grad_send, grad_keep, grad_sent)
    )
    pair = jnp.stack([frame, shifted(frame, "zl", 1)])
    ids = outliers[0]
    blocks = (ids[None, :] // 128 == jnp.arange(64)[:, None]).astype(jnp.bfloat16)
    lanes = (ids[:, None] % 128 == jnp.arange(128)[None, :]).astype(jnp.bfloat16)
    mask = jnp.dot(blocks, lanes, preferred_element_type=jnp.float32).reshape(TP, 1, 1024)

    squares = jnp.sum(wide(hidden_all[:, 131:134, :128]), axis=(0, 1)).reshape(1, 128)
    inverse = lax.rsqrt((squares + swap_core(squares)) / 8192.0 + NORM_EPS)
    quant = quantize(place, hidden_all, mask, inverse)
    quant, pair = tie((quant, pair))
    quants = exchange(quant, NEAR)
    before, after = shifted(pair, "x", 1), shifted(pair, "x", -1)
    across = jnp.concatenate([shifted(before[:, :64], "x", 1), shifted(after[:, 64:], "x", -1)], 1)
    frames = jnp.concatenate([pair, after, across, before])
    incoming = lax.ppermute(grad_sent, SEC, pairs)
    quants, frames, incoming, quant, grad_send, grad_keep = tie(
        (quants, frames, incoming, quant, grad_send, grad_keep)
    )
    quants_other = swap_core(quants)
    parts = outer(place, frames, quants.reshape(1024, 512), quants_other.reshape(1024, 512))
    r2_grad = rotor_grad(place, quant, swap_core(quant), value_weight, value_grad)
    grad_recv = swap_core(grad_send)
    grad_sum = chip_sum([wide(grad_keep[turn]) + wide(grad_recv[turn]) for turn in range(4)])
    parts = exchange(parts, "zh").reshape(4, 2, 512, 128)
    sums = jnp.sum(wide(parts), axis=0)
    r1_grad = sums[0] + wide(shifted(sums[1].astype(jnp.bfloat16), "yh", 1))

    mask_mine = lax.dynamic_index_in_dim(mask, lax.axis_index(TPA), 0, keepdims=False)
    inverse = inverse.reshape(128, 1)
    normed = wide(hidden_in) * inverse
    bounded = jnp.tanh(normed / (7.0 * act_scale))
    slope = jnp.where(mask_mine > 0.0, 1.0, 1.0 - bounded * bounded)
    emitted = (wide(incoming) + inverse * (grad_sum * slope)).astype(jnp.bfloat16)
    return (emitted, r1_grad, r2_grad)


def solution(mesh):
    fine = Mesh(mesh.devices.reshape(4, 4, 2, 2, 4, 2), SEC + TPA)
    both = P(SEC, TPA)
    in_specs = (both, both, both, both, both, both, P(SEC, None))
    out_specs = (both, P(TPA, SEC), both)
    return jax.shard_map(local, mesh=fine, in_specs=in_specs, out_specs=out_specs, check_vma=False)
```

time: 350 us -> 178 us (0.51)
  the two profiles are of different devices: /device:TPU:8 before, /device:TPU:1 now
where the time goes in v1:
time: 178 us; the launch traced here: 176 us
  starting transfers between devices  91 us (51%)
  waiting for transfers between devices  48.8 us (27%)
  Pallas kernels  21.3 us (12%)
  other arithmetic  10 us (6%)
  local copies, waits for them, and re-layouts  4.17 us (2%)
    ppermute x17, starting transfers between devices, shifted(): lax.ppermute(value, axis, [(chip, (chip + turn) % count) for chip in rang...  59.6 us
    ppermute x17, waiting for transfers between devices, shifted(): lax.ppermute(value, axis, [(chip, (chip + turn) % count) for chip in rang...  42.9 us
    all_to_all x3, starting transfers between devices, exchange(): return lax.all_to_all(value, axes, split_axis=0, concat_axis=0, tiled=True)  17.9 us
    ppermute x1, starting transfers between devices, local(): incoming = lax.ppermute(grad_sent, SEC, pairs)  13.4 us
    pallas_call x1, Pallas kernels, weight_grad(): pl.pallas_call(weight_grad_kernel, grid_spec=pltpu.PrefetchScalarGridSpec...  6.15 us
    ppermute x1, waiting for transfers between devices, local(): incoming = lax.ppermute(grad_sent, SEC, pairs)  5.92 us
    pallas_call x1, Pallas kernels, rotor_grad(): pl.pallas_call(rotor_grad_kernel, grid_spec=pltpu.PrefetchScalarGridSpec(...  4.31 us
    unnamed x22, local copies, waits for them, and re-layouts  4.05 us
  transfers between devices with their start and end apart: 21, of which 8 were waited for; matrix products, arithmetic and copies ran while one was open for 5% of the time, Pallas kernels for 10%

profile of v1, /device:TPU:1, one launch (start us, length us, event | category | flops | bytes accessed | tf_op | source)
XLA Modules:
  0.0 176.5 jit_solution(17595814856568463646)
XLA Ops:
  0.6 0.0 copy-start.4
  0.7 1.1 copy-done.4
  1.7 0.7 copy-done.7
  2.4 0.1 prepare.1
  2.6 1.0 copy-done.1
  3.6 5.4 %all-to-all-start = ((bf16[4,144,1024]{2,1,0:T(8,128)(2,1)}), bf16[4,144,1024]{2,1,0:T(8,128)(2,1)S(1)}, u32[]{:S(2)}, u32[]{:S(2)}) async-start(bf16[4,144,1024]{2,1,0:T(8,128)(2,1)} %copy-done.1), calls=%async_computation | async-start | bytes 2359296 | tf_op jit(solution)/shard_map/all_to_all | solution.py:339
  9.0 0.1 stack.32.core_ref.place_ref
  9.1 3.5 %rotate.1 = (bf16[8192,128]{1,0:T(8,128)(2,1)S(1)}, f32[1,128]{1,0:T(1,128)S(1)}, bf16[4,128,512]{2,1,0:T(8,128)(2,1)S(1)}, bf16[4,128,512]{2,1,0:T(8,128)(2,1)S(1)}) custom-call(s32[5]{0:T(128)S(1)} %stack.32.core_ref.place_ref, bf16[8192,128]{1,0:T(8,128)(2,1)S(1)} %copy-done, bf16[128,128]{1,0:T(8,128)(2,1)S(1)} %copy-done.9, bf16[128,128]{1,0:T(8,128)(2,1)S(1)} %copy-done.6), custom_call_target="tpu_custom_call" | custom-call | flops 23000000512 | bytes 1 | tf_op jit(solution)/shard_map/rotate/pallas_call | solution.py:117
  12.6 6.9 %collective-permute-start = (bf16[4,128,512]{2,1,0:T(8,128)(2,1)S(1)}, bf16[4,128,512]{2,1,0:T(8,128)(2,1)S(1)}, u32[]{:S(2)}, u32[]{:S(2)}) collective-permute-start(bf16[4,128,512]{2,1,0:T(8,128)(2,1)S(1)} %get-tuple-element.23), channel_id=1, source_target_pairs={{0,1},{1,0},{2,3},{3,2},{4,5},{5,4},{6,7},{7,6},{8,9},{9,8},{10,11... | collective-permute-start | bytes 1572872 | tf_op jit(solution)/shard_map/ppermute | solution.py:344
  19.5 0.0 copy-start.10
  19.5 6.2 %weight_grad.1 = (bf16[4,128,1024]{2,1,0:T(8,128)(2,1)}, bf16[4,128,1024]{2,1,0:T(8,128)(2,1)S(1)}) custom-call(s32[5]{0:T(128)S(1)} %stack.32.core_ref.place_ref, bf16[8192,128]{1,0:T(8,128)(2,1)S(1)} %get-tuple-element.24.rot_ref, f32[1,128]{1,0:T(1,128)S(1)} %get-tuple-element.25.top_ref, bf16[128,128]{1,0:T(8,128)(2,1)S(1)} %copy-done.6), custom_call_target="tpu_custom_call" | custom-call | flops 10350000128 | bytes 1 | tf_op jit(solution)/shard_map/weight_grad/pallas_call | solution.py:163
  25.7 0.0 collective-permute-done
  25.7 0.1 fusion.13
  25.8 3.6 %collective-permute-start.1 = (bf16[128,512]{1,0:T(8,128)(2,1)S(1)}, bf16[128,512]{1,0:T(8,128)(2,1)S(1)}, u32[]{:S(2)}, u32[]{:S(2)}) collective-permute-start(bf16[128,512]{1,0:T(8,128)(2,1)S(1)} %get-tuple-element.44), channel_id=1, source_target_pairs={{0,2},{2,4},{4,6},{6,0},{1,3},{3,5},{5,7},{7,1},{8,10},{10,12},{12... | collective-permute-start | bytes 393224 | tf_op jit(solution)/shard_map/ppermute | solution.py:344
  29.4 3.7 %collective-permute-start.3 = (bf16[128,512]{1,0:T(8,128)(2,1)S(1)}, bf16[128,512]{1,0:T(8,128)(2,1)S(1)}, u32[]{:S(2)}, u32[]{:S(2)}) collective-permute-start(bf16[128,512]{1,0:T(8,128)(2,1)S(1)} %get-tuple-element.45), channel_id=1, source_target_pairs={{0,6},{2,0},{4,2},{6,4},{1,7},{3,1},{5,3},{7,5},{8,14},{10,8},{12,... | collective-permute-start | bytes 393224 | tf_op jit(solution)/shard_map/ppermute | solution.py:344
  33.2 2.5 %collective-permute-start.2 = (bf16[128,512]{1,0:T(8,128)(2,1)S(1)}, bf16[128,512]{1,0:T(8,128)(2,1)S(1)}, u32[]{:S(2)}, u32[]{:S(2)}) collective-permute-start(bf16[128,512]{1,0:T(8,128)(2,1)S(1)} %get-tuple-element.46), channel_id=1, source_target_pairs={{0,4},{2,6},{4,0},{6,2},{1,5},{3,7},{5,1},{7,3},{8,12},{10,14},{12... | collective-permute-start | bytes 393224 | tf_op jit(solution)/shard_map/ppermute | solution.py:344
  35.7 0.0 collective-permute-done.1
  35.7 5.1 %collective-permute-done.3 = bf16[128,512]{1,0:T(8,128)(2,1)S(1)} collective-permute-done((bf16[128,512]{1,0:T(8,128)(2,1)S(1)}, bf16[128,512]{1,0:T(8,128)(2,1)S(1)}, u32[]{:S(2)}, u32[]{:S(2)}) %collective-permute-start.3) | collective-permute-done | bytes 131104 | tf_op jit(solution)/shard_map/ppermute | solution.py:344
  40.8 6.0 %collective-permute-done.2 = bf16[128,512]{1,0:T(8,128)(2,1)S(1)} collective-permute-done((bf16[128,512]{1,0:T(8,128)(2,1)S(1)}, bf16[128,512]{1,0:T(8,128)(2,1)S(1)}, u32[]{:S(2)}, u32[]{:S(2)}) %collective-permute-start.2) | collective-permute-done | bytes 131104 | tf_op jit(solution)/shard_map/ppermute | solution.py:344
  46.7 0.1 fusion.12
  46.8 0.0 all-to-all-done.all_ref
  46.9 4.9 %collective-permute-start.4 = (f32[1,128]{1,0:T(1,128)S(1)}, f32[1,128]{1,0:T(1,128)S(1)}, u32[]{:S(2)}, u32[]{:S(2)}) collective-permute-start(f32[1,128]{1,0:T(1,128)S(1)} %bitcast.71), channel_id=1, source_target_pairs={{0,1},{1,0},{2,3},{3,2},{4,5},{5,4},{6,7},{7,6},{8,9},{9,8},{10,11... | collective-permute-start | bytes 1544 | tf_op jit(solution)/shard_map/ppermute | solution.py:344
  51.8 0.2 fusion.17
  52.0 4.0 %collective-permute-start.5 = (bf16[128,512]{1,0:T(8,128)(2,1)S(1)}, bf16[128,512]{1,0:T(8,128)(2,1)S(1)}, u32[]{:S(2)}, u32[]{:S(2)}) collective-permute-start(bf16[128,512]{1,0:T(8,128)(2,1)S(1)} %fusion.12), channel_id=1, source_target_pairs={{0,16},{16,0},{1,17},{17,1},{2,18},{18,2},{3,19},{19,3},{4,20},{20... | collective-permute-start | bytes 393224 | tf_op jit(solution)/shard_map/ppermute | solution.py:344
  56.0 0.0 collective-permute-done.4
  56.0 3.4 %quantize.1.mine_ref = bf16[8,128,512]{2,1,0:T(8,128)(2,1)} custom-call(s32[5]{0:T(128)S(1)} %stack.32.core_ref.place_ref, bf16[4,144,1024]{2,1,0:T(8,128)(2,1)S(1)} %all-to-all-done.all_ref, f32[8,1,1024]{2,1,0:T(1,128)S(1)} %bitcast.65, f32[1,128]{1,0:T(1,128)S(1)} %add_rsqrt_fusion.inv_ref), custom_call_target="tpu_custom_call" | custom-call | flops 1 | bytes 1 | tf_op jit(solution)/shard_map/quantize/pallas_call | solution.py:209
  59.5 0.4 collective-permute-done.5
  59.8 0.7 pad_maximum_fusion.1
  60.6 5.0 %all-to-all-start.1 = ((bf16[8,128,512]{2,1,0:T(8,128)(2,1)}), bf16[8,128,512]{2,1,0:T(8,128)(2,1)S(1)}, u32[]{:S(2)}, u32[]{:S(2)}) async-start(bf16[8,128,512]{2,1,0:T(8,128)(2,1)} %quantize.1.mine_ref), calls=%async_computation.1 | async-start | bytes 2097152 | tf_op jit(solution)/shard_map/all_to_all | solution.py:339
  65.5 3.4 %collective-permute-start.7 = (bf16[2,128,512]{2,1,0:T(8,128)(2,1)}, bf16[2,128,512]{2,1,0:T(8,128)(2,1)S(1)}, u32[]{:S(2)}, u32[]{:S(2)}) collective-permute-start(bf16[2,128,512]{2,1,0:T(8,128)(2,1)} %pad_maximum_fusion.1), channel_id=1, source_target_pairs={{0,128},{128,256},{256,384},{384,0},{1,129},{129,257},{257,385},{3... | collective-permute-start | bytes 786440 | tf_op jit(solution)/shard_map/ppermute | solution.py:344
  68.9 3.1 %collective-permute-start.6 = (bf16[2,128,512]{2,1,0:T(8,128)(2,1)}, bf16[2,128,512]{2,1,0:T(8,128)(2,1)S(1)}, u32[]{:S(2)}, u32[]{:S(2)}) collective-permute-start(bf16[2,128,512]{2,1,0:T(8,128)(2,1)} %pad_maximum_fusion.1), channel_id=1, source_target_pairs={{0,384},{128,0},{256,128},{384,256},{1,385},{129,1},{257,129},{385... | collective-permute-start | bytes 786440 | tf_op jit(solution)/shard_map/ppermute | solution.py:344
  72.1 13.5 %collective-permute-done.7 = bf16[2,128,512]{2,1,0:T(8,128)(2,1)S(1)} collective-permute-done((bf16[2,128,512]{2,1,0:T(8,128)(2,1)}, bf16[2,128,512]{2,1,0:T(8,128)(2,1)S(1)}, u32[]{:S(2)}, u32[]{:S(2)}) %collective-permute-start.7) | collective-permute-done | bytes 262176 | tf_op jit(solution)/shard_map/ppermute | solution.py:344
  85.5 1.9 %collective-permute-start.8 = (bf16[2,64,512]{2,1,0:T(8,128)(2,1)S(1)}, bf16[2,64,512]{2,1,0:T(8,128)(2,1)S(1)}, u32[]{:S(2)}, u32[]{:S(2)}) collective-permute-start(bf16[2,64,512]{2,1,0:T(8,128)(2,1)S(1)} %slice.89), channel_id=1, source_target_pairs={{0,128},{128,256},{256,384},{384,0},{1,129},{129,257},{257,385},{3... | collective-permute-start | bytes 393224 | tf_op jit(solution)/shard_map/ppermute | solution.py:344
  87.5 0.0 collective-permute-done.6
  87.5 4.6 %collective-permute-start.9 = (bf16[2,64,512]{2,1,0:T(8,128)(2,1)S(1)}, bf16[2,64,512]{2,1,0:T(8,128)(2,1)S(1)}, u32[]{:S(2)}, u32[]{:S(2)}) collective-permute-start(bf16[2,64,512]{2,1,0:T(8,128)(2,1)S(1)} %slice.90), channel_id=1, source_target_pairs={{0,384},{128,0},{256,128},{384,256},{1,385},{129,1},{257,129},{385... | collective-permute-start | bytes 393224 | tf_op jit(solution)/shard_map/ppermute | solution.py:344
  92.1 13.4 %collective-permute-start.10 = (bf16[128,1024]{1,0:T(8,128)(2,1)}, bf16[128,1024]{1,0:T(8,128)(2,1)}, u32[]{:S(2)}, u32[]{:S(2)}) collective-permute-start(bf16[128,1024]{1,0:T(8,128)(2,1)} %param.8), channel_id=1, source_target_pairs={{0,504},{8,0},{16,8},{24,16},{32,24},{40,32},{48,40},{56,48},{64,5... | collective-permute-start | bytes 786440 | tf_op jit(solution)/shard_map/ppermute | solution.py:389
  105.5 0.0 collective-permute-done.8
  105.5 0.0 collective-permute-done.9
  105.5 2.0 %pad_maximum_fusion.frame_ref = bf16[8,128,512]{2,1,0:T(8,128)(2,1)} fusion(bf16[2,128,512]{2,1,0:T(8,128)(2,1)S(1)} %collective-permute-done.7, bf16[2,64,512]{2,1,0:T(8,128)(2,1)S(1)} %collective-permute-done.9, bf16[2,64,512]{2,1,0:T(8,128)(2,1)S(1)} %collective-permute-done.8, bf16[2,128,512]{2,1,0:T(8,128)(2,1)S(1)} %collective-permute-done.6, ...), kind=kLoop, calls=%fused_computation.1 | loop fusion | flops 5242880 | bytes 2097152 | tf_op jit(solution)/shard_map/concatenate | solution.py:388
  107.5 5.9 %collective-permute-done.10 = bf16[128,1024]{1,0:T(8,128)(2,1)} collective-permute-done((bf16[128,1024]{1,0:T(8,128)(2,1)}, bf16[128,1024]{1,0:T(8,128)(2,1)}, u32[]{:S(2)}, u32[]{:S(2)}) %collective-permute-start.10) | collective-permute-done | bytes 262176 | tf_op jit(solution)/shard_map/ppermute | solution.py:389
  113.4 0.0 all-to-all-done.1
  113.5 2.8 %collective-permute-start.15 = (bf16[8,128,512]{2,1,0:T(8,128)(2,1)S(1)}, bf16[8,128,512]{2,1,0:T(8,128)(2,1)S(1)}, u32[]{:S(2)}, u32[]{:S(2)}) collective-permute-start(bf16[8,128,512]{2,1,0:T(8,128)(2,1)S(1)} %all-to-all-done.1), channel_id=1, source_target_pairs={{0,1},{1,0},{2,3},{3,2},{4,5},{5,4},{6,7},{7,6},{8,9},{9,8},{10,11... | collective-permute-start | bytes 3145736 | tf_op jit(solution)/shard_map/ppermute | solution.py:344
  116.2 2.3 %collective-permute-done.15 = bf16[8,128,512]{2,1,0:T(8,128)(2,1)S(1)} collective-permute-done((bf16[8,128,512]{2,1,0:T(8,128)(2,1)S(1)}, bf16[8,128,512]{2,1,0:T(8,128)(2,1)S(1)}, u32[]{:S(2)}, u32[]{:S(2)}) %collective-permute-start.15) | collective-permute-done | bytes 1048608 | tf_op jit(solution)/shard_map/ppermute | solution.py:344
  118.5 1.2 copy-done.2
  119.7 3.8 %outer.1 = bf16[8,512,128]{2,1,0:T(8,128)(2,1)} custom-call(s32[5]{0:T(128)S(1)} %stack.32.core_ref.place_ref, bf16[8,128,512]{2,1,0:T(8,128)(2,1)S(1)} %copy-done.2, bf16[1024,512]{1,0:T(8,128)(2,1)S(1)} %bitcast.63, bf16[1024,512]{1,0:T(8,128)(2,1)S(1)} %bitcast.64), custom_call_target="tpu_custom_call" | custom-call | flops 1 | bytes 1 | tf_op jit(solution)/shard_map/outer/pallas_call | solution.py:315
  123.5 7.5 %all-to-all-start.2 = ((bf16[8,512,128]{2,1,0:T(8,128)(2,1)}), bf16[8,512,128]{2,1,0:T(8,128)(2,1)}, u32[]{:S(2)}, u32[]{:S(2)}) async-start(bf16[8,512,128]{2,1,0:T(8,128)(2,1)} %outer.1), calls=%async_computation.2 | async-start | bytes 2097152 | tf_op jit(solution)/shard_map/all_to_all | solution.py:339
  131.0 2.6 %collective-permute-start.11 = (bf16[4,128,1024]{2,1,0:T(8,128)(2,1)}, bf16[4,128,1024]{2,1,0:T(8,128)(2,1)}, u32[]{:S(2)}, u32[]{:S(2)}) collective-permute-start(bf16[4,128,1024]{2,1,0:T(8,128)(2,1)} %get-tuple-element.37), channel_id=1, source_target_pairs={{0,1},{1,0},{2,3},{3,2},{4,5},{5,4},{6,7},{7,6},{8,9},{9,8},{10,11... | collective-permute-start | bytes 3145736 | tf_op jit(solution)/shard_map/ppermute | solution.py:344
  133.6 1.9 %collective-permute-start.17 = (bf16[8,128,512]{2,1,0:T(8,128)(2,1)}, bf16[8,128,512]{2,1,0:T(8,128)(2,1)S(1)}, u32[]{:S(2)}, u32[]{:S(2)}) collective-permute-start(bf16[8,128,512]{2,1,0:T(8,128)(2,1)} %quantize.1.mine_ref), channel_id=1, source_target_pairs={{0,1},{1,0},{2,3},{3,2},{4,5},{5,4},{6,7},{7,6},{8,9},{9,8},{10,11... | collective-permute-start | bytes 3145736 | tf_op jit(solution)/shard_map/ppermute | solution.py:344
  135.5 0.6 collective-permute-done.11
  136.2 2.4 %fusion.6 = (bf16[128,1024]{1,0:T(8,128)(2,1)}, bf16[128,1024]{1,0:T(8,128)(2,1)}, bf16[128,1024]{1,0:T(8,128)(2,1)}) fusion(bf16[4,128,1024]{2,1,0:T(8,128)(2,1)} %collective-permute-done.11, bf16[4,128,1024]{2,1,0:T(8,128)(2,1)} %copy-done.3), kind=kLoop, calls=%fused_computation.12 | loop fusion | flops 1572864 | bytes 2359296 | tf_op jit(solution)/shard_map/convert_element_type | solution.py:362
  138.6 1.9 %collective-permute-start.12 = (bf16[128,1024]{1,0:T(8,128)(2,1)}, bf16[128,1024]{1,0:T(8,128)(2,1)}, u32[]{:S(2)}, u32[]{:S(2)}) collective-permute-start(bf16[128,1024]{1,0:T(8,128)(2,1)} %get-tuple-element.41), channel_id=1, source_target_pairs={{0,2},{2,4},{4,6},{6,0},{1,3},{3,5},{5,7},{7,1},{8,10},{10,12},{12... | collective-permute-start | bytes 786440 | tf_op jit(solution)/shard_map/ppermute | solution.py:344
  140.5 5.2 %collective-permute-start.14 = (bf16[128,1024]{1,0:T(8,128)(2,1)}, bf16[128,1024]{1,0:T(8,128)(2,1)}, u32[]{:S(2)}, u32[]{:S(2)}) collective-permute-start(bf16[128,1024]{1,0:T(8,128)(2,1)} %get-tuple-element.42), channel_id=1, source_target_pairs={{0,6},{2,0},{4,2},{6,4},{1,7},{3,1},{5,3},{7,5},{8,14},{10,8},{12,... | collective-permute-start | bytes 786440 | tf_op jit(solution)/shard_map/ppermute | solution.py:344
  145.6 1.9 %collective-permute-start.13 = (bf16[128,1024]{1,0:T(8,128)(2,1)}, bf16[128,1024]{1,0:T(8,128)(2,1)}, u32[]{:S(2)}, u32[]{:S(2)}) collective-permute-start(bf16[128,1024]{1,0:T(8,128)(2,1)} %get-tuple-element.43), channel_id=1, source_target_pairs={{0,4},{2,6},{4,0},{6,2},{1,5},{3,7},{5,1},{7,3},{8,12},{10,14},{12... | collective-permute-start | bytes 786440 | tf_op jit(solution)/shard_map/ppermute | solution.py:344
  147.6 0.0 collective-permute-done.17.other_ref
  147.6 0.0 copy-start.5
  147.6 4.3 %rotor_grad.1 = f32[128,128]{1,0:T(8,128)} custom-call(s32[5]{0:T(128)S(1)} %stack.32.core_ref.place_ref, bf16[8,128,512]{2,1,0:T(8,128)(2,1)} %quantize.1.mine_ref, bf16[8,128,512]{2,1,0:T(8,128)(2,1)S(1)} %collective-permute-done.17.other_ref, bf16[8,1024,128]{2,1,0:T(8,128)(2,1)S(1)} %bitcast.61, bf16[8,1024,128]{2,1,0:T(8,128)(2,1)S(1)} %bitcast.62, ...), custom_call_target="tpu_custom_call" | custom-call | flops 1 | bytes 1 | tf_op jit(solution)/shard_map/rotor_grad/pallas_call | solution.py:263
  151.9 0.0 all-to-all-done.2
  151.9 1.4 convert_reduce_fusion
  153.4 4.8 %collective-permute-start.16 = (bf16[512,128]{1,0:T(8,128)(2,1)S(1)}, bf16[512,128]{1,0:T(8,128)(2,1)S(1)}, u32[]{:S(2)}, u32[]{:S(2)}) collective-permute-start(bf16[512,128]{1,0:T(8,128)(2,1)S(1)} %fusion.16), channel_id=1, source_target_pairs={{0,8},{8,0},{1,9},{9,1},{2,10},{10,2},{3,11},{11,3},{4,12},{12,4},... | collective-permute-start | bytes 393224 | tf_op jit(solution)/shard_map/ppermute | solution.py:344
  158.2 0.0 collective-permute-done.12
  158.2 0.0 collective-permute-done.14
  158.2 15.1 %collective-permute-done.13 = bf16[128,1024]{1,0:T(8,128)(2,1)} collective-permute-done((bf16[128,1024]{1,0:T(8,128)(2,1)}, bf16[128,1024]{1,0:T(8,128)(2,1)}, u32[]{:S(2)}, u32[]{:S(2)}) %collective-permute-start.13) | collective-permute-done | bytes 262176 | tf_op jit(solution)/shard_map/ppermute | solution.py:344
  173.3 2.4 %fusion.5 = bf16[128,1024]{1,0:T(8,128)(2,1)} fusion(bf16[128,1024]{1,0:T(8,128)(2,1)S(1)} %copy-done.5, bf16[128,1024]{1,0:T(8,128)(2,1)} %collective-permute-done.14, bf16[128,1024]{1,0:T(8,128)(2,1)} %collective-permute-done.13, bf16[128,1024]{1,0:T(8,128)(2,1)} %collective-permute-done.12, bf16[128,1024]{1,0:T(8,128)(2,1)} %collective-permute-done.10, ...), kind=kLoop, calls=%fused_computation.8 | loop fusion | flops 2621440 | bytes 2102784 | tf_op jit(solution)/shard_map/convert_element_type | solution.py:407
  175.8 0.7 fusion.9
  (25 shorter events, 0.2 us)
Async XLA Ops:
  0.6 8.5 %copy-start = (bf16[8192,128]{1,0:T(8,128)(2,1)S(1)}, bf16[8192,128]{1,0:T(8,128)(2,1)}, u32[]{:S(2)}) copy-start(bf16[8192,128]{1,0:T(8,128)(2,1)} %w_ref.1) | copy-start | bytes 6291460
  0.6 1.1 copy-start.4
  1.7 0.7 copy-start.7
  2.4 6.7 %copy-start.6 = (bf16[128,128]{1,0:T(8,128)(2,1)S(1)}, bf16[128,128]{1,0:T(8,128)(2,1)}, u32[]{:S(2)}) copy-start(bf16[128,128]{1,0:T(8,128)(2,1)} %dv_ref.5) | copy-start | bytes 98308
  2.4 6.7 %copy-start.9 = (bf16[128,128]{1,0:T(8,128)(2,1)S(1)}, bf16[128,128]{1,0:T(8,128)(2,1)}, u32[]{:S(2)}) copy-start(bf16[128,128]{1,0:T(8,128)(2,1)} %r2_ref.1) | copy-start | bytes 98308
  2.6 1.0 copy-start.1
  3.6 43.2 %all-to-all-start = ((bf16[4,144,1024]{2,1,0:T(8,128)(2,1)}), bf16[4,144,1024]{2,1,0:T(8,128)(2,1)S(1)}, u32[]{:S(2)}, u32[]{:S(2)}) async-start(bf16[4,144,1024]{2,1,0:T(8,128)(2,1)} %copy-done.1), calls=%async_computation | async-start | bytes 2359296 | tf_op jit(solution)/shard_map/all_to_all | solution.py:339
  12.6 13.1 %collective-permute-start = (bf16[4,128,512]{2,1,0:T(8,128)(2,1)S(1)}, bf16[4,128,512]{2,1,0:T(8,128)(2,1)S(1)}, u32[]{:S(2)}, u32[]{:S(2)}) collective-permute-start(bf16[4,128,512]{2,1,0:T(8,128)(2,1)S(1)} %get-tuple-element.23), channel_id=1, source_target_pairs={{0,1},{1,0},{2,3},{3,2},{4,5},{5,4},{6,7},{7,6},{8,9},{9,8},{10,11... | collective-permute-start | bytes 1572872 | tf_op jit(solution)/shard_map/ppermute | solution.py:344
  19.5 6.2 %copy-start.10 = (s32[1,128]{1,0:T(1,128)S(1)}, s32[1,128]{1,0:T(1,128)}, u32[]{:S(2)}) copy-start(s32[1,128]{1,0:T(1,128)} %param.13) | copy-start | bytes 1540
  25.7 21.1 %copy-start.3 = (bf16[4,128,1024]{2,1,0:T(8,128)(2,1)}, bf16[4,128,1024]{2,1,0:T(8,128)(2,1)S(1)}, u32[]{:S(2)}) copy-start(bf16[4,128,1024]{2,1,0:T(8,128)(2,1)S(1)} %get-tuple-element.36) | copy-start | bytes 3145732
  25.8 9.8 %collective-permute-start.1 = (bf16[128,512]{1,0:T(8,128)(2,1)S(1)}, bf16[128,512]{1,0:T(8,128)(2,1)S(1)}, u32[]{:S(2)}, u32[]{:S(2)}) collective-permute-start(bf16[128,512]{1,0:T(8,128)(2,1)S(1)} %get-tuple-element.44), channel_id=1, source_target_pairs={{0,2},{2,4},{4,6},{6,0},{1,3},{3,5},{5,7},{7,1},{8,10},{10,12},{12... | collective-permute-start | bytes 393224 | tf_op jit(solution)/shard_map/ppermute | solution.py:344
  29.4 11.4 %collective-permute-start.3 = (bf16[128,512]{1,0:T(8,128)(2,1)S(1)}, bf16[128,512]{1,0:T(8,128)(2,1)S(1)}, u32[]{:S(2)}, u32[]{:S(2)}) collective-permute-start(bf16[128,512]{1,0:T(8,128)(2,1)S(1)} %get-tuple-element.45), channel_id=1, source_target_pairs={{0,6},{2,0},{4,2},{6,4},{1,7},{3,1},{5,3},{7,5},{8,14},{10,8},{12,... | collective-permute-start | bytes 393224 | tf_op jit(solution)/shard_map/ppermute | solution.py:344
  33.2 13.6 %collective-permute-start.2 = (bf16[128,512]{1,0:T(8,128)(2,1)S(1)}, bf16[128,512]{1,0:T(8,128)(2,1)S(1)}, u32[]{:S(2)}, u32[]{:S(2)}) collective-permute-start(bf16[128,512]{1,0:T(8,128)(2,1)S(1)} %get-tuple-element.46), channel_id=1, source_target_pairs={{0,4},{2,6},{4,0},{6,2},{1,5},{3,7},{5,1},{7,3},{8,12},{10,14},{12... | collective-permute-start | bytes 393224 | tf_op jit(solution)/shard_map/ppermute | solution.py:344
  46.9 9.1 %collective-permute-start.4 = (f32[1,128]{1,0:T(1,128)S(1)}, f32[1,128]{1,0:T(1,128)S(1)}, u32[]{:S(2)}, u32[]{:S(2)}) collective-permute-start(f32[1,128]{1,0:T(1,128)S(1)} %bitcast.71), channel_id=1, source_target_pairs={{0,1},{1,0},{2,3},{3,2},{4,5},{5,4},{6,7},{7,6},{8,9},{9,8},{10,11... | collective-permute-start | bytes 1544 | tf_op jit(solution)/shard_map/ppermute | solution.py:344
  52.0 7.8 %collective-permute-start.5 = (bf16[128,512]{1,0:T(8,128)(2,1)S(1)}, bf16[128,512]{1,0:T(8,128)(2,1)S(1)}, u32[]{:S(2)}, u32[]{:S(2)}) collective-permute-start(bf16[128,512]{1,0:T(8,128)(2,1)S(1)} %fusion.12), channel_id=1, source_target_pairs={{0,16},{16,0},{1,17},{17,1},{2,18},{18,2},{3,19},{19,3},{4,20},{20... | collective-permute-start | bytes 393224 | tf_op jit(solution)/shard_map/ppermute | solution.py:344
  60.6 52.9 %all-to-all-start.1 = ((bf16[8,128,512]{2,1,0:T(8,128)(2,1)}), bf16[8,128,512]{2,1,0:T(8,128)(2,1)S(1)}, u32[]{:S(2)}, u32[]{:S(2)}) async-start(bf16[8,128,512]{2,1,0:T(8,128)(2,1)} %quantize.1.mine_ref), calls=%async_computation.1 | async-start | bytes 2097152 | tf_op jit(solution)/shard_map/all_to_all | solution.py:339
  65.5 20.0 %collective-permute-start.7 = (bf16[2,128,512]{2,1,0:T(8,128)(2,1)}, bf16[2,128,512]{2,1,0:T(8,128)(2,1)S(1)}, u32[]{:S(2)}, u32[]{:S(2)}) collective-permute-start(bf16[2,128,512]{2,1,0:T(8,128)(2,1)} %pad_maximum_fusion.1), channel_id=1, source_target_pairs={{0,128},{128,256},{256,384},{384,0},{1,129},{129,257},{257,385},{3... | collective-permute-start | bytes 786440 | tf_op jit(solution)/shard_map/ppermute | solution.py:344
  68.9 18.5 %collective-permute-start.6 = (bf16[2,128,512]{2,1,0:T(8,128)(2,1)}, bf16[2,128,512]{2,1,0:T(8,128)(2,1)S(1)}, u32[]{:S(2)}, u32[]{:S(2)}) collective-permute-start(bf16[2,128,512]{2,1,0:T(8,128)(2,1)} %pad_maximum_fusion.1), channel_id=1, source_target_pairs={{0,384},{128,0},{256,128},{384,256},{1,385},{129,1},{257,129},{385... | collective-permute-start | bytes 786440 | tf_op jit(solution)/shard_map/ppermute | solution.py:344
  85.5 20.0 %collective-permute-start.8 = (bf16[2,64,512]{2,1,0:T(8,128)(2,1)S(1)}, bf16[2,64,512]{2,1,0:T(8,128)(2,1)S(1)}, u32[]{:S(2)}, u32[]{:S(2)}) collective-permute-start(bf16[2,64,512]{2,1,0:T(8,128)(2,1)S(1)} %slice.89), channel_id=1, source_target_pairs={{0,128},{128,256},{256,384},{384,0},{1,129},{129,257},{257,385},{3... | collective-permute-start | bytes 393224 | tf_op jit(solution)/shard_map/ppermute | solution.py:344
  87.5 18.0 %collective-permute-start.9 = (bf16[2,64,512]{2,1,0:T(8,128)(2,1)S(1)}, bf16[2,64,512]{2,1,0:T(8,128)(2,1)S(1)}, u32[]{:S(2)}, u32[]{:S(2)}) collective-permute-start(bf16[2,64,512]{2,1,0:T(8,128)(2,1)S(1)} %slice.90), channel_id=1, source_target_pairs={{0,384},{128,0},{256,128},{384,256},{1,385},{129,1},{257,129},{385... | collective-permute-start | bytes 393224 | tf_op jit(solution)/shard_map/ppermute | solution.py:344
  92.1 21.4 %collective-permute-start.10 = (bf16[128,1024]{1,0:T(8,128)(2,1)}, bf16[128,1024]{1,0:T(8,128)(2,1)}, u32[]{:S(2)}, u32[]{:S(2)}) collective-permute-start(bf16[128,1024]{1,0:T(8,128)(2,1)} %param.8), channel_id=1, source_target_pairs={{0,504},{8,0},{16,8},{24,16},{32,24},{40,32},{48,40},{56,48},{64,5... | collective-permute-start | bytes 786440 | tf_op jit(solution)/shard_map/ppermute | solution.py:389
  113.5 5.0 %collective-permute-start.15 = (bf16[8,128,512]{2,1,0:T(8,128)(2,1)S(1)}, bf16[8,128,512]{2,1,0:T(8,128)(2,1)S(1)}, u32[]{:S(2)}, u32[]{:S(2)}) collective-permute-start(bf16[8,128,512]{2,1,0:T(8,128)(2,1)S(1)} %all-to-all-done.1), channel_id=1, source_target_pairs={{0,1},{1,0},{2,3},{3,2},{4,5},{5,4},{6,7},{7,6},{8,9},{9,8},{10,11... | collective-permute-start | bytes 3145736 | tf_op jit(solution)/shard_map/ppermute | solution.py:344
  118.5 1.2 copy-start.2
  123.5 12.1 %copy-start.8 = (f32[1,1024]{1,0:T(1,128)S(1)}, f32[1,1024]{1,0:T(1,128)}, u32[]{:S(2)}) copy-start(f32[1,1024]{1,0:T(1,128)} %scale_ref.1) | copy-start | bytes 12292
  123.5 28.4 %all-to-all-start.2 = ((bf16[8,512,128]{2,1,0:T(8,128)(2,1)}), bf16[8,512,128]{2,1,0:T(8,128)(2,1)}, u32[]{:S(2)}, u32[]{:S(2)}) async-start(bf16[8,512,128]{2,1,0:T(8,128)(2,1)} %outer.1), calls=%async_computation.2 | async-start | bytes 2097152 | tf_op jit(solution)/shard_map/all_to_all | solution.py:339
  131.0 5.2 %collective-permute-start.11 = (bf16[4,128,1024]{2,1,0:T(8,128)(2,1)}, bf16[4,128,1024]{2,1,0:T(8,128)(2,1)}, u32[]{:S(2)}, u32[]{:S(2)}) collective-permute-start(bf16[4,128,1024]{2,1,0:T(8,128)(2,1)} %get-tuple-element.37), channel_id=1, source_target_pairs={{0,1},{1,0},{2,3},{3,2},{4,5},{5,4},{6,7},{7,6},{8,9},{9,8},{10,11... | collective-permute-start | bytes 3145736 | tf_op jit(solution)/shard_map/ppermute | solution.py:344
  133.6 14.0 %collective-permute-start.17 = (bf16[8,128,512]{2,1,0:T(8,128)(2,1)}, bf16[8,128,512]{2,1,0:T(8,128)(2,1)S(1)}, u32[]{:S(2)}, u32[]{:S(2)}) collective-permute-start(bf16[8,128,512]{2,1,0:T(8,128)(2,1)} %quantize.1.mine_ref), channel_id=1, source_target_pairs={{0,1},{1,0},{2,3},{3,2},{4,5},{5,4},{6,7},{7,6},{8,9},{9,8},{10,11... | collective-permute-start | bytes 3145736 | tf_op jit(solution)/shard_map/ppermute | solution.py:344
  138.6 19.6 %collective-permute-start.12 = (bf16[128,1024]{1,0:T(8,128)(2,1)}, bf16[128,1024]{1,0:T(8,128)(2,1)}, u32[]{:S(2)}, u32[]{:S(2)}) collective-permute-start(bf16[128,1024]{1,0:T(8,128)(2,1)} %get-tuple-element.41), channel_id=1, source_target_pairs={{0,2},{2,4},{4,6},{6,0},{1,3},{3,5},{5,7},{7,1},{8,10},{10,12},{12... | collective-permute-start | bytes 786440 | tf_op jit(solution)/shard_map/ppermute | solution.py:344
  140.5 17.7 %collective-permute-start.14 = (bf16[128,1024]{1,0:T(8,128)(2,1)}, bf16[128,1024]{1,0:T(8,128)(2,1)}, u32[]{:S(2)}, u32[]{:S(2)}) collective-permute-start(bf16[128,1024]{1,0:T(8,128)(2,1)} %get-tuple-element.42), channel_id=1, source_target_pairs={{0,6},{2,0},{4,2},{6,4},{1,7},{3,1},{5,3},{7,5},{8,14},{10,8},{12,... | collective-permute-start | bytes 786440 | tf_op jit(solution)/shard_map/ppermute | solution.py:344
  145.6 27.7 %collective-permute-start.13 = (bf16[128,1024]{1,0:T(8,128)(2,1)}, bf16[128,1024]{1,0:T(8,128)(2,1)}, u32[]{:S(2)}, u32[]{:S(2)}) collective-permute-start(bf16[128,1024]{1,0:T(8,128)(2,1)} %get-tuple-element.43), channel_id=1, source_target_pairs={{0,4},{2,6},{4,0},{6,2},{1,5},{3,7},{5,1},{7,3},{8,12},{10,14},{12... | collective-permute-start | bytes 786440 | tf_op jit(solution)/shard_map/ppermute | solution.py:344
  147.6 25.7 %copy-start.5 = (bf16[128,1024]{1,0:T(8,128)(2,1)S(1)}, bf16[128,1024]{1,0:T(8,128)(2,1)}, u32[]{:S(2)}) copy-start(bf16[128,1024]{1,0:T(8,128)(2,1)} %x_ref.1) | copy-start | bytes 786436
  153.4 22.4 %collective-permute-start.16 = (bf16[512,128]{1,0:T(8,128)(2,1)S(1)}, bf16[512,128]{1,0:T(8,128)(2,1)S(1)}, u32[]{:S(2)}, u32[]{:S(2)}) collective-permute-start(bf16[512,128]{1,0:T(8,128)(2,1)S(1)} %fusion.16), channel_id=1, source_target_pairs={{0,8},{8,0},{1,9},{9,1},{2,10},{10,2},{3,11},{11,3},{4,12},{12,4},... | collective-permute-start | bytes 393224 | tf_op jit(solution)/shard_map/ppermute | solution.py:344

commit v2 on v1

--- a/solution.py
+++ b/solution.py
@@ -14,7 +14,7 @@
 TP = 8
 BIG = 32 << 20
 CHEAP = pl.CostEstimate(flops=1, bytes_accessed=1, transcendentals=0)
-LONG = pl.CostEstimate(flops=9_000_000_000, bytes_accessed=1, transcendentals=0)
+LONG = pl.CostEstimate(flops=23_000_000_000, bytes_accessed=1, transcendentals=0)
 SEC = ("x", "zh", "zl", "yh")
 TPA = ("yl", "c")
 NEAR = ("x", "zl")
@@ -46,34 +46,22 @@
     )
 
 
-def three_terms(value):
-    top = value.astype(jnp.bfloat16).astype(jnp.float32)
-    rest = value - top
+def prepare_kernel(x_ref, scale_ref, out_ref):
+    scale = scale_ref[...]
+    top = scale.astype(jnp.bfloat16).astype(jnp.float32)
+    rest = scale - top
     mid = rest.astype(jnp.bfloat16).astype(jnp.float32)
-    return top, mid, rest - mid
-
-
-def prepare_kernel(x_ref, scale_ref, out_ref):
-    squares = jnp.zeros((128, 128), jnp.float32)
-    for lane in range(8):
-        x = x_ref[:, lane * 128 : (lane + 1) * 128].astype(jnp.float32)
-        squares += x * x
-    squares = jnp.sum(jnp.transpose(squares), axis=0, keepdims=True)
-    squares = jnp.concatenate([squares] + [jnp.zeros((1, 896), jnp.float32)], axis=1)
-    row = lax.broadcasted_iota(jnp.int32, (16, 1024), 0)
-    extra = jnp.zeros((16, 1024), jnp.float32)
-    for index, term in enumerate(three_terms(scale_ref[...]) + three_terms(squares)):
-        extra = jnp.where(row == index, term, extra)
-    extra = extra.astype(jnp.bfloat16)
-    for copy in range(4):
-        out_ref[copy, 0:128, :] = x_ref[...]
-        out_ref[copy, 128:144, :] = extra
+    low = rest - mid
+    row = lax.broadcasted_iota(jnp.int32, (16, scale.shape[1]), 0)
+    extra = jnp.where(row == 0, top, jnp.where(row == 1, mid, jnp.where(row == 2, low, 0.0)))
+    out_ref[0:128, :] = x_ref[...]
+    out_ref[128:144, :] = extra.astype(jnp.bfloat16)
 
 
 def prepare(hidden, scale):
     return pl.pallas_call(
         prepare_kernel,
-        out_shape=jax.ShapeDtypeStruct((4, 144, 1024), jnp.bfloat16),
+        out_shape=jax.ShapeDtypeStruct((144, 1024), jnp.bfloat16),
         compiler_params=pltpu.CompilerParams(vmem_limit_bytes=BIG),
         cost_estimate=CHEAP,
         name="prepare",
@@ -99,7 +87,7 @@
     def _():
         for part in range(4):
             prod = dot_nt(dv_ref[...], rot[part * 512 : (part + 1) * 512]).astype(jnp.bfloat16)
-            chip = (step * 2 + part // 2 + 4 - core_ref[1]) % 4
+            chip = step * 2 + part // 2
 
             @pl.when(core == part % 2)
             def _():
@@ -138,54 +126,32 @@
             half,
         ],
         compiler_params=pltpu.CompilerParams(vmem_limit_bytes=BIG),
-        cost_estimate=pl.CostEstimate(flops=23000000000, bytes_accessed=1, transcendentals=0),
+        cost_estimate=LONG,
         name="rotate",
     )(core, weight, rotor, value_grad)
 
 
-def weight_grad_kernel(core_ref, rot_ref, top_ref, dv_ref, send_ref, keep_ref):
-    index = pl.program_id(0)
+def weight_grad_kernel(rot_ref, top_ref, dv_ref, out_ref):
     step = top_ref[...] / 7.0 + SCALE_FLOOR
     quant = soft_quant(rot_ref[...].astype(jnp.float32), 1.0 / step, step * 7.0)
-    prod = dot_nt(dv_ref[...], quant.astype(jnp.bfloat16)).astype(jnp.bfloat16)
-
-    @pl.when(index < 4)
-    def _():
-        send_ref[0] = prod
-
-    @pl.when(index >= 4)
-    def _():
-        keep_ref[0] = prod
-
-
-def weight_grad(core, rot, top, value_grad):
-    half = jax.ShapeDtypeStruct((4, 128, 1024), jnp.bfloat16)
+    out_ref[0] = dot_nt(dv_ref[...], quant.astype(jnp.bfloat16)).astype(jnp.bfloat16)
+
+
+def weight_grad(rot, top, value_grad):
     return pl.pallas_call(
         weight_grad_kernel,
-        grid_spec=pltpu.PrefetchScalarGridSpec(
-            num_scalar_prefetch=1,
-            grid=(8,),
-            in_specs=[
-                pl.BlockSpec(
-                    (1024, 128),
-                    lambda i, core: (
-                        ((i + core[1]) % 4) * 2 + jnp.where(i < 4, 1 - core[0], core[0]),
-                        0,
-                    ),
-                ),
-                pl.BlockSpec((1, 128), lambda i, core: (0, 0)),
-                pl.BlockSpec((128, 128), lambda i, core: (0, 0)),
-            ],
-            out_specs=[
-                pl.BlockSpec((1, 128, 1024), lambda i, core: (jnp.minimum(i, 3), 0, 0)),
-                pl.BlockSpec((1, 128, 1024), lambda i, core: (jnp.maximum(i - 4, 0), 0, 0)),
-            ],
-        ),
-        out_shape=[half, half],
-        compiler_params=pltpu.CompilerParams(vmem_limit_bytes=BIG),
-        cost_estimate=pl.CostEstimate(flops=10350000000, bytes_accessed=1, transcendentals=0),
+        grid=(8,),
+        in_specs=[
+            pl.BlockSpec((1024, 128), lambda i: (i, 0)),
+            pl.BlockSpec((1, 128), lambda i: (0, 0)),
+            pl.BlockSpec((128, 128), lambda i: (0, 0)),
+        ],
+        out_specs=pl.BlockSpec((1, 128, 1024), lambda i: (i, 0, 0)),
+        out_shape=jax.ShapeDtypeStruct((8, 128, 1024), jnp.bfloat16),
+        compiler_params=pltpu.CompilerParams(vmem_limit_bytes=BIG),
+        cost_estimate=CHEAP,
         name="weight_grad",
-    )(core, rot, top, value_grad)
+    )(rot, top, value_grad)
 
 
 def quant_kernel(core_ref, all_ref, mask_ref, inv_ref, quant_ref):
@@ -220,7 +186,7 @@
         ),
         out_shape=jax.ShapeDtypeStruct((8, 128, 512), jnp.bfloat16),
         compiler_params=pltpu.CompilerParams(vmem_limit_bytes=BIG),
-        cost_estimate=CHEAP,
+        cost_estimate=pl.CostEstimate(flops=10_350_000_000, bytes_accessed=1, transcendentals=0),
         name="quantize",
     )(core, hidden_all, mask, inverse)
 
@@ -282,19 +248,12 @@
     )(core, mine, other, weight, weight, value_grad)
 
 
-def outer_kernel(place_ref, frame_ref, mine_ref, other_ref, out_ref, left_ref):
-    x, zl, yh = place_ref[2], place_ref[3], place_ref[4]
-
-    @pl.when(pl.program_id(0) == 0)
-    def _():
-        for near in range(8):
-            turn = (near // 2 + 4 - x) % 4
-            flip = (near % 2 + zl) % 2
-            left_ref[near * 128 : (near + 1) * 128, :] = frame_ref[turn * 2 + flip]
+def outer_kernel(place_ref, frame_ref, mine_ref, other_ref, out_ref):
+    yh = place_ref[1]
 
     def product(quant_ref):
         prod = lax.dot_general(
-            left_ref[...],
+            frame_ref[...],
             quant_ref[...],
             (((0,), (0,)), ((), ())),
             preferred_element_type=jnp.float32,
@@ -318,7 +277,7 @@
             num_scalar_prefetch=1,
             grid=(4,),
             in_specs=[
-                pl.BlockSpec((8, 128, 512), lambda i, place: (0, 0, 0)),
+                pl.BlockSpec((1024, 512), lambda i, place: (0, 0)),
                 pl.BlockSpec((1024, 256), lambda i, place: (0, jnp.minimum(i, 1))),
                 pl.BlockSpec((1024, 256), lambda i, place: (0, jnp.maximum(i - 2, 0))),
             ],
@@ -326,7 +285,6 @@
                 (2, 512, 128),
                 lambda i, place: (jnp.where(i < 2, place[0], 1 - place[0]) * 2 + i % 2, 0, 0),
             ),
-            scratch_shapes=[pltpu.VMEM((1024, 512), jnp.bfloat16)],
         ),
         out_shape=jax.ShapeDtypeStruct((8, 512, 128), jnp.bfloat16),
         compiler_params=pltpu.CompilerParams(vmem_limit_bytes=BIG),
@@ -351,50 +309,40 @@
 def local(hidden_in, grad_sent, value_grad, value_weight, rotation, act_scale, outliers):
     sections = 64
     pairs = [(source, (source - 1) % sections) for source in range(sections)]
-    place = jnp.stack([lax.axis_index(axis) for axis in ("c", "yl", "x", "zl", "yh")])
-    place = place.astype(jnp.int32)
+    place = jnp.stack([lax.axis_index("c"), lax.axis_index("yh")]).astype(jnp.int32)
     wide = lambda value: value.astype(jnp.float32)
     tie = lax.optimization_barrier
 
-    def chip_sum(pair):
-        total = pair[0]
-        for turn in (1, 2, 3):
-            total = total + wide(shifted(pair[turn].astype(jnp.bfloat16), "yl", turn))
-        return total
-
-    hidden_all = exchange(prepare(hidden_in, act_scale), "yl")
+    hidden_all = lax.all_gather(prepare(hidden_in, act_scale), "yl", axis=0)
 
     rot, peak, frame_keep, frame_send = rotate(place, value_weight, rotation, value_grad)
-    frame_recv = swap_core(frame_send)
-    frame = chip_sum([wide(frame_keep[turn]) + wide(frame_recv[turn]) for turn in range(4)])
-    frame = frame.astype(jnp.bfloat16)
-    grad_send, grad_keep = weight_grad(place, rot, peak, value_grad)
-    hidden_all, frame, grad_send, grad_keep, grad_sent = tie(
-        (hidden_all, frame, grad_send, grad_keep, grad_sent)
-    )
-    pair = jnp.stack([frame, shifted(frame, "zl", 1)])
+    frame_pair = (wide(frame_keep) + wide(swap_core(frame_send))).astype(jnp.bfloat16)
+    rot, frame_pair, hidden_two = tie((rot, frame_pair, hidden_in))
+    frame_terms = exchange(frame_pair, "yl")
+    squares = jnp.sum(wide(hidden_two) * wide(hidden_two), axis=1).reshape(1, 128)
+    squares = squares + swap_core(squares)
+    moved = [shifted(squares, "yl", turn) for turn in (1, 2, 3)]
+    inverse = lax.rsqrt((squares + moved[0] + moved[1] + moved[2]) / 8192.0 + NORM_EPS)
+    frame_terms, inverse, rot = tie((frame_terms, inverse, rot))
+    frame = jnp.sum(wide(frame_terms), axis=0).astype(jnp.bfloat16)
+    frames = exchange(jnp.broadcast_to(frame[None], (8, 128, 512)), NEAR).reshape(1024, 512)
+    grad_parts = weight_grad(rot, peak, value_grad)
+
     ids = outliers[0]
     blocks = (ids[None, :] // 128 == jnp.arange(64)[:, None]).astype(jnp.bfloat16)
     lanes = (ids[:, None] % 128 == jnp.arange(128)[None, :]).astype(jnp.bfloat16)
     mask = jnp.dot(blocks, lanes, preferred_element_type=jnp.float32).reshape(TP, 1, 1024)
 
-    squares = jnp.sum(wide(hidden_all[:, 131:134, :128]), axis=(0, 1)).reshape(1, 128)
-    inverse = lax.rsqrt((squares + swap_core(squares)) / 8192.0 + NORM_EPS)
+    hidden_all, mask, grad_parts = tie((hidden_all, mask, grad_parts))
+    grad_sum = lax.psum_scatter(grad_parts, TPA, scatter_dimension=0, tiled=False)
     quant = quantize(place, hidden_all, mask, inverse)
-    quant, pair = tie((quant, pair))
+    frames, quant = tie((frames, quant))
     quants = exchange(quant, NEAR)
-    before, after = shifted(pair, "x", 1), shifted(pair, "x", -1)
-    across = jnp.concatenate([shifted(before[:, :64], "x", 1), shifted(after[:, 64:], "x", -1)], 1)
-    frames = jnp.concatenate([pair, after, across, before])
+    r2_grad = rotor_grad(place, quant, swap_core(quant), value_weight, value_grad)
+    quants, r2_grad, grad_sent = tie((quants, r2_grad, grad_sent))
+    quants_other = swap_core(quants)
     incoming = lax.ppermute(grad_sent, SEC, pairs)
-    quants, frames, incoming, quant, grad_send, grad_keep = tie(
-        (quants, frames, incoming, quant, grad_send, grad_keep)
-    )
-    quants_other = swap_core(quants)
     parts = outer(place, frames, quants.reshape(1024, 512), quants_other.reshape(1024, 512))
-    r2_grad = rotor_grad(place, quant, swap_core(quant), value_weight, value_grad)
-    grad_recv = swap_core(grad_send)
-    grad_sum = chip_sum([wide(grad_keep[turn]) + wide(grad_recv[turn]) for turn in range(4)])
     parts = exchange(parts, "zh").reshape(4, 2, 512, 128)
     sums = jnp.sum(wide(parts), axis=0)
     r1_grad = sums[0] + wide(shifted(sums[1].astype(jnp.bfloat16), "yh", 1))
@@ -404,7 +352,7 @@
     normed = wide(hidden_in) * inverse
     bounded = jnp.tanh(normed / (7.0 * act_scale))
     slope = jnp.where(mask_mine > 0.0, 1.0, 1.0 - bounded * bounded)
-    emitted = (wide(incoming) + inverse * (grad_sum * slope)).astype(jnp.bfloat16)
+    emitted = (wide(incoming) + inverse * (wide(grad_sum) * slope)).astype(jnp.bfloat16)
     return (emitted, r1_grad, r2_grad)
 
 

time: 178 us -> 158 us (0.89)
  the two profiles are of different devices: /device:TPU:1 before, /device:TPU:48 now
where the time goes in v2:
time: 158 us; the launch traced here: 157 us
  waiting for transfers between devices  58.1 us (37%)
  starting transfers between devices  51.6 us (33%)
  Pallas kernels  18.4 us (12%)
  between operations  14.2 us (9%)
  local copies, waits for them, and re-layouts  9.01 us (6%)
  other arithmetic  5.12 us (3%)
    all_to_all x4, waiting for transfers between devices, exchange(): return lax.all_to_all(value, axes, split_axis=0, concat_axis=0, tiled=True)  35.1 us
    all_to_all x4, starting transfers between devices, exchange(): return lax.all_to_all(value, axes, split_axis=0, concat_axis=0, tiled=True)  30 us
    ppermute x8, waiting for transfers between devices, shifted(): lax.ppermute(value, axis, [(chip, (chip + turn) % count) for chip in rang...  20.4 us
    ppermute x8, starting transfers between devices, shifted(): lax.ppermute(value, axis, [(chip, (chip + turn) % count) for chip in rang...  18.3 us
    unnamed x26, local copies, waits for them, and re-layouts  7.94 us
    pallas_call x1, Pallas kernels, outer(): pl.pallas_call(outer_kernel, grid_spec=pltpu.PrefetchScalarGridSpec(num_s...  4.58 us
    pallas_call x1, Pallas kernels, weight_grad(): pl.pallas_call(weight_grad_kernel, grid=(8,), in_specs=[pl.BlockSpec((102...  4.37 us
    pallas_call x1, Pallas kernels, rotate(): pl.pallas_call(rotate_kernel, grid_spec=pltpu.PrefetchScalarGridSpec(num_...  3.49 us
  transfers between devices with their start and end apart: 15, of which 12 were waited for; matrix products, arithmetic and copies ran while one was open for 4% of the time, Pallas kernels for 10%

profile of v2, /device:TPU:48, one launch (start us, length us, event | category | flops | bytes accessed | tf_op | source)
XLA Modules:
  0.0 156.7 jit_solution(3806341786114504061)
XLA Ops:
  7.2 0.0 all-gather.3.cloned.1.call-start
  7.2 0.1 pad_add_fusion.core_ref.place_ref
  7.3 0.0 copy-start
  7.3 1.6 %copy-done = bf16[8192,128]{1,0:T(8,128)(2,1)S(1)} copy-done((bf16[8192,128]{1,0:T(8,128)(2,1)S(1)}, bf16[8192,128]{1,0:T(8,128)(2,1)}, u32[]{:S(2)}) %copy-start) | copy-done | bytes 2097176
  8.9 0.0 copy-start.6
  8.9 0.8 copy-done.6
  9.6 0.8 copy-done.10
  10.4 3.5 %rotate.1 = (bf16[8192,128]{1,0:T(8,128)(2,1)S(1)}, f32[1,128]{1,0:T(1,128)S(1)}, bf16[4,128,512]{2,1,0:T(8,128)(2,1)S(1)}, bf16[4,128,512]{2,1,0:T(8,128)(2,1)S(1)}) custom-call(s32[2]{0:T(128)S(1)} %pad_add_fusion.core_ref.place_ref, bf16[8192,128]{1,0:T(8,128)(2,1)S(1)} %copy-done, bf16[128,128]{1,0:T(8,128)(2,1)S(1)} %copy-done.10, ...), custom_call_target="tpu_custom_call" | custom-call | flops 23000000512 | bytes 1 | tf_op jit(solution)/shard_map/rotate/pallas_call | solution.py:105
  13.9 1.9 %collective-permute-start = (bf16[4,128,512]{2,1,0:T(8,128)(2,1)S(1)}, bf16[4,128,512]{2,1,0:T(8,128)(2,1)}, u32[]{:S(2)}, u32[]{:S(2)}) collective-permute-start(bf16[4,128,512]{2,1,0:T(8,128)(2,1)S(1)} %get-tuple-element.23), channel_id=1, source_target_pairs={{0,1},{1,0},{2,3},{3,2},{4,5},{5,4},{6,7},{7,6},{8,9},{9,8},{10,11... | collective-permute-start | bytes 1572872 | tf_op jit(solution)/shard_map/ppermute | solution.py:302
  15.8 0.0 copy-done.5
  15.8 0.0 copy-done.8
  15.9 0.8 prepare.1
  16.6 0.0 all-gather.3.cloned.1.call-update
  16.6 1.2 collective-permute-done
  17.8 2.0 %add_convert_fusion = bf16[4,128,512]{2,1,0:T(8,128)(2,1)} fusion(bf16[4,128,512]{2,1,0:T(8,128)(2,1)} %collective-permute-done, bf16[4,128,512]{2,1,0:T(8,128)(2,1)S(1)} %get-tuple-element.22), kind=kLoop, calls=%fused_computation.1 | loop fusion | flops 1048576 | bytes 1572864 | tf_op jit(solution)/shard_map/convert_element_type | solution.py:319
  19.8 5.6 %all-to-all-start = ((bf16[4,128,512]{2,1,0:T(8,128)(2,1)}), bf16[4,128,512]{2,1,0:T(8,128)(2,1)S(1)}, u32[]{:S(2)}, u32[]{:S(2)}) async-start(bf16[4,128,512]{2,1,0:T(8,128)(2,1)} %add_convert_fusion), calls=%async_computation | async-start | bytes 1048576 | tf_op jit(solution)/shard_map/all_to_all | solution.py:297
  25.4 0.1 multiply_reduce_fusion
  25.5 1.9 %collective-permute-start.1 = (f32[1,128]{1,0:T(1,128)S(1)}, f32[1,128]{1,0:T(1,128)S(1)}, u32[]{:S(2)}, u32[]{:S(2)}) collective-permute-start(f32[1,128]{1,0:T(1,128)S(1)} %bitcast.37), channel_id=1, source_target_pairs={{0,1},{1,0},{2,3},{3,2},{4,5},{5,4},{6,7},{7,6},{8,9},{9,8},{10,11... | collective-permute-start | bytes 1544 | tf_op jit(solution)/shard_map/ppermute | solution.py:302
  27.4 1.1 collective-permute-done.1
  28.5 3.4 %collective-permute-start.2 = (f32[1,128]{1,0:T(1,128)S(1)}, f32[1,128]{1,0:T(1,128)S(1)}, u32[]{:S(2)}, u32[]{:S(2)}) collective-permute-start(f32[1,128]{1,0:T(1,128)S(1)} %bitcast_add_fusion), channel_id=1, source_target_pairs={{0,2},{2,4},{4,6},{6,0},{1,3},{3,5},{5,7},{7,1},{8,10},{10,12},{12... | collective-permute-start | bytes 1544 | tf_op jit(solution)/shard_map/ppermute | solution.py:302
  31.9 2.5 %collective-permute-start.3 = (f32[1,128]{1,0:T(1,128)S(1)}, f32[1,128]{1,0:T(1,128)S(1)}, u32[]{:S(2)}, u32[]{:S(2)}) collective-permute-start(f32[1,128]{1,0:T(1,128)S(1)} %bitcast_add_fusion), channel_id=1, source_target_pairs={{0,4},{2,6},{4,0},{6,2},{1,5},{3,7},{5,1},{7,3},{8,12},{10,14},{12... | collective-permute-start | bytes 1544 | tf_op jit(solution)/shard_map/ppermute | solution.py:302
  34.4 2.9 %collective-permute-start.4 = (f32[1,128]{1,0:T(1,128)S(1)}, f32[1,128]{1,0:T(1,128)S(1)}, u32[]{:S(2)}, u32[]{:S(2)}) collective-permute-start(f32[1,128]{1,0:T(1,128)S(1)} %bitcast_add_fusion), channel_id=1, source_target_pairs={{0,6},{2,0},{4,2},{6,4},{1,7},{3,1},{5,3},{7,5},{8,14},{10,8},{12,... | collective-permute-start | bytes 1544 | tf_op jit(solution)/shard_map/ppermute | solution.py:302
  37.3 0.8 collective-permute-done.2
  38.1 0.1 collective-permute-done.3
  38.2 1.6 %collective-permute-done.4 = f32[1,128]{1,0:T(1,128)S(1)} collective-permute-done((f32[1,128]{1,0:T(1,128)S(1)}, f32[1,128]{1,0:T(1,128)S(1)}, u32[]{:S(2)}, u32[]{:S(2)}) %collective-permute-start.4) | collective-permute-done | bytes 544 | tf_op jit(solution)/shard_map/ppermute | solution.py:302
  39.8 0.0 all-to-all-done
  39.8 0.1 reduce_sum.31
  39.9 1.1 broadcast_in_dim.20
  41.0 8.2 %all-to-all-start.1 = ((bf16[8,128,512]{2,1,0:T(8,128)(2,1)}), bf16[8,128,512]{2,1,0:T(8,128)(2,1)S(1)}, u32[]{:S(2)}, u32[]{:S(2)}) async-start(bf16[8,128,512]{2,1,0:T(8,128)(2,1)} %broadcast_in_dim.20), calls=%async_computation.1 | async-start | bytes 2097152 | tf_op jit(solution)/shard_map/all_to_all | solution.py:297
  49.2 0.0 copy-done.12
  49.2 0.2 fusion.5
  49.4 0.0 copy-done.7
  49.4 4.4 %weight_grad.1 = bf16[8,128,1024]{2,1,0:T(8,128)(2,1)S(1)} custom-call(bf16[8192,128]{1,0:T(8,128)(2,1)S(1)} %get-tuple-element.28.rot_ref, f32[1,128]{1,0:T(1,128)S(1)} %get-tuple-element.29.top_ref, bf16[128,128]{1,0:T(8,128)(2,1)S(1)} %copy-done.7), custom_call_target="tpu_custom_call" | custom-call | flops 1 | bytes 1 | tf_op jit(solution)/shard_map/weight_grad/pallas_call | solution.py:141
  53.8 0.0 copy-start.2
  53.8 1.3 copy-done.2
  55.1 1.9 %all-gather.3.cloned.1.call-done = bf16[576,1024]{1,0:T(8,128)(2,1)} async-done(((bf16[144,1024]{1,0:T(8,128)(2,1)}), bf16[576,1024]{1,0:T(8,128)(2,1)}) %all-gather.3.cloned.1.call-update) | async-done | bytes 1179664 | tf_op jit(solution)/shard_map/all_gather | solution.py:316
  57.0 1.3 copy-done.9
  58.3 2.5 %quantize.1.mine_ref = bf16[8,128,512]{2,1,0:T(8,128)(2,1)S(1)} custom-call(s32[2]{0:T(128)S(1)} %pad_add_fusion.core_ref.place_ref, bf16[4,144,1024]{2,1,0:T(8,128)(2,1)S(1)} %bitcast.34, f32[8,1,1024]{2,1,0:T(1,128)S(1)} %bitcast.32, f32[1,128]{1,0:T(1,128)S(1)} %add_rsqrt_fusion.inv_ref), custom_call_target="tpu_custom_call" | custom-call | flops 10350000128 | bytes 1 | tf_op jit(solution)/shard_map/quantize/pallas_call | solution.py:175
  60.9 0.0 copy-start.3
  60.9 1.0 copy-done.3
  61.9 0.1 all-to-all-done.1
  61.9 5.8 %all-to-all-start.2 = ((bf16[8,128,512]{2,1,0:T(8,128)(2,1)}), bf16[8,128,512]{2,1,0:T(8,128)(2,1)}, u32[]{:S(2)}, u32[]{:S(2)}) async-start(bf16[8,128,512]{2,1,0:T(8,128)(2,1)} %copy-done.3), calls=%async_computation.2 | async-start | bytes 2097152 | tf_op jit(solution)/shard_map/all_to_all | solution.py:297
  67.8 0.0 reduce-scatter.2.cloned.1.call-start
  67.8 0.7 reduce-scatter.2.cloned.1.call-update
  68.5 1.9 %collective-permute-start.5 = (bf16[8,128,512]{2,1,0:T(8,128)(2,1)}, bf16[8,128,512]{2,1,0:T(8,128)(2,1)S(1)}, u32[]{:S(2)}, u32[]{:S(2)}) collective-permute-start(bf16[8,128,512]{2,1,0:T(8,128)(2,1)} %copy-done.3), channel_id=1, source_target_pairs={{0,1},{1,0},{2,3},{3,2},{4,5},{5,4},{6,7},{7,6},{8,9},{9,8},{10,11... | collective-permute-start | bytes 3145736 | tf_op jit(solution)/shard_map/ppermute | solution.py:302
  70.4 2.8 %collective-permute-done.5.other_ref = bf16[8,128,512]{2,1,0:T(8,128)(2,1)S(1)} collective-permute-done((bf16[8,128,512]{2,1,0:T(8,128)(2,1)}, bf16[8,128,512]{2,1,0:T(8,128)(2,1)S(1)}, u32[]{:S(2)}, u32[]{:S(2)}) %collective-permute-start.5) | collective-permute-done | bytes 1048608 | tf_op jit(solution)/shard_map/ppermute | solution.py:302
  73.3 0.0 copy-done.1
  73.3 1.2 copy-done.4
  74.5 2.7 %rotor_grad.1 = f32[128,128]{1,0:T(8,128)} custom-call(s32[2]{0:T(128)S(1)} %pad_add_fusion.core_ref.place_ref, bf16[8,128,512]{2,1,0:T(8,128)(2,1)S(1)} %copy-done.4, bf16[8,128,512]{2,1,0:T(8,128)(2,1)S(1)} %collective-permute-done.5.other_ref, bf16[8,1024,128]{2,1,0:T(8,128)(2,1)S(1)} %bitcast.27, bf16[8,1024,128]{2,1,0:T(8,128)(2,1)S(1)} %bitcast.28, ...), custom_call_target="tpu_custom_call" | custom-call | flops 1 | bytes 1 | tf_op jit(solution)/shard_map/rotor_grad/pallas_call | solution.py:229
  77.2 6.6 %all-to-all-done.2 = bf16[8,128,512]{2,1,0:T(8,128)(2,1)} async-done(((bf16[8,128,512]{2,1,0:T(8,128)(2,1)}), bf16[8,128,512]{2,1,0:T(8,128)(2,1)}, u32[]{:S(2)}, u32[]{:S(2)}) %all-to-all-start.2) | async-done | bytes 1048608 | tf_op jit(solution)/shard_map/all_to_all | solution.py:297
  83.8 1.9 %collective-permute-start.7 = (bf16[8,128,512]{2,1,0:T(8,128)(2,1)}, bf16[8,128,512]{2,1,0:T(8,128)(2,1)S(1)}, u32[]{:S(2)}, u32[]{:S(2)}) collective-permute-start(bf16[8,128,512]{2,1,0:T(8,128)(2,1)} %all-to-all-done.2), channel_id=1, source_target_pairs={{0,1},{1,0},{2,3},{3,2},{4,5},{5,4},{6,7},{7,6},{8,9},{9,8},{10,11... | collective-permute-start | bytes 3145736 | tf_op jit(solution)/shard_map/ppermute | solution.py:302
  85.8 2.8 %collective-permute-done.7 = bf16[8,128,512]{2,1,0:T(8,128)(2,1)S(1)} collective-permute-done((bf16[8,128,512]{2,1,0:T(8,128)(2,1)}, bf16[8,128,512]{2,1,0:T(8,128)(2,1)S(1)}, u32[]{:S(2)}, u32[]{:S(2)}) %collective-permute-start.7) | collective-permute-done | bytes 1048608 | tf_op jit(solution)/shard_map/ppermute | solution.py:302
  88.6 4.6 %outer.1 = bf16[8,512,128]{2,1,0:T(8,128)(2,1)} custom-call(s32[2]{0:T(128)S(1)} %pad_add_fusion.core_ref.place_ref, bf16[1024,512]{1,0:T(8,128)(2,1)S(1)} %bitcast.29, bf16[1024,512]{1,0:T(8,128)(2,1)} %bitcast.12.mine_ref, bf16[1024,512]{1,0:T(8,128)(2,1)S(1)} %bitcast.30), custom_call_target="tpu_custom_call" | custom-call | flops 1 | bytes 1 | tf_op jit(solution)/shard_map/outer/pallas_call | solution.py:274
  93.2 10.4 %all-to-all-start.3 = ((bf16[8,512,128]{2,1,0:T(8,128)(2,1)}), bf16[8,512,128]{2,1,0:T(8,128)(2,1)S(1)}, u32[]{:S(2)}, u32[]{:S(2)}) async-start(bf16[8,512,128]{2,1,0:T(8,128)(2,1)} %outer.1), calls=%async_computation.4 | async-start | bytes 2097152 | tf_op jit(solution)/shard_map/all_to_all | solution.py:297
  103.6 0.0 copy-done.11
  103.6 3.2 %collective-permute-start.6 = (bf16[128,1024]{1,0:T(8,128)(2,1)S(1)}, bf16[128,1024]{1,0:T(8,128)(2,1)S(1)}, u32[]{:S(2)}, u32[]{:S(2)}) collective-permute-start(bf16[128,1024]{1,0:T(8,128)(2,1)S(1)} %copy-done.11), channel_id=1, source_target_pairs={{0,504},{8,0},{16,8},{24,16},{32,24},{40,32},{48,40},{56,48},{64,5... | collective-permute-start | bytes 786440 | tf_op jit(solution)/shard_map/ppermute | solution.py:344
  106.8 28.4 %all-to-all-done.3 = bf16[8,512,128]{2,1,0:T(8,128)(2,1)S(1)} async-done(((bf16[8,512,128]{2,1,0:T(8,128)(2,1)}), bf16[8,512,128]{2,1,0:T(8,128)(2,1)S(1)}, u32[]{:S(2)}, u32[]{:S(2)}) %all-to-all-start.3) | async-done | bytes 1048608 | tf_op jit(solution)/shard_map/all_to_all | solution.py:297
  135.2 0.1 convert_reduce_fusion
  135.4 1.9 %collective-permute-start.8 = (bf16[512,128]{1,0:T(8,128)(2,1)S(1)}, bf16[512,128]{1,0:T(8,128)(2,1)S(1)}, u32[]{:S(2)}, u32[]{:S(2)}) collective-permute-start(bf16[512,128]{1,0:T(8,128)(2,1)S(1)} %fusion.4), channel_id=1, source_target_pairs={{0,8},{8,0},{1,9},{9,1},{2,10},{10,2},{3,11},{11,3},{4,12},{12,4},... | collective-permute-start | bytes 393224 | tf_op jit(solution)/shard_map/ppermute | solution.py:302
  137.3 0.0 collective-permute-done.6
  137.3 0.0 reduce-scatter.2.cloned.1.call-done
  137.4 1.9 %fusion.2 = bf16[128,1024]{1,0:T(8,128)(2,1)} fusion(bf16[128,1024]{1,0:T(8,128)(2,1)S(1)} %copy-done.5, bf16[128,1024]{1,0:T(8,128)(2,1)S(1)} %collective-permute-done.6, bf16[1,128,1024]{2,1,0:T(8,128)(2,1)} %reduce-scatter.2.cloned.1.call-done, f32[1024]{0:T(1024)S(1)} %bitcast.36, f32[128]{0:T(128)S(1)} %bitcast.31, pred[1024]{0:T(1024)(128)(4,1)S(1)} %compare_reduce_fusion), kind=kLoop, calls=%fused_computation.5 | loop fusion | flops 1572864 | bytes 1054208 | tf_op jit(solution)/shard_map/convert_element_type | solution.py:355
  139.3 9.9 %collective-permute-done.8 = bf16[512,128]{1,0:T(8,128)(2,1)S(1)} collective-permute-done((bf16[512,128]{1,0:T(8,128)(2,1)S(1)}, bf16[512,128]{1,0:T(8,128)(2,1)S(1)}, u32[]{:S(2)}, u32[]{:S(2)}) %collective-permute-start.8) | collective-permute-done | bytes 131104 | tf_op jit(solution)/shard_map/ppermute | solution.py:302
  149.2 0.7 fusion.3
  (16 shorter events, 0.1 us)
Async XLA Ops:
  7.2 49.9 %all-gather.3.cloned.1.call-start = ((), (), s32[]{:S(2)}) async-start(), calls=%async_computation.6 | async-start | bytes 1474560 | tf_op jit(solution)/shard_map/all_gather | solution.py:316
  7.3 1.6 %copy-start = (bf16[8192,128]{1,0:T(8,128)(2,1)S(1)}, bf16[8192,128]{1,0:T(8,128)(2,1)}, u32[]{:S(2)}) copy-start(bf16[8192,128]{1,0:T(8,128)(2,1)} %w_ref.1) | copy-start | bytes 6291460
  8.9 0.8 copy-start.6
  9.6 0.8 copy-start.10
  10.4 5.4 %copy-start.5 = (bf16[128,1024]{1,0:T(8,128)(2,1)S(1)}, bf16[128,1024]{1,0:T(8,128)(2,1)}, u32[]{:S(2)}) copy-start(bf16[128,1024]{1,0:T(8,128)(2,1)} %x_ref.1) | copy-start | bytes 786436
  10.4 5.4 %copy-start.8 = (f32[1,1024]{1,0:T(1,128)S(1)}, f32[1,1024]{1,0:T(1,128)}, u32[]{:S(2)}) copy-start(f32[1,1024]{1,0:T(1,128)} %scale_ref.1) | copy-start | bytes 12292
  13.9 3.9 %collective-permute-start = (bf16[4,128,512]{2,1,0:T(8,128)(2,1)S(1)}, bf16[4,128,512]{2,1,0:T(8,128)(2,1)}, u32[]{:S(2)}, u32[]{:S(2)}) collective-permute-start(bf16[4,128,512]{2,1,0:T(8,128)(2,1)S(1)} %get-tuple-element.23), channel_id=1, source_target_pairs={{0,1},{1,0},{2,3},{3,2},{4,5},{5,4},{6,7},{7,6},{8,9},{9,8},{10,11... | collective-permute-start | bytes 1572872 | tf_op jit(solution)/shard_map/ppermute | solution.py:302
  19.8 20.0 %all-to-all-start = ((bf16[4,128,512]{2,1,0:T(8,128)(2,1)}), bf16[4,128,512]{2,1,0:T(8,128)(2,1)S(1)}, u32[]{:S(2)}, u32[]{:S(2)}) async-start(bf16[4,128,512]{2,1,0:T(8,128)(2,1)} %add_convert_fusion), calls=%async_computation | async-start | bytes 1048576 | tf_op jit(solution)/shard_map/all_to_all | solution.py:297
  25.4 23.8 %copy-start.12 = (s32[1,128]{1,0:T(1,128)S(1)}, s32[1,128]{1,0:T(1,128)}, u32[]{:S(2)}) copy-start(s32[1,128]{1,0:T(1,128)} %param.13) | copy-start | bytes 1540
  25.4 24.0 %copy-start.7 = (bf16[128,128]{1,0:T(8,128)(2,1)S(1)}, bf16[128,128]{1,0:T(8,128)(2,1)}, u32[]{:S(2)}) copy-start(bf16[128,128]{1,0:T(8,128)(2,1)} %dv_ref.5) | copy-start | bytes 98308
  25.5 3.0 %collective-permute-start.1 = (f32[1,128]{1,0:T(1,128)S(1)}, f32[1,128]{1,0:T(1,128)S(1)}, u32[]{:S(2)}, u32[]{:S(2)}) collective-permute-start(f32[1,128]{1,0:T(1,128)S(1)} %bitcast.37), channel_id=1, source_target_pairs={{0,1},{1,0},{2,3},{3,2},{4,5},{5,4},{6,7},{7,6},{8,9},{9,8},{10,11... | collective-permute-start | bytes 1544 | tf_op jit(solution)/shard_map/ppermute | solution.py:302
  28.5 9.6 %collective-permute-start.2 = (f32[1,128]{1,0:T(1,128)S(1)}, f32[1,128]{1,0:T(1,128)S(1)}, u32[]{:S(2)}, u32[]{:S(2)}) collective-permute-start(f32[1,128]{1,0:T(1,128)S(1)} %bitcast_add_fusion), channel_id=1, source_target_pairs={{0,2},{2,4},{4,6},{6,0},{1,3},{3,5},{5,7},{7,1},{8,10},{10,12},{12... | collective-permute-start | bytes 1544 | tf_op jit(solution)/shard_map/ppermute | solution.py:302
  31.9 6.3 %collective-permute-start.3 = (f32[1,128]{1,0:T(1,128)S(1)}, f32[1,128]{1,0:T(1,128)S(1)}, u32[]{:S(2)}, u32[]{:S(2)}) collective-permute-start(f32[1,128]{1,0:T(1,128)S(1)} %bitcast_add_fusion), channel_id=1, source_target_pairs={{0,4},{2,6},{4,0},{6,2},{1,5},{3,7},{5,1},{7,3},{8,12},{10,14},{12... | collective-permute-start | bytes 1544 | tf_op jit(solution)/shard_map/ppermute | solution.py:302
  34.4 5.4 %collective-permute-start.4 = (f32[1,128]{1,0:T(1,128)S(1)}, f32[1,128]{1,0:T(1,128)S(1)}, u32[]{:S(2)}, u32[]{:S(2)}) collective-permute-start(f32[1,128]{1,0:T(1,128)S(1)} %bitcast_add_fusion), channel_id=1, source_target_pairs={{0,6},{2,0},{4,2},{6,4},{1,7},{3,1},{5,3},{7,5},{8,14},{10,8},{12,... | collective-permute-start | bytes 1544 | tf_op jit(solution)/shard_map/ppermute | solution.py:302
  41.0 21.0 %all-to-all-start.1 = ((bf16[8,128,512]{2,1,0:T(8,128)(2,1)}), bf16[8,128,512]{2,1,0:T(8,128)(2,1)S(1)}, u32[]{:S(2)}, u32[]{:S(2)}) async-start(bf16[8,128,512]{2,1,0:T(8,128)(2,1)} %broadcast_in_dim.20), calls=%async_computation.1 | async-start | bytes 2097152 | tf_op jit(solution)/shard_map/all_to_all | solution.py:297
  53.8 1.3 copy-start.2
  57.0 1.3 copy-start.9
  60.9 1.0 copy-start.3
  61.9 11.3 %copy-start.1 = (bf16[8192,128]{1,0:T(8,128)(2,1)S(1)}, bf16[8192,128]{1,0:T(8,128)(2,1)}, u32[]{:S(2)}) copy-start(bf16[8192,128]{1,0:T(8,128)(2,1)} %w_ref.1) | copy-start | bytes 6291460
  61.9 21.9 %all-to-all-start.2 = ((bf16[8,128,512]{2,1,0:T(8,128)(2,1)}), bf16[8,128,512]{2,1,0:T(8,128)(2,1)}, u32[]{:S(2)}, u32[]{:S(2)}) async-start(bf16[8,128,512]{2,1,0:T(8,128)(2,1)} %copy-done.3), calls=%async_computation.2 | async-start | bytes 2097152 | tf_op jit(solution)/shard_map/all_to_all | solution.py:297
  67.8 69.6 %reduce-scatter.2.cloned.1.call-start = ((), (), s32[]{:S(2)}) async-start(), calls=%async_computation.5 | async-start | bytes 2359296 | tf_op jit(solution)/shard_map/reduce_scatter | solution.py:337
  68.5 4.8 %collective-permute-start.5 = (bf16[8,128,512]{2,1,0:T(8,128)(2,1)}, bf16[8,128,512]{2,1,0:T(8,128)(2,1)S(1)}, u32[]{:S(2)}, u32[]{:S(2)}) collective-permute-start(bf16[8,128,512]{2,1,0:T(8,128)(2,1)} %copy-done.3), channel_id=1, source_target_pairs={{0,1},{1,0},{2,3},{3,2},{4,5},{5,4},{6,7},{7,6},{8,9},{9,8},{10,11... | collective-permute-start | bytes 3145736 | tf_op jit(solution)/shard_map/ppermute | solution.py:302
  73.3 1.2 copy-start.4
  83.8 4.8 %collective-permute-start.7 = (bf16[8,128,512]{2,1,0:T(8,128)(2,1)}, bf16[8,128,512]{2,1,0:T(8,128)(2,1)S(1)}, u32[]{:S(2)}, u32[]{:S(2)}) collective-permute-start(bf16[8,128,512]{2,1,0:T(8,128)(2,1)} %all-to-all-done.2), channel_id=1, source_target_pairs={{0,1},{1,0},{2,3},{3,2},{4,5},{5,4},{6,7},{7,6},{8,9},{9,8},{10,11... | collective-permute-start | bytes 3145736 | tf_op jit(solution)/shard_map/ppermute | solution.py:302
  93.2 10.4 %copy-start.11 = (bf16[128,1024]{1,0:T(8,128)(2,1)S(1)}, bf16[128,1024]{1,0:T(8,128)(2,1)}, u32[]{:S(2)}) copy-start(bf16[128,1024]{1,0:T(8,128)(2,1)} %param.8) | copy-start | bytes 786436
  93.2 42.0 %all-to-all-start.3 = ((bf16[8,512,128]{2,1,0:T(8,128)(2,1)}), bf16[8,512,128]{2,1,0:T(8,128)(2,1)S(1)}, u32[]{:S(2)}, u32[]{:S(2)}) async-start(bf16[8,512,128]{2,1,0:T(8,128)(2,1)} %outer.1), calls=%async_computation.4 | async-start | bytes 2097152 | tf_op jit(solution)/shard_map/all_to_all | solution.py:297
  103.6 33.7 %collective-permute-start.6 = (bf16[128,1024]{1,0:T(8,128)(2,1)S(1)}, bf16[128,1024]{1,0:T(8,128)(2,1)S(1)}, u32[]{:S(2)}, u32[]{:S(2)}) collective-permute-start(bf16[128,1024]{1,0:T(8,128)(2,1)S(1)} %copy-done.11), channel_id=1, source_target_pairs={{0,504},{8,0},{16,8},{24,16},{32,24},{40,32},{48,40},{56,48},{64,5... | collective-permute-start | bytes 786440 | tf_op jit(solution)/shard_map/ppermute | solution.py:344
  135.4 13.8 %collective-permute-start.8 = (bf16[512,128]{1,0:T(8,128)(2,1)S(1)}, bf16[512,128]{1,0:T(8,128)(2,1)S(1)}, u32[]{:S(2)}, u32[]{:S(2)}) collective-permute-start(bf16[512,128]{1,0:T(8,128)(2,1)S(1)} %fusion.4), channel_id=1, source_target_pairs={{0,8},{8,0},{1,9},{9,1},{2,10},{10,2},{3,11},{11,3},{4,12},{12,4},... | collective-permute-start | bytes 393224 | tf_op jit(solution)/shard_map/ppermute | solution.py:302
Sparse Core Ops, SparseCore 0:
  16.8 40.2 all-gather.2
  71.4 52.6 reduce-scatter.1

commit v3 on v2

--- a/solution.py
+++ b/solution.py
@@ -46,14 +46,24 @@
     )
 
 
+def three_terms(value):
+    top = value.astype(jnp.bfloat16).astype(jnp.float32)
+    rest = value - top
+    mid = rest.astype(jnp.bfloat16).astype(jnp.float32)
+    return top, mid, rest - mid
+
+
 def prepare_kernel(x_ref, scale_ref, out_ref):
-    scale = scale_ref[...]
-    top = scale.astype(jnp.bfloat16).astype(jnp.float32)
-    rest = scale - top
-    mid = rest.astype(jnp.bfloat16).astype(jnp.float32)
-    low = rest - mid
-    row = lax.broadcasted_iota(jnp.int32, (16, scale.shape[1]), 0)
-    extra = jnp.where(row == 0, top, jnp.where(row == 1, mid, jnp.where(row == 2, low, 0.0)))
+    squares = jnp.zeros((128, 128), jnp.float32)
+    for lane in range(8):
+        x = x_ref[:, lane * 128 : (lane + 1) * 128].astype(jnp.float32)
+        squares += x * x
+    squares = jnp.sum(jnp.transpose(squares), axis=0, keepdims=True)
+    squares = jnp.concatenate([squares] + [jnp.zeros((1, 896), jnp.float32)], axis=1)
+    row = lax.broadcasted_iota(jnp.int32, (16, 1024), 0)
+    extra = jnp.zeros((16, 1024), jnp.float32)
+    for index, term in enumerate(three_terms(scale_ref[...]) + three_terms(squares)):
+        extra = jnp.where(row == index, term, extra)
     out_ref[0:128, :] = x_ref[...]
     out_ref[128:144, :] = extra.astype(jnp.bfloat16)
 
@@ -154,8 +164,12 @@
     )(rot, top, value_grad)
 
 
-def quant_kernel(core_ref, all_ref, mask_ref, inv_ref, quant_ref):
-    inverse = jnp.transpose(jnp.broadcast_to(inv_ref[...], (128, 128)))
+def quant_kernel(half_ref, all_ref, sum_ref, mask_ref, quant_ref, inv_ref):
+    squares = jnp.sum(sum_ref[...].astype(jnp.float32), axis=0)
+    squares = squares[3:4] + squares[4:5] + squares[5:6]
+    inverse = lax.rsqrt(squares / 8192.0 + NORM_EPS)
+    inv_ref[...] = inverse
+    inverse = jnp.transpose(jnp.broadcast_to(inverse, (128, 128)))
     mask = mask_ref[0]
     scale = all_ref[0, 128:144, :].astype(jnp.float32)
     scale = scale[0:1] + scale[1:2] + scale[2:3]
@@ -171,24 +185,30 @@
         quant_ref[zl, :, place * 128 : (place + 1) * 128] = quant
 
 
-def quantize(core, hidden_all, mask, inverse):
+def quantize(half, hidden_all, mask, name):
     return pl.pallas_call(
         quant_kernel,
         grid_spec=pltpu.PrefetchScalarGridSpec(
             num_scalar_prefetch=1,
             grid=(4,),
             in_specs=[
-                pl.BlockSpec((1, 144, 1024), lambda i, core: (i, 0, 0)),
-                pl.BlockSpec((1, 1, 1024), lambda i, core: (i * 2 + core[0], 0, 0)),
-                pl.BlockSpec((1, 128), lambda i, core: (0, 0)),
-            ],
-            out_specs=pl.BlockSpec((2, 128, 512), lambda i, core: (i, 0, 0)),
+                pl.BlockSpec((1, 144, 1024), lambda i, half: (i * 2 + half[0], 0, 0)),
+                pl.BlockSpec((8, 16, 128), lambda i, half: (0, 8, 0)),
+                pl.BlockSpec((1, 1, 1024), lambda i, half: (i * 2 + half[0], 0, 0)),
+            ],
+            out_specs=[
+                pl.BlockSpec((2, 128, 512), lambda i, half: (i, 0, 0)),
+                pl.BlockSpec((1, 128), lambda i, half: (0, 0)),
+            ],
         ),
-        out_shape=jax.ShapeDtypeStruct((8, 128, 512), jnp.bfloat16),
-        compiler_params=pltpu.CompilerParams(vmem_limit_bytes=BIG),
-        cost_estimate=pl.CostEstimate(flops=10_350_000_000, bytes_accessed=1, transcendentals=0),
-        name="quantize",
-    )(core, hidden_all, mask, inverse)
+        out_shape=[
+            jax.ShapeDtypeStruct((8, 128, 512), jnp.bfloat16),
+            jax.ShapeDtypeStruct((1, 128), jnp.float32),
+        ],
+        compiler_params=pltpu.CompilerParams(vmem_limit_bytes=BIG),
+        cost_estimate=CHEAP,
+        name=name,
+    )(half, hidden_all, hidden_all, mask)
 
 
 def rotor_grad_kernel(core_ref, mine_ref, other_ref, wm_ref, wo_ref, dv_ref, r2_ref, total_ref):
@@ -248,49 +268,38 @@
     )(core, mine, other, weight, weight, value_grad)
 
 
-def outer_kernel(place_ref, frame_ref, mine_ref, other_ref, out_ref):
-    yh = place_ref[1]
-
-    def product(quant_ref):
-        prod = lax.dot_general(
-            frame_ref[...],
-            quant_ref[...],
-            (((0,), (0,)), ((), ())),
-            preferred_element_type=jnp.float32,
-        ).astype(jnp.bfloat16)
-        for part in range(2):
-            out_ref[(part + yh) % 2] = prod[:, part * 128 : (part + 1) * 128]
-
-    @pl.when(pl.program_id(0) < 2)
-    def _():
-        product(mine_ref)
-
-    @pl.when(pl.program_id(0) >= 2)
-    def _():
-        product(other_ref)
-
-
-def outer(place, frames, mine, other):
+def outer_kernel(place_ref, frame_ref, quant_ref, *rest):
+    out_ref, yh = rest[-1], place_ref[1]
+    prod = lax.dot_general(
+        frame_ref[...],
+        quant_ref[...],
+        (((0,), (0,)), ((), ())),
+        preferred_element_type=jnp.float32,
+    ).astype(jnp.bfloat16)
+    for part in range(2):
+        out_ref[(part + yh) % 2] = prod[:, part * 128 : (part + 1) * 128]
+
+
+def outer(place, frames, quants, into, name):
+    more = [] if into is None else [into]
     return pl.pallas_call(
         outer_kernel,
         grid_spec=pltpu.PrefetchScalarGridSpec(
             num_scalar_prefetch=1,
-            grid=(4,),
+            grid=(2,),
             in_specs=[
                 pl.BlockSpec((1024, 512), lambda i, place: (0, 0)),
-                pl.BlockSpec((1024, 256), lambda i, place: (0, jnp.minimum(i, 1))),
-                pl.BlockSpec((1024, 256), lambda i, place: (0, jnp.maximum(i - 2, 0))),
-            ],
-            out_specs=pl.BlockSpec(
-                (2, 512, 128),
-                lambda i, place: (jnp.where(i < 2, place[0], 1 - place[0]) * 2 + i % 2, 0, 0),
-            ),
+                pl.BlockSpec((1024, 256), lambda i, place: (0, i)),
+            ]
+            + [pl.BlockSpec(memory_space=pl.ANY)] * len(more),
+            out_specs=pl.BlockSpec((2, 512, 128), lambda i, place: (place[0] * 2 + i, 0, 0)),
         ),
         out_shape=jax.ShapeDtypeStruct((8, 512, 128), jnp.bfloat16),
-        compiler_params=pltpu.CompilerParams(vmem_limit_bytes=BIG),
-        cost_estimate=CHEAP,
-        name="outer",
-    )(place, frames, mine, other)
+        input_output_aliases={3: 0} if more else {},
+        compiler_params=pltpu.CompilerParams(vmem_limit_bytes=BIG),
+        cost_estimate=CHEAP,
+        name=name,
+    )(place, frames, quants, *more)
 
 
 def exchange(value, axes):
@@ -309,24 +318,22 @@
 def local(hidden_in, grad_sent, value_grad, value_weight, rotation, act_scale, outliers):
     sections = 64
     pairs = [(source, (source - 1) % sections) for source in range(sections)]
-    place = jnp.stack([lax.axis_index("c"), lax.axis_index("yh")]).astype(jnp.int32)
+    core, yh = lax.axis_index("c"), lax.axis_index("yh")
+    place = jnp.stack([core, yh]).astype(jnp.int32)
+    other = jnp.stack([1 - core, yh]).astype(jnp.int32)
     wide = lambda value: value.astype(jnp.float32)
     tie = lax.optimization_barrier
 
-    hidden_all = lax.all_gather(prepare(hidden_in, act_scale), "yl", axis=0)
+    hidden_all = lax.all_gather(prepare(hidden_in, act_scale), TPA, axis=0)
 
     rot, peak, frame_keep, frame_send = rotate(place, value_weight, rotation, value_grad)
     frame_pair = (wide(frame_keep) + wide(swap_core(frame_send))).astype(jnp.bfloat16)
-    rot, frame_pair, hidden_two = tie((rot, frame_pair, hidden_in))
+    rot, frame_pair = tie((rot, frame_pair))
     frame_terms = exchange(frame_pair, "yl")
-    squares = jnp.sum(wide(hidden_two) * wide(hidden_two), axis=1).reshape(1, 128)
-    squares = squares + swap_core(squares)
-    moved = [shifted(squares, "yl", turn) for turn in (1, 2, 3)]
-    inverse = lax.rsqrt((squares + moved[0] + moved[1] + moved[2]) / 8192.0 + NORM_EPS)
-    frame_terms, inverse, rot = tie((frame_terms, inverse, rot))
+    grad_parts = weight_grad(rot, peak, value_grad)
+    frame_terms, grad_parts = tie((frame_terms, grad_parts))
     frame = jnp.sum(wide(frame_terms), axis=0).astype(jnp.bfloat16)
     frames = exchange(jnp.broadcast_to(frame[None], (8, 128, 512)), NEAR).reshape(1024, 512)
-    grad_parts = weight_grad(rot, peak, value_grad)
 
     ids = outliers[0]
     blocks = (ids[None, :] // 128 == jnp.arange(64)[:, None]).astype(jnp.bfloat16)
@@ -335,14 +342,16 @@
 
     hidden_all, mask, grad_parts = tie((hidden_all, mask, grad_parts))
     grad_sum = lax.psum_scatter(grad_parts, TPA, scatter_dimension=0, tiled=False)
-    quant = quantize(place, hidden_all, mask, inverse)
-    frames, quant = tie((frames, quant))
+    quant, inverse = quantize(place, hidden_all, mask, "quantize")
+    frames, quant, hidden_all = tie((frames, quant, hidden_all))
     quants = exchange(quant, NEAR)
-    r2_grad = rotor_grad(place, quant, swap_core(quant), value_weight, value_grad)
+    quant_other, _ = quantize(other, hidden_all, mask, "quantize_other")
+    r2_grad = rotor_grad(place, quant, quant_other, value_weight, value_grad)
     quants, r2_grad, grad_sent = tie((quants, r2_grad, grad_sent))
-    quants_other = swap_core(quants)
+    quants_other = swap_core(quants).reshape(1024, 512)
     incoming = lax.ppermute(grad_sent, SEC, pairs)
-    parts = outer(place, frames, quants.reshape(1024, 512), quants_other.reshape(1024, 512))
+    parts = outer(place, frames, quants.reshape(1024, 512), None, "outer")
+    parts = outer(other, frames, quants_other, parts, "outer_other")
     parts = exchange(parts, "zh").reshape(4, 2, 512, 128)
     sums = jnp.sum(wide(parts), axis=0)
     r1_grad = sums[0] + wide(shifted(sums[1].astype(jnp.bfloat16), "yh", 1))

time: 158 us -> 160 us (1.013)
  the two profiles are of different devices: /device:TPU:48 before, /device:TPU:40 now
where the time goes in v3:
time: 160 us; the launch traced here: 159 us
  waiting for transfers between devices  74.2 us (46%)
  starting transfers between devices  34.5 us (22%)
  Pallas kernels  22.3 us (14%)
  between operations  14.2 us (9%)
  local copies, waits for them, and re-layouts  9.87 us (6%)
  other arithmetic  3.96 us (2%)
    all_to_all x4, waiting for transfers between devices, exchange(): return lax.all_to_all(value, axes, split_axis=0, concat_axis=0, tiled=True)  53 us
    all_to_all x4, starting transfers between devices, exchange(): return lax.all_to_all(value, axes, split_axis=0, concat_axis=0, tiled=True)  24.2 us
    ppermute x3, waiting for transfers between devices, shifted(): lax.ppermute(value, axis, [(chip, (chip + turn) % count) for chip in rang...  11.7 us
    all_gather x1, waiting for transfers between devices, local(): hidden_all = lax.all_gather(prepare(hidden_in, act_scale), TPA, axis=0)  8.86 us
    unnamed x32, local copies, waits for them, and re-layouts  8.75 us
    ppermute x3, starting transfers between devices, shifted(): lax.ppermute(value, axis, [(chip, (chip + turn) % count) for chip in rang...  6.18 us
    pallas_call x2, Pallas kernels, outer(): pl.pallas_call(outer_kernel, grid_spec=pltpu.PrefetchScalarGridSpec(num_s...  5.62 us
    pallas_call x2, Pallas kernels, quantize(): pl.pallas_call(quant_kernel, grid_spec=pltpu.PrefetchScalarGridSpec(num_s...  5.22 us
  transfers between devices with their start and end apart: 10, of which 7 were waited for; matrix products, arithmetic and copies ran while one was open for 3% of the time, Pallas kernels for 13%

profile of v3, /device:TPU:40, one launch (start us, length us, event | category | flops | bytes accessed | tf_op | source)
XLA Modules:
  0.0 159.3 jit_solution(561427979406661192)
XLA Ops:
  7.2 0.0 all-gather.3.cloned.1.call-start
  7.2 0.0 copy-start.7
  7.2 0.9 copy-done.7
  8.2 0.0 copy-start.11
  8.2 0.7 copy-done.11
  8.8 0.9 prepare.1
  9.7 0.0 all-gather.3.cloned.1.call-update
  9.7 0.1 pad_add_fusion
  9.8 0.0 copy-start.2
  9.8 1.6 copy-done.2
  11.4 0.0 copy-start.9
  11.4 0.8 copy-done.9
  12.2 0.0 copy-start.13
  12.2 0.8 copy-done.13
  12.9 3.5 %rotate.1 = (bf16[8192,128]{1,0:T(8,128)(2,1)S(1)}, f32[1,128]{1,0:T(1,128)S(1)}, bf16[4,128,512]{2,1,0:T(8,128)(2,1)S(1)}, bf16[4,128,512]{2,1,0:T(8,128)(2,1)S(1)}) custom-call(s32[2]{0:T(128)S(1)} %get-tuple-element.43.core_ref.half_ref.place_ref, bf16[8192,128]{1,0:T(8,128)(2,1)S(1)} %copy-done.2, bf16[128,128]{1,0:T(8,128)(2,1)S(1)} %copy-done.13, ...), custom_call_target="tpu_custom_call" | custom-call | flops 23000000512 | bytes 1 | tf_op jit(solution)/shard_map/rotate/pallas_call | solution.py:115
  16.4 0.0 copy-start.10
  16.4 1.9 %collective-permute-start = (bf16[4,128,512]{2,1,0:T(8,128)(2,1)S(1)}, bf16[4,128,512]{2,1,0:T(8,128)(2,1)S(1)}, u32[]{:S(2)}, u32[]{:S(2)}) collective-permute-start(bf16[4,128,512]{2,1,0:T(8,128)(2,1)S(1)} %get-tuple-element.25), channel_id=1, source_target_pairs={{0,1},{1,0},{2,3},{3,2},{4,5},{5,4},{6,7},{7,6},{8,9},{9,8},{10,11... | collective-permute-start | bytes 1572872 | tf_op jit(solution)/shard_map/ppermute | solution.py:311
  18.4 1.9 %collective-permute-done = bf16[4,128,512]{2,1,0:T(8,128)(2,1)S(1)} collective-permute-done((bf16[4,128,512]{2,1,0:T(8,128)(2,1)S(1)}, bf16[4,128,512]{2,1,0:T(8,128)(2,1)S(1)}, u32[]{:S(2)}, u32[]{:S(2)}) %collective-permute-start) | collective-permute-done | bytes 524320 | tf_op jit(solution)/shard_map/ppermute | solution.py:311
  20.2 0.9 add_convert_fusion
  21.2 4.8 %all-to-all-start = ((bf16[4,128,512]{2,1,0:T(8,128)(2,1)}), bf16[4,128,512]{2,1,0:T(8,128)(2,1)S(1)}, u32[]{:S(2)}, u32[]{:S(2)}) async-start(bf16[4,128,512]{2,1,0:T(8,128)(2,1)} %add_convert_fusion), calls=%async_computation | async-start | bytes 1048576 | tf_op jit(solution)/shard_map/all_to_all | solution.py:306
  26.0 0.0 copy-done.10
  26.0 4.4 %weight_grad.1 = bf16[8,128,1024]{2,1,0:T(8,128)(2,1)S(1)} custom-call(bf16[8192,128]{1,0:T(8,128)(2,1)S(1)} %get-tuple-element.27.rot_ref, f32[1,128]{1,0:T(1,128)S(1)} %get-tuple-element.28.top_ref, bf16[128,128]{1,0:T(8,128)(2,1)S(1)} %copy-done.10), custom_call_target="tpu_custom_call" | custom-call | flops 1 | bytes 1 | tf_op jit(solution)/shard_map/weight_grad/pallas_call | solution.py:151
  30.3 0.0 copy-start.4
  30.3 1.3 copy-done.4
  31.7 14.1 %all-to-all-done = bf16[4,128,512]{2,1,0:T(8,128)(2,1)S(1)} async-done(((bf16[4,128,512]{2,1,0:T(8,128)(2,1)}), bf16[4,128,512]{2,1,0:T(8,128)(2,1)S(1)}, u32[]{:S(2)}, u32[]{:S(2)}) %all-to-all-start) | async-done | bytes 524320 | tf_op jit(solution)/shard_map/all_to_all | solution.py:306
  45.7 0.1 reduce_sum.21
  45.8 1.1 broadcast_in_dim.20
  46.9 6.1 %all-to-all-start.1 = ((bf16[8,128,512]{2,1,0:T(8,128)(2,1)}), bf16[8,128,512]{2,1,0:T(8,128)(2,1)S(1)}, u32[]{:S(2)}, u32[]{:S(2)}) async-start(bf16[8,128,512]{2,1,0:T(8,128)(2,1)} %broadcast_in_dim.20), calls=%async_computation.1 | async-start | bytes 2097152 | tf_op jit(solution)/shard_map/all_to_all | solution.py:306
  53.0 0.0 copy-done.15
  53.1 0.2 fusion.5
  53.3 8.9 %all-gather.3.cloned.1.call-done = bf16[1152,1024]{1,0:T(8,128)(2,1)} async-done(((bf16[144,1024]{1,0:T(8,128)(2,1)}), bf16[1152,1024]{1,0:T(8,128)(2,1)}) %all-gather.3.cloned.1.call-update) | async-done | bytes 2359312 | tf_op jit(solution)/shard_map/all_gather | solution.py:327
  62.1 1.7 %copy-done = bf16[1152,1024]{1,0:T(8,128)(2,1)S(1)} copy-done((bf16[1152,1024]{1,0:T(8,128)(2,1)S(1)}, bf16[1152,1024]{1,0:T(8,128)(2,1)}, u32[]{:S(2)}) %copy-start) | copy-done | bytes 2359320
  63.8 2.6 %quantize.1 = (bf16[8,128,512]{2,1,0:T(8,128)(2,1)S(1)}, f32[1,128]{1,0:T(1,128)S(1)}) custom-call(s32[2]{0:T(128)S(1)} %get-tuple-element.43.core_ref.half_ref.place_ref, bf16[8,144,1024]{2,1,0:T(8,128)(2,1)S(1)} %bitcast.26, bf16[8,144,1024]{2,1,0:T(8,128)(2,1)S(1)} %bitcast.27, f32[8,1,1024]{2,1,0:T(1,128)S(1)} %bitcast.35), custom_call_target="tpu_custom_call" | custom-call | flops 1 | bytes 1 | tf_op jit(solution)/shard_map/quantize/pallas_call | solution.py:189
  66.4 0.0 copy-start.5
  66.4 1.0 copy-done.5
  67.4 0.6 all-to-all-done.1
  68.0 6.1 %all-to-all-start.2 = ((bf16[8,128,512]{2,1,0:T(8,128)(2,1)}), bf16[8,128,512]{2,1,0:T(8,128)(2,1)}, u32[]{:S(2)}, u32[]{:S(2)}) async-start(bf16[8,128,512]{2,1,0:T(8,128)(2,1)} %copy-done.5), calls=%async_computation.2 | async-start | bytes 2097152 | tf_op jit(solution)/shard_map/all_to_all | solution.py:306
  74.1 0.0 reduce-scatter.2.cloned.1.call-start
  74.1 0.7 reduce-scatter.2.cloned.1.call-update
  74.8 0.0 copy-done.1
  74.8 0.0 copy-start.3
  74.8 0.0 copy-start.6
  74.9 2.6 %quantize_other.1 = (bf16[8,128,512]{2,1,0:T(8,128)(2,1)S(1)}, f32[1,128]{1,0:T(1,128)}) custom-call(s32[2]{0:T(128)S(1)} %get-tuple-element.44.half_ref.place_ref, bf16[8,144,1024]{2,1,0:T(8,128)(2,1)S(1)} %bitcast.28, bf16[8,144,1024]{2,1,0:T(8,128)(2,1)S(1)} %bitcast.29, f32[8,1,1024]{2,1,0:T(1,128)S(1)} %bitcast.36), custom_call_target="tpu_custom_call" | custom-call | flops 1 | bytes 1 | tf_op jit(solution)/shard_map/quantize_other/pallas_call | solution.py:189
  77.5 0.0 copy-done.3
  77.5 0.0 copy-done.6
  77.5 2.7 %rotor_grad.1 = f32[128,128]{1,0:T(8,128)} custom-call(s32[2]{0:T(128)S(1)} %get-tuple-element.43.core_ref.half_ref.place_ref, bf16[8,128,512]{2,1,0:T(8,128)(2,1)S(1)} %copy-done.6, bf16[8,128,512]{2,1,0:T(8,128)(2,1)S(1)} %get-tuple-element.36.other_ref, bf16[8,1024,128]{2,1,0:T(8,128)(2,1)S(1)} %bitcast.32, bf16[8,1024,128]{2,1,0:T(8,128)(2,1)S(1)} %bitcast.33, ...), custom_call_target="tpu_custom_call" | custom-call | flops 1 | bytes 1 | tf_op jit(solution)/shard_map/rotor_grad/pallas_call | solution.py:249
  80.2 10.5 %all-to-all-done.2 = bf16[8,128,512]{2,1,0:T(8,128)(2,1)} async-done(((bf16[8,128,512]{2,1,0:T(8,128)(2,1)}), bf16[8,128,512]{2,1,0:T(8,128)(2,1)}, u32[]{:S(2)}, u32[]{:S(2)}) %all-to-all-start.2) | async-done | bytes 1048608 | tf_op jit(solution)/shard_map/all_to_all | solution.py:306
  90.7 2.3 %collective-permute-start.2 = (bf16[8,128,512]{2,1,0:T(8,128)(2,1)}, bf16[8,128,512]{2,1,0:T(8,128)(2,1)S(1)}, u32[]{:S(2)}, u32[]{:S(2)}) collective-permute-start(bf16[8,128,512]{2,1,0:T(8,128)(2,1)} %all-to-all-done.2), channel_id=1, source_target_pairs={{0,1},{1,0},{2,3},{3,2},{4,5},{5,4},{6,7},{7,6},{8,9},{9,8},{10,11... | collective-permute-start | bytes 3145736 | tf_op jit(solution)/shard_map/ppermute | solution.py:311
  93.1 3.3 %outer.1.rest_0_ = bf16[8,512,128]{2,1,0:T(8,128)(2,1)} custom-call(s32[2]{0:T(128)S(1)} %get-tuple-element.43.core_ref.half_ref.place_ref, bf16[1024,512]{1,0:T(8,128)(2,1)S(1)} %bitcast.30, bf16[1024,512]{1,0:T(8,128)(2,1)} %bitcast.13.quant_ref), custom_call_target="tpu_custom_call" | custom-call | flops 1 | bytes 1 | tf_op jit(solution)/shard_map/outer/pallas_call | solution.py:285
  96.3 0.0 collective-permute-done.2
  96.3 2.3 %outer_other.1 = bf16[8,512,128]{2,1,0:T(8,128)(2,1)} custom-call(s32[2]{0:T(128)S(1)} %get-tuple-element.44.half_ref.place_ref, bf16[1024,512]{1,0:T(8,128)(2,1)S(1)} %bitcast.31, bf16[1024,512]{1,0:T(8,128)(2,1)S(1)} %bitcast.34, bf16[8,512,128]{2,1,0:T(8,128)(2,1)} %outer.1.rest_0_), custom_call_target="tpu_custom_call", output_to_operand_aliasing={{}: (3, {})} | custom-call | flops 1 | bytes 1 | tf_op jit(solution)/shard_map/outer_other/pallas_call | solution.py:285
  98.7 7.2 %all-to-all-start.3 = ((bf16[8,512,128]{2,1,0:T(8,128)(2,1)}), bf16[8,512,128]{2,1,0:T(8,128)(2,1)S(1)}, u32[]{:S(2)}, u32[]{:S(2)}) async-start(bf16[8,512,128]{2,1,0:T(8,128)(2,1)} %outer_other.1), calls=%async_computation.4 | async-start | bytes 2097152 | tf_op jit(solution)/shard_map/all_to_all | solution.py:306
  105.9 0.0 copy-done.12
  105.9 0.0 copy-done.14
  105.9 4.1 %collective-permute-start.1 = (bf16[128,1024]{1,0:T(8,128)(2,1)S(1)}, bf16[128,1024]{1,0:T(8,128)(2,1)S(1)}, u32[]{:S(2)}, u32[]{:S(2)}) collective-permute-start(bf16[128,1024]{1,0:T(8,128)(2,1)S(1)} %copy-done.14), channel_id=1, source_target_pairs={{0,504},{8,0},{16,8},{24,16},{32,24},{40,32},{48,40},{56,48},{64,5... | collective-permute-start | bytes 786440 | tf_op jit(solution)/shard_map/ppermute | solution.py:352
  110.0 27.8 %all-to-all-done.3 = bf16[8,512,128]{2,1,0:T(8,128)(2,1)S(1)} async-done(((bf16[8,512,128]{2,1,0:T(8,128)(2,1)}), bf16[8,512,128]{2,1,0:T(8,128)(2,1)S(1)}, u32[]{:S(2)}, u32[]{:S(2)}) %all-to-all-start.3) | async-done | bytes 1048608 | tf_op jit(solution)/shard_map/all_to_all | solution.py:306
  137.9 0.1 convert_reduce_fusion
  138.0 1.9 %collective-permute-start.3 = (bf16[512,128]{1,0:T(8,128)(2,1)S(1)}, bf16[512,128]{1,0:T(8,128)(2,1)S(1)}, u32[]{:S(2)}, u32[]{:S(2)}) collective-permute-start(bf16[512,128]{1,0:T(8,128)(2,1)S(1)} %fusion.4), channel_id=1, source_target_pairs={{0,8},{8,0},{1,9},{9,1},{2,10},{10,2},{3,11},{11,3},{4,12},{12,4},... | collective-permute-start | bytes 393224 | tf_op jit(solution)/shard_map/ppermute | solution.py:311
  140.0 0.0 collective-permute-done.1
  140.0 0.0 reduce-scatter.2.cloned.1.call-done
  140.0 0.0 copy-done.8
  140.0 1.9 %fusion.2 = bf16[128,1024]{1,0:T(8,128)(2,1)} fusion(bf16[128,1024]{1,0:T(8,128)(2,1)S(1)} %copy-done.8, bf16[128,1024]{1,0:T(8,128)(2,1)S(1)} %collective-permute-done.1, bf16[1,128,1024]{2,1,0:T(8,128)(2,1)} %reduce-scatter.2.cloned.1.call-done, f32[1024]{0:T(1024)S(1)} %bitcast.40, f32[128]{0:T(128)S(1)} %bitcast.38, pred[1024]{0:T(1024)(128)(4,1)S(1)} %compare_reduce_fusion), kind=kLoop, calls=%fused_computation.5 | loop fusion | flops 1572864 | bytes 1054208 | tf_op jit(solution)/shard_map/convert_element_type | solution.py:364
  141.9 9.8 %collective-permute-done.3 = bf16[512,128]{1,0:T(8,128)(2,1)S(1)} collective-permute-done((bf16[512,128]{1,0:T(8,128)(2,1)S(1)}, bf16[512,128]{1,0:T(8,128)(2,1)S(1)}, u32[]{:S(2)}, u32[]{:S(2)}) %collective-permute-start.3) | collective-permute-done | bytes 131104 | tf_op jit(solution)/shard_map/ppermute | solution.py:311
  151.8 0.7 fusion.3
  (11 shorter events, 0.1 us)
Async XLA Ops:
  7.2 55.0 %all-gather.3.cloned.1.call-start = ((), (), s32[]{:S(2)}) async-start(), calls=%async_computation.6 | async-start | bytes 2654208 | tf_op jit(solution)/shard_map/all_gather | solution.py:327
  7.2 1.0 copy-start.7
  8.2 0.7 copy-start.11
  9.8 1.6 copy-start.2
  11.4 0.8 copy-start.9
  12.2 0.8 copy-start.13
  16.4 9.5 %copy-start.10 = (bf16[128,128]{1,0:T(8,128)(2,1)S(1)}, bf16[128,128]{1,0:T(8,128)(2,1)}, u32[]{:S(2)}) copy-start(bf16[128,128]{1,0:T(8,128)(2,1)} %dv_ref.5) | copy-start | bytes 98308
  16.4 3.8 %collective-permute-start = (bf16[4,128,512]{2,1,0:T(8,128)(2,1)S(1)}, bf16[4,128,512]{2,1,0:T(8,128)(2,1)S(1)}, u32[]{:S(2)}, u32[]{:S(2)}) collective-permute-start(bf16[4,128,512]{2,1,0:T(8,128)(2,1)S(1)} %get-tuple-element.25), channel_id=1, source_target_pairs={{0,1},{1,0},{2,3},{3,2},{4,5},{5,4},{6,7},{7,6},{8,9},{9,8},{10,11... | collective-permute-start | bytes 1572872 | tf_op jit(solution)/shard_map/ppermute | solution.py:311
  21.2 24.6 %all-to-all-start = ((bf16[4,128,512]{2,1,0:T(8,128)(2,1)}), bf16[4,128,512]{2,1,0:T(8,128)(2,1)S(1)}, u32[]{:S(2)}, u32[]{:S(2)}) async-start(bf16[4,128,512]{2,1,0:T(8,128)(2,1)} %add_convert_fusion), calls=%async_computation | async-start | bytes 1048576 | tf_op jit(solution)/shard_map/all_to_all | solution.py:306
  30.3 1.3 copy-start.4
  31.7 21.4 %copy-start.15 = (s32[1,128]{1,0:T(1,128)S(1)}, s32[1,128]{1,0:T(1,128)}, u32[]{:S(2)}) copy-start(s32[1,128]{1,0:T(1,128)} %param.13) | copy-start | bytes 1540
  46.9 21.0 %all-to-all-start.1 = ((bf16[8,128,512]{2,1,0:T(8,128)(2,1)}), bf16[8,128,512]{2,1,0:T(8,128)(2,1)S(1)}, u32[]{:S(2)}, u32[]{:S(2)}) async-start(bf16[8,128,512]{2,1,0:T(8,128)(2,1)} %broadcast_in_dim.20), calls=%async_computation.1 | async-start | bytes 2097152 | tf_op jit(solution)/shard_map/all_to_all | solution.py:306
  62.1 1.7 %copy-start = (bf16[1152,1024]{1,0:T(8,128)(2,1)S(1)}, bf16[1152,1024]{1,0:T(8,128)(2,1)}, u32[]{:S(2)}) copy-start(bf16[1152,1024]{1,0:T(8,128)(2,1)} %all-gather.3.cloned.1.call-done) | copy-start | bytes 7077892
  66.4 1.0 copy-start.5
  68.0 6.9 %copy-start.1 = (bf16[1152,1024]{1,0:T(8,128)(2,1)S(1)}, bf16[1152,1024]{1,0:T(8,128)(2,1)}, u32[]{:S(2)}) copy-start(bf16[1152,1024]{1,0:T(8,128)(2,1)} %all-gather.3.cloned.1.call-done) | copy-start | bytes 7077892
  68.0 22.8 %all-to-all-start.2 = ((bf16[8,128,512]{2,1,0:T(8,128)(2,1)}), bf16[8,128,512]{2,1,0:T(8,128)(2,1)}, u32[]{:S(2)}, u32[]{:S(2)}) async-start(bf16[8,128,512]{2,1,0:T(8,128)(2,1)} %copy-done.5), calls=%async_computation.2 | async-start | bytes 2097152 | tf_op jit(solution)/shard_map/all_to_all | solution.py:306
  74.1 65.9 %reduce-scatter.2.cloned.1.call-start = ((), (), s32[]{:S(2)}) async-start(), calls=%async_computation.5 | async-start | bytes 2359296 | tf_op jit(solution)/shard_map/reduce_scatter | solution.py:344
  74.8 2.6 %copy-start.3 = (bf16[8192,128]{1,0:T(8,128)(2,1)S(1)}, bf16[8192,128]{1,0:T(8,128)(2,1)}, u32[]{:S(2)}) copy-start(bf16[8192,128]{1,0:T(8,128)(2,1)} %w_ref.1) | copy-start | bytes 6291460
  74.8 2.6 %copy-start.6 = (bf16[8,128,512]{2,1,0:T(8,128)(2,1)S(1)}, bf16[8,128,512]{2,1,0:T(8,128)(2,1)}, u32[]{:S(2)}) copy-start(bf16[8,128,512]{2,1,0:T(8,128)(2,1)} %copy-done.5) | copy-start | bytes 3145732
  90.7 5.6 %collective-permute-start.2 = (bf16[8,128,512]{2,1,0:T(8,128)(2,1)}, bf16[8,128,512]{2,1,0:T(8,128)(2,1)S(1)}, u32[]{:S(2)}, u32[]{:S(2)}) collective-permute-start(bf16[8,128,512]{2,1,0:T(8,128)(2,1)} %all-to-all-done.2), channel_id=1, source_target_pairs={{0,1},{1,0},{2,3},{3,2},{4,5},{5,4},{6,7},{7,6},{8,9},{9,8},{10,11... | collective-permute-start | bytes 3145736 | tf_op jit(solution)/shard_map/ppermute | solution.py:311
  98.7 7.2 %copy-start.12 = (f32[1,1024]{1,0:T(1,128)S(1)}, f32[1,1024]{1,0:T(1,128)}, u32[]{:S(2)}) copy-start(f32[1,1024]{1,0:T(1,128)} %scale_ref.1) | copy-start | bytes 12292
  98.7 7.2 %copy-start.14 = (bf16[128,1024]{1,0:T(8,128)(2,1)S(1)}, bf16[128,1024]{1,0:T(8,128)(2,1)}, u32[]{:S(2)}) copy-start(bf16[128,1024]{1,0:T(8,128)(2,1)} %param.8) | copy-start | bytes 786436
  98.7 41.3 %copy-start.8 = (bf16[128,1024]{1,0:T(8,128)(2,1)S(1)}, bf16[128,1024]{1,0:T(8,128)(2,1)}, u32[]{:S(2)}) copy-start(bf16[128,1024]{1,0:T(8,128)(2,1)} %x_ref.1) | copy-start | bytes 786436
  98.7 39.2 %all-to-all-start.3 = ((bf16[8,512,128]{2,1,0:T(8,128)(2,1)}), bf16[8,512,128]{2,1,0:T(8,128)(2,1)S(1)}, u32[]{:S(2)}, u32[]{:S(2)}) async-start(bf16[8,512,128]{2,1,0:T(8,128)(2,1)} %outer_other.1), calls=%async_computation.4 | async-start | bytes 2097152 | tf_op jit(solution)/shard_map/all_to_all | solution.py:306
  105.9 34.0 %collective-permute-start.1 = (bf16[128,1024]{1,0:T(8,128)(2,1)S(1)}, bf16[128,1024]{1,0:T(8,128)(2,1)S(1)}, u32[]{:S(2)}, u32[]{:S(2)}) collective-permute-start(bf16[128,1024]{1,0:T(8,128)(2,1)S(1)} %copy-done.14), channel_id=1, source_target_pairs={{0,504},{8,0},{16,8},{24,16},{32,24},{40,32},{48,40},{56,48},{64,5... | collective-permute-start | bytes 786440 | tf_op jit(solution)/shard_map/ppermute | solution.py:352
  138.0 13.7 %collective-permute-start.3 = (bf16[512,128]{1,0:T(8,128)(2,1)S(1)}, bf16[512,128]{1,0:T(8,128)(2,1)S(1)}, u32[]{:S(2)}, u32[]{:S(2)}) collective-permute-start(bf16[512,128]{1,0:T(8,128)(2,1)S(1)} %fusion.4), channel_id=1, source_target_pairs={{0,8},{8,0},{1,9},{9,1},{2,10},{10,2},{3,11},{11,3},{4,12},{12,4},... | collective-permute-start | bytes 393224 | tf_op jit(solution)/shard_map/ppermute | solution.py:311
Sparse Core Ops, SparseCore 0:
  10.1 52.0 all-gather.2
  77.8 52.7 reduce-scatter.1

commit v4 on v2

--- a/solution.py
+++ b/solution.py
@@ -68,90 +68,106 @@
     )(hidden, scale)
 
 
-def rotate_kernel(core_ref, w_ref, r2_ref, dv_ref, rot_ref, top_ref, keep_ref, send_ref):
+def rotated_rows(w_ref, r2_ref):
+    rot = jnp.dot(w_ref[...], r2_ref[...], preferred_element_type=jnp.float32)
+    return rot.astype(jnp.bfloat16)
+
+
+def keep_top(top_ref, rot):
     step = pl.program_id(0)
+    top = jnp.max(jnp.abs(rot.astype(jnp.float32)), axis=0, keepdims=True)
+
+    @pl.when(step == 0)
+    def _():
+        top_ref[...] = top
+
+    @pl.when(step > 0)
+    def _():
+        top_ref[...] = jnp.maximum(top_ref[...], top)
+
+
+def frame_kernel(core_ref, w_ref, r2_ref, dv_ref, top_ref, keep_ref, send_ref):
     core = core_ref[0]
-    rot = jnp.dot(w_ref[...], r2_ref[...], preferred_element_type=jnp.float32).astype(jnp.bfloat16)
-    rot_ref[...] = rot
-    top = jnp.max(jnp.abs(rot.astype(jnp.float32)), axis=0, keepdims=True)
-
-    @pl.when(step == 0)
-    def _():
-        top_ref[...] = top
-
-    @pl.when(step > 0)
-    def _():
-        top_ref[...] = jnp.maximum(top_ref[...], top)
-
-    @pl.when(step < 2)
-    def _():
-        for part in range(4):
-            prod = dot_nt(dv_ref[...], rot[part * 512 : (part + 1) * 512]).astype(jnp.bfloat16)
-            chip = step * 2 + part // 2
-
-            @pl.when(core == part % 2)
-            def _():
-                keep_ref[chip] = prod
-
-            @pl.when(core != part % 2)
-            def _():
-                send_ref[chip] = prod
-
-
-def rotate(core, weight, rotor, value_grad):
+    rot = rotated_rows(w_ref, r2_ref)
+    keep_top(top_ref, rot)
+    for part in range(4):
+        prod = dot_nt(dv_ref[...], rot[part * 512 : (part + 1) * 512]).astype(jnp.bfloat16)
+
+        @pl.when(core == part % 2)
+        def _():
+            keep_ref[part // 2] = prod
+
+        @pl.when(core != part % 2)
+        def _():
+            send_ref[part // 2] = prod
+
+
+def frame_parts(core, weight, rotor, value_grad):
     whole = lambda i, core: (0, 0)
-    block = lambda i, core: (i, 0)
     half = jax.ShapeDtypeStruct((4, 128, 512), jnp.bfloat16)
     return pl.pallas_call(
-        rotate_kernel,
+        frame_kernel,
         grid_spec=pltpu.PrefetchScalarGridSpec(
             num_scalar_prefetch=1,
-            grid=(4,),
+            grid=(2,),
             in_specs=[
-                pl.BlockSpec((2048, 128), block),
+                pl.BlockSpec((2048, 128), lambda i, core: (i, 0)),
                 pl.BlockSpec((128, 128), whole),
                 pl.BlockSpec((128, 128), whole),
             ],
             out_specs=[
-                pl.BlockSpec((2048, 128), block),
                 pl.BlockSpec((1, 128), whole),
-                pl.BlockSpec((4, 128, 512), lambda i, core: (0, 0, 0)),
-                pl.BlockSpec((4, 128, 512), lambda i, core: (0, 0, 0)),
+                pl.BlockSpec((2, 128, 512), lambda i, core: (i, 0, 0)),
+                pl.BlockSpec((2, 128, 512), lambda i, core: (i, 0, 0)),
             ],
         ),
-        out_shape=[
-            jax.ShapeDtypeStruct((8192, 128), jnp.bfloat16),
-            jax.ShapeDtypeStruct((1, 128), jnp.float32),
-            half,
-            half,
+        out_shape=[jax.ShapeDtypeStruct((1, 128), jnp.float32), half, half],
+        compiler_params=pltpu.CompilerParams(vmem_limit_bytes=BIG),
+        cost_estimate=LONG,
+        name="frame_parts",
+    )(core, weight, rotor, value_grad)
+
+
+def top_kernel(w_ref, r2_ref, top_ref):
+    keep_top(top_ref, rotated_rows(w_ref, r2_ref))
+
+
+def rest_top(weight, rotor):
+    return pl.pallas_call(
+        top_kernel,
+        grid=(2,),
+        in_specs=[
+            pl.BlockSpec((2048, 128), lambda i: (i + 2, 0)),
+            pl.BlockSpec((128, 128), lambda i: (0, 0)),
         ],
-        compiler_params=pltpu.CompilerParams(vmem_limit_bytes=BIG),
-        cost_estimate=LONG,
-        name="rotate",
-    )(core, weight, rotor, value_grad)
-
-
-def weight_grad_kernel(rot_ref, top_ref, dv_ref, out_ref):
-    step = top_ref[...] / 7.0 + SCALE_FLOOR
-    quant = soft_quant(rot_ref[...].astype(jnp.float32), 1.0 / step, step * 7.0)
+        out_specs=pl.BlockSpec((1, 128), lambda i: (0, 0)),
+        out_shape=jax.ShapeDtypeStruct((1, 128), jnp.float32),
+        compiler_params=pltpu.CompilerParams(vmem_limit_bytes=BIG),
+        cost_estimate=CHEAP,
+        name="rest_top",
+    )(weight, rotor)
+
+
+def weight_grad_kernel(w_ref, r2_ref, one_ref, two_ref, dv_ref, out_ref):
+    step = jnp.maximum(one_ref[...], two_ref[...]) / 7.0 + SCALE_FLOOR
+    rot = rotated_rows(w_ref, r2_ref).astype(jnp.float32)
+    quant = soft_quant(rot, 1.0 / step, step * 7.0)
     out_ref[0] = dot_nt(dv_ref[...], quant.astype(jnp.bfloat16)).astype(jnp.bfloat16)
 
 
-def weight_grad(rot, top, value_grad):
+def weight_grad(weight, rotor, top_one, top_two, value_grad):
+    small = pl.BlockSpec((128, 128), lambda i: (0, 0))
+    row = pl.BlockSpec((1, 128), lambda i: (0, 0))
     return pl.pallas_call(
         weight_grad_kernel,
         grid=(8,),
-        in_specs=[
-            pl.BlockSpec((1024, 128), lambda i: (i, 0)),
-            pl.BlockSpec((1, 128), lambda i: (0, 0)),
-            pl.BlockSpec((128, 128), lambda i: (0, 0)),
-        ],
+        in_specs=[pl.BlockSpec((1024, 128), lambda i: (i, 0)), small, row, row, small],
         out_specs=pl.BlockSpec((1, 128, 1024), lambda i: (i, 0, 0)),
         out_shape=jax.ShapeDtypeStruct((8, 128, 1024), jnp.bfloat16),
         compiler_params=pltpu.CompilerParams(vmem_limit_bytes=BIG),
         cost_estimate=CHEAP,
         name="weight_grad",
-    )(rot, top, value_grad)
+    )(weight, rotor, top_one, top_two, value_grad)
 
 
 def quant_kernel(core_ref, all_ref, mask_ref, inv_ref, quant_ref):
@@ -248,49 +264,38 @@
     )(core, mine, other, weight, weight, value_grad)
 
 
-def outer_kernel(place_ref, frame_ref, mine_ref, other_ref, out_ref):
-    yh = place_ref[1]
-
-    def product(quant_ref):
-        prod = lax.dot_general(
-            frame_ref[...],
-            quant_ref[...],
-            (((0,), (0,)), ((), ())),
-            preferred_element_type=jnp.float32,
-        ).astype(jnp.bfloat16)
-        for part in range(2):
-            out_ref[(part + yh) % 2] = prod[:, part * 128 : (part + 1) * 128]
-
-    @pl.when(pl.program_id(0) < 2)
-    def _():
-        product(mine_ref)
-
-    @pl.when(pl.program_id(0) >= 2)
-    def _():
-        product(other_ref)
-
-
-def outer(place, frames, mine, other):
+def outer_kernel(place_ref, frame_ref, quant_ref, *rest):
+    out_ref, yh = rest[-1], place_ref[1]
+    prod = lax.dot_general(
+        frame_ref[...],
+        quant_ref[...],
+        (((0,), (0,)), ((), ())),
+        preferred_element_type=jnp.float32,
+    ).astype(jnp.bfloat16)
+    for part in range(2):
+        out_ref[(part + yh) % 2] = prod[:, part * 128 : (part + 1) * 128]
+
+
+def outer(place, frames, quants, into, name):
+    more = [] if into is None else [into]
     return pl.pallas_call(
         outer_kernel,
         grid_spec=pltpu.PrefetchScalarGridSpec(
             num_scalar_prefetch=1,
-            grid=(4,),
+            grid=(2,),
             in_specs=[
                 pl.BlockSpec((1024, 512), lambda i, place: (0, 0)),
-                pl.BlockSpec((1024, 256), lambda i, place: (0, jnp.minimum(i, 1))),
-                pl.BlockSpec((1024, 256), lambda i, place: (0, jnp.maximum(i - 2, 0))),
-            ],
-            out_specs=pl.BlockSpec(
-                (2, 512, 128),
-                lambda i, place: (jnp.where(i < 2, place[0], 1 - place[0]) * 2 + i % 2, 0, 0),
-            ),
+                pl.BlockSpec((1024, 256), lambda i, place: (0, i)),
+            ]
+            + [pl.BlockSpec(memory_space=pl.ANY)] * len(more),
+            out_specs=pl.BlockSpec((2, 512, 128), lambda i, place: (place[0] * 2 + i, 0, 0)),
         ),
         out_shape=jax.ShapeDtypeStruct((8, 512, 128), jnp.bfloat16),
-        compiler_params=pltpu.CompilerParams(vmem_limit_bytes=BIG),
-        cost_estimate=CHEAP,
-        name="outer",
-    )(place, frames, mine, other)
+        input_output_aliases={3: 0} if more else {},
+        compiler_params=pltpu.CompilerParams(vmem_limit_bytes=BIG),
+        cost_estimate=CHEAP,
+        name=name,
+    )(place, frames, quants, *more)
 
 
 def exchange(value, axes):
@@ -306,27 +311,35 @@
     return shifted(value, "c", 1)
 
 
+def flipped(value, bit):
+    return lax.ppermute(value, "yl", [(chip, chip ^ bit) for chip in range(4)])
+
+
 def local(hidden_in, grad_sent, value_grad, value_weight, rotation, act_scale, outliers):
     sections = 64
     pairs = [(source, (source - 1) % sections) for source in range(sections)]
-    place = jnp.stack([lax.axis_index("c"), lax.axis_index("yh")]).astype(jnp.int32)
+    core, yh = lax.axis_index("c"), lax.axis_index("yh")
+    place = jnp.stack([core, yh]).astype(jnp.int32)
+    other = jnp.stack([1 - core, yh]).astype(jnp.int32)
     wide = lambda value: value.astype(jnp.float32)
     tie = lax.optimization_barrier
 
     hidden_all = lax.all_gather(prepare(hidden_in, act_scale), "yl", axis=0)
 
-    rot, peak, frame_keep, frame_send = rotate(place, value_weight, rotation, value_grad)
+    top_one, frame_keep, frame_send = frame_parts(place, value_weight, rotation, value_grad)
     frame_pair = (wide(frame_keep) + wide(swap_core(frame_send))).astype(jnp.bfloat16)
-    rot, frame_pair, hidden_two = tie((rot, frame_pair, hidden_in))
+    frame_pair, hidden_two = tie((frame_pair, hidden_in))
     frame_terms = exchange(frame_pair, "yl")
     squares = jnp.sum(wide(hidden_two) * wide(hidden_two), axis=1).reshape(1, 128)
     squares = squares + swap_core(squares)
-    moved = [shifted(squares, "yl", turn) for turn in (1, 2, 3)]
-    inverse = lax.rsqrt((squares + moved[0] + moved[1] + moved[2]) / 8192.0 + NORM_EPS)
-    frame_terms, inverse, rot = tie((frame_terms, inverse, rot))
+    squares = squares + flipped(squares, 1)
+    squares = squares + flipped(squares, 2)
+    inverse = lax.rsqrt(squares / 8192.0 + NORM_EPS)
+    frame_terms, inverse, rotor = tie((frame_terms, inverse, rotation))
     frame = jnp.sum(wide(frame_terms), axis=0).astype(jnp.bfloat16)
     frames = exchange(jnp.broadcast_to(frame[None], (8, 128, 512)), NEAR).reshape(1024, 512)
-    grad_parts = weight_grad(rot, peak, value_grad)
+    top_two = rest_top(value_weight, rotor)
+    grad_parts = weight_grad(value_weight, rotor, top_one, top_two, value_grad)
 
     ids = outliers[0]
     blocks = (ids[None, :] // 128 == jnp.arange(64)[:, None]).astype(jnp.bfloat16)
@@ -340,9 +353,10 @@
     quants = exchange(quant, NEAR)
     r2_grad = rotor_grad(place, quant, swap_core(quant), value_weight, value_grad)
     quants, r2_grad, grad_sent = tie((quants, r2_grad, grad_sent))
-    quants_other = swap_core(quants)
+    quants_other = swap_core(quants).reshape(1024, 512)
     incoming = lax.ppermute(grad_sent, SEC, pairs)
-    parts = outer(place, frames, quants.reshape(1024, 512), quants_other.reshape(1024, 512))
+    parts = outer(place, frames, quants.reshape(1024, 512), None, "outer")
+    parts = outer(other, frames, quants_other, parts, "outer_other")
     parts = exchange(parts, "zh").reshape(4, 2, 512, 128)
     sums = jnp.sum(wide(parts), axis=0)
     r1_grad = sums[0] + wide(shifted(sums[1].astype(jnp.bfloat16), "yh", 1))

time: 158 us -> 155 us (0.981)
  starting transfers between devices: 51.6 us -> 44.1 us
  waiting for transfers between devices: 58.1 us -> 61 us
  Pallas kernels: 18.4 us -> 20.9 us
    ppermute x0 -> x2, waiting for transfers between devices: none -> 8.64 us  [flipped(): return lax.ppermute(value, 'yl', [(chip, chip ^ bit) for chip in range(4)])]
    ppermute x8 -> x5, starting transfers between devices: 18.3 us -> 9.71 us  [shifted(): lax.ppermute(value, axis, [(chip, (chip + turn) % count) for chip in rang...]
    ppermute x8 -> x5, waiting for transfers between devices: 20.4 us -> 14.8 us  [shifted(): lax.ppermute(value, axis, [(chip, (chip + turn) % count) for chip in rang...]
    ppermute x0 -> x2, starting transfers between devices: none -> 5.27 us  [flipped(): return lax.ppermute(value, 'yl', [(chip, chip ^ bit) for chip in range(4)])]
    all_to_all x4, starting transfers between devices: 30 us -> 26 us  [exchange(): return lax.all_to_all(value, axes, split_axis=0, concat_axis=0, tiled=True)]
    pallas_call x1 -> x2, Pallas kernels: 4.58 us -> 5.63 us  [outer(): pl.pallas_call(outer_kernel, grid_spec=pltpu.PrefetchScalarGridSpec(num_s...]
    pallas_call x1 -> x2, Pallas kernels: 3.49 us -> 3.88 us  [the longest x1 3.21 us: frame_parts(): pl.pallas_call(frame_kernel, grid_spec=pltpu.PrefetchScalarGridSpec(num_s...]
    unnamed x26 -> x28, local copies, waits for them, and re-layouts: 7.94 us -> 7.94 us
  transfers between devices with their start and end apart: 15 -> 14, of which waited for: 12 -> 10; matrix products, arithmetic and copies ran while one was open for 4% -> 3% of each run, Pallas kernels for 10% -> 11%
where the time goes in v4:
time: 155 us; the launch traced here: 154 us
  waiting for transfers between devices  61 us (39%)
  starting transfers between devices  44.1 us (28%)
  Pallas kernels  20.9 us (13%)
  between operations  14.3 us (9%)
  local copies, waits for them, and re-layouts  9.02 us (6%)
  other arithmetic  4.19 us (3%)
    all_to_all x4, waiting for transfers between devices, exchange(): return lax.all_to_all(value, axes, split_axis=0, concat_axis=0, tiled=True)  36.3 us
    all_to_all x4, starting transfers between devices, exchange(): return lax.all_to_all(value, axes, split_axis=0, concat_axis=0, tiled=True)  26 us
    ppermute x5, waiting for transfers between devices, shifted(): lax.ppermute(value, axis, [(chip, (chip + turn) % count) for chip in rang...  14.8 us
    ppermute x5, starting transfers between devices, shifted(): lax.ppermute(value, axis, [(chip, (chip + turn) % count) for chip in rang...  9.71 us
    ppermute x2, waiting for transfers between devices, flipped(): return lax.ppermute(value, 'yl', [(chip, chip ^ bit) for chip in range(4)])  8.64 us
    unnamed x28, local copies, waits for them, and re-layouts  7.94 us
    pallas_call x2, Pallas kernels, outer(): pl.pallas_call(outer_kernel, grid_spec=pltpu.PrefetchScalarGridSpec(num_s...  5.63 us
    pallas_call x1, Pallas kernels, weight_grad(): pl.pallas_call(weight_grad_kernel, grid=(8,), in_specs=[pl.BlockSpec((102...  5.35 us
  transfers between devices with their start and end apart: 14, of which 10 were waited for; matrix products, arithmetic and copies ran while one was open for 3% of the time, Pallas kernels for 11%

profile of v4, /device:TPU:48, one launch (start us, length us, event | category | flops | bytes accessed | tf_op | source)
XLA Modules:
  0.0 153.7 jit_solution(1851555904706733622)
XLA Ops:
  7.2 0.0 all-gather.3.cloned.1.call-start
  7.2 0.1 pad_add_fusion.core_ref.place_ref
  7.3 1.6 %copy-done = bf16[8192,128]{1,0:T(8,128)(2,1)S(1)} copy-done((bf16[8192,128]{1,0:T(8,128)(2,1)S(1)}, bf16[8192,128]{1,0:T(8,128)(2,1)}, u32[]{:S(2)}) %copy-start) | copy-done | bytes 2097176
  8.9 0.8 copy-done.6
  9.6 0.8 copy-done.8
  10.4 3.2 %frame_parts.1 = (f32[1,128]{1,0:T(1,128)S(1)}, bf16[4,128,512]{2,1,0:T(8,128)(2,1)S(1)}, bf16[4,128,512]{2,1,0:T(8,128)(2,1)S(1)}) custom-call(s32[2]{0:T(128)S(1)} %pad_add_fusion.core_ref.place_ref, bf16[8192,128]{1,0:T(8,128)(2,1)S(1)} %copy-done, bf16[128,128]{1,0:T(8,128)(2,1)S(1)} %copy-done.6, bf16[128,128]{1,0:T(8,128)(2,1)S(1)} %copy-done.8), custom_call_target="tpu_custom_call" | custom-call | flops 23000000512 | bytes 1 | tf_op jit(solution)/shard_map/frame_parts/pallas_call | solution.py:108
  13.6 1.9 %collective-permute-start = (bf16[4,128,512]{2,1,0:T(8,128)(2,1)S(1)}, bf16[4,128,512]{2,1,0:T(8,128)(2,1)S(1)}, u32[]{:S(2)}, u32[]{:S(2)}) collective-permute-start(bf16[4,128,512]{2,1,0:T(8,128)(2,1)S(1)} %get-tuple-element.20), channel_id=1, source_target_pairs={{0,1},{1,0},{2,3},{3,2},{4,5},{5,4},{6,7},{7,6},{8,9},{9,8},{10,11... | collective-permute-start | bytes 1572872 | tf_op jit(solution)/shard_map/ppermute | solution.py:307
  15.5 0.0 copy-done.5
  15.6 0.0 copy-done.10
  15.6 0.8 prepare.1
  16.3 0.0 all-gather.3.cloned.1.call-update
  16.4 1.1 collective-permute-done
  17.4 1.0 add_convert_fusion
  18.4 5.6 %all-to-all-start = ((bf16[4,128,512]{2,1,0:T(8,128)(2,1)}), bf16[4,128,512]{2,1,0:T(8,128)(2,1)S(1)}, u32[]{:S(2)}, u32[]{:S(2)}) async-start(bf16[4,128,512]{2,1,0:T(8,128)(2,1)} %add_convert_fusion), calls=%async_computation | async-start | bytes 1048576 | tf_op jit(solution)/shard_map/all_to_all | solution.py:302
  24.0 0.1 multiply_reduce_fusion
  24.1 2.0 %collective-permute-start.1 = (f32[1,128]{1,0:T(1,128)S(1)}, f32[1,128]{1,0:T(1,128)S(1)}, u32[]{:S(2)}, u32[]{:S(2)}) collective-permute-start(f32[1,128]{1,0:T(1,128)S(1)} %bitcast.39), channel_id=1, source_target_pairs={{0,1},{1,0},{2,3},{3,2},{4,5},{5,4},{6,7},{7,6},{8,9},{9,8},{10,11... | collective-permute-start | bytes 1544 | tf_op jit(solution)/shard_map/ppermute | solution.py:307
  26.1 1.1 collective-permute-done.1
  27.2 3.4 %collective-permute-start.2 = (f32[1,128]{1,0:T(1,128)S(1)}, f32[1,128]{1,0:T(1,128)S(1)}, u32[]{:S(2)}, u32[]{:S(2)}) collective-permute-start(f32[1,128]{1,0:T(1,128)S(1)} %bitcast_add_fusion), channel_id=1, source_target_pairs={{0,2},{2,0},{4,6},{6,4},{1,3},{3,1},{5,7},{7,5},{8,10},{10,8},{12,... | collective-permute-start | bytes 1544 | tf_op jit(solution)/shard_map/ppermute | solution.py:315
  30.6 4.2 %collective-permute-done.2 = f32[1,128]{1,0:T(1,128)S(1)} collective-permute-done((f32[1,128]{1,0:T(1,128)S(1)}, f32[1,128]{1,0:T(1,128)S(1)}, u32[]{:S(2)}, u32[]{:S(2)}) %collective-permute-start.2) | collective-permute-done | bytes 544 | tf_op jit(solution)/shard_map/ppermute | solution.py:315
  34.8 1.9 %collective-permute-start.3 = (f32[1,128]{1,0:T(1,128)S(1)}, f32[1,128]{1,0:T(1,128)S(1)}, u32[]{:S(2)}, u32[]{:S(2)}) collective-permute-start(f32[1,128]{1,0:T(1,128)S(1)} %add.47), channel_id=1, source_target_pairs={{0,4},{2,6},{4,0},{6,2},{1,5},{3,7},{5,1},{7,3},{8,12},{10,14},{12... | collective-permute-start | bytes 1544 | tf_op jit(solution)/shard_map/ppermute | solution.py:315
  36.7 4.4 %collective-permute-done.3 = f32[1,128]{1,0:T(1,128)S(1)} collective-permute-done((f32[1,128]{1,0:T(1,128)S(1)}, f32[1,128]{1,0:T(1,128)S(1)}, u32[]{:S(2)}, u32[]{:S(2)}) %collective-permute-start.3) | collective-permute-done | bytes 544 | tf_op jit(solution)/shard_map/ppermute | solution.py:315
  41.2 0.0 all-to-all-done
  41.2 0.1 reduce_sum.31
  41.3 1.1 broadcast_in_dim.20
  42.3 6.3 %all-to-all-start.1 = ((bf16[8,128,512]{2,1,0:T(8,128)(2,1)}), bf16[8,128,512]{2,1,0:T(8,128)(2,1)S(1)}, u32[]{:S(2)}, u32[]{:S(2)}) async-start(bf16[8,128,512]{2,1,0:T(8,128)(2,1)} %broadcast_in_dim.20), calls=%async_computation.1 | async-start | bytes 2097152 | tf_op jit(solution)/shard_map/all_to_all | solution.py:302
  48.6 0.0 copy-done.13
  48.6 0.2 fusion.5
  48.8 0.0 copy-done.1
  48.8 0.0 copy-done.7
  48.8 0.7 rest_top.1.two_ref
  49.5 0.0 copy-done.9
  49.5 5.4 %weight_grad.1 = bf16[8,128,1024]{2,1,0:T(8,128)(2,1)S(1)} custom-call(bf16[8192,128]{1,0:T(8,128)(2,1)S(1)} %copy-done.1, bf16[128,128]{1,0:T(8,128)(2,1)S(1)} %copy-done.7, f32[1,128]{1,0:T(1,128)S(1)} %get-tuple-element.25.one_ref, f32[1,128]{1,0:T(1,128)S(1)} %rest_top.1.two_ref, bf16[128,128]{1,0:T(8,128)(2,1)S(1)} %copy-done.9), custom_call_target="tpu_custom_call" | custom-call | flops 1 | bytes 1 | tf_op jit(solution)/shard_map/weight_grad/pallas_call | solution.py:161
  54.9 0.0 copy-start.2
  54.9 1.3 copy-done.2
  56.2 0.5 all-gather.3.cloned.1.call-done
  56.7 1.3 copy-done.11
  58.0 2.5 %quantize.1.mine_ref = bf16[8,128,512]{2,1,0:T(8,128)(2,1)S(1)} custom-call(s32[2]{0:T(128)S(1)} %pad_add_fusion.core_ref.place_ref, bf16[4,144,1024]{2,1,0:T(8,128)(2,1)S(1)} %bitcast.36, f32[8,1,1024]{2,1,0:T(1,128)S(1)} %bitcast.34, f32[1,128]{1,0:T(1,128)S(1)} %add_rsqrt_fusion.inv_ref), custom_call_target="tpu_custom_call" | custom-call | flops 10350000128 | bytes 1 | tf_op jit(solution)/shard_map/quantize/pallas_call | solution.py:191
  60.6 0.0 copy-start.3
  60.6 1.0 copy-done.3
  61.6 1.2 all-to-all-done.1
  62.7 4.2 %all-to-all-start.2 = ((bf16[8,128,512]{2,1,0:T(8,128)(2,1)}), bf16[8,128,512]{2,1,0:T(8,128)(2,1)}, u32[]{:S(2)}, u32[]{:S(2)}) async-start(bf16[8,128,512]{2,1,0:T(8,128)(2,1)} %copy-done.3), calls=%async_computation.2 | async-start | bytes 2097152 | tf_op jit(solution)/shard_map/all_to_all | solution.py:302
  67.0 0.0 reduce-scatter.2.cloned.1.call-start
  67.0 0.7 reduce-scatter.2.cloned.1.call-update
  67.7 1.9 %collective-permute-start.4 = (bf16[8,128,512]{2,1,0:T(8,128)(2,1)}, bf16[8,128,512]{2,1,0:T(8,128)(2,1)S(1)}, u32[]{:S(2)}, u32[]{:S(2)}) collective-permute-start(bf16[8,128,512]{2,1,0:T(8,128)(2,1)} %copy-done.3), channel_id=1, source_target_pairs={{0,1},{1,0},{2,3},{3,2},{4,5},{5,4},{6,7},{7,6},{8,9},{9,8},{10,11... | collective-permute-start | bytes 3145736 | tf_op jit(solution)/shard_map/ppermute | solution.py:307
  69.7 2.8 %collective-permute-done.4.other_ref = bf16[8,128,512]{2,1,0:T(8,128)(2,1)S(1)} collective-permute-done((bf16[8,128,512]{2,1,0:T(8,128)(2,1)}, bf16[8,128,512]{2,1,0:T(8,128)(2,1)S(1)}, u32[]{:S(2)}, u32[]{:S(2)}) %collective-permute-start.4) | collective-permute-done | bytes 1048608 | tf_op jit(solution)/shard_map/ppermute | solution.py:307
  72.5 1.2 copy-done.4
  73.7 2.7 %rotor_grad.1 = f32[128,128]{1,0:T(8,128)} custom-call(s32[2]{0:T(128)S(1)} %pad_add_fusion.core_ref.place_ref, bf16[8,128,512]{2,1,0:T(8,128)(2,1)S(1)} %copy-done.4, bf16[8,128,512]{2,1,0:T(8,128)(2,1)S(1)} %collective-permute-done.4.other_ref, bf16[8,1024,128]{2,1,0:T(8,128)(2,1)S(1)} %bitcast.28, bf16[8,1024,128]{2,1,0:T(8,128)(2,1)S(1)} %bitcast.29, ...), custom_call_target="tpu_custom_call" | custom-call | flops 1 | bytes 1 | tf_op jit(solution)/shard_map/rotor_grad/pallas_call | solution.py:245
  76.4 6.3 %all-to-all-done.2 = bf16[8,128,512]{2,1,0:T(8,128)(2,1)} async-done(((bf16[8,128,512]{2,1,0:T(8,128)(2,1)}), bf16[8,128,512]{2,1,0:T(8,128)(2,1)}, u32[]{:S(2)}, u32[]{:S(2)}) %all-to-all-start.2) | async-done | bytes 1048608 | tf_op jit(solution)/shard_map/all_to_all | solution.py:302
  82.7 1.9 %collective-permute-start.6 = (bf16[8,128,512]{2,1,0:T(8,128)(2,1)}, bf16[8,128,512]{2,1,0:T(8,128)(2,1)S(1)}, u32[]{:S(2)}, u32[]{:S(2)}) collective-permute-start(bf16[8,128,512]{2,1,0:T(8,128)(2,1)} %all-to-all-done.2), channel_id=1, source_target_pairs={{0,1},{1,0},{2,3},{3,2},{4,5},{5,4},{6,7},{7,6},{8,9},{9,8},{10,11... | collective-permute-start | bytes 3145736 | tf_op jit(solution)/shard_map/ppermute | solution.py:307
  84.6 0.1 pad_add_fusion.1.place_ref
  84.7 3.3 %outer.1.rest_0_ = bf16[8,512,128]{2,1,0:T(8,128)(2,1)} custom-call(s32[2]{0:T(128)S(1)} %pad_add_fusion.core_ref.place_ref, bf16[1024,512]{1,0:T(8,128)(2,1)S(1)} %bitcast.30, bf16[1024,512]{1,0:T(8,128)(2,1)} %bitcast.14.quant_ref), custom_call_target="tpu_custom_call" | custom-call | flops 1 | bytes 1 | tf_op jit(solution)/shard_map/outer/pallas_call | solution.py:281
  88.0 0.0 collective-permute-done.6
  88.0 2.3 %outer_other.1 = bf16[8,512,128]{2,1,0:T(8,128)(2,1)} custom-call(s32[2]{0:T(128)S(1)} %pad_add_fusion.1.place_ref, bf16[1024,512]{1,0:T(8,128)(2,1)S(1)} %bitcast.31, bf16[1024,512]{1,0:T(8,128)(2,1)S(1)} %bitcast.32, bf16[8,512,128]{2,1,0:T(8,128)(2,1)} %outer.1.rest_0_), custom_call_target="tpu_custom_call", output_to_operand_aliasing={{}: (3, {})} | custom-call | flops 1 | bytes 1 | tf_op jit(solution)/shard_map/outer_other/pallas_call | solution.py:281
  90.3 9.9 %all-to-all-start.3 = ((bf16[8,512,128]{2,1,0:T(8,128)(2,1)}), bf16[8,512,128]{2,1,0:T(8,128)(2,1)S(1)}, u32[]{:S(2)}, u32[]{:S(2)}) async-start(bf16[8,512,128]{2,1,0:T(8,128)(2,1)} %outer_other.1), calls=%async_computation.4 | async-start | bytes 2097152 | tf_op jit(solution)/shard_map/all_to_all | solution.py:302
  100.3 0.0 copy-done.12
  100.3 3.1 %collective-permute-start.5 = (bf16[128,1024]{1,0:T(8,128)(2,1)S(1)}, bf16[128,1024]{1,0:T(8,128)(2,1)S(1)}, u32[]{:S(2)}, u32[]{:S(2)}) collective-permute-start(bf16[128,1024]{1,0:T(8,128)(2,1)S(1)} %copy-done.12), channel_id=1, source_target_pairs={{0,504},{8,0},{16,8},{24,16},{32,24},{40,32},{48,40},{56,48},{64,5... | collective-permute-start | bytes 786440 | tf_op jit(solution)/shard_map/ppermute | solution.py:357
  103.4 28.8 %all-to-all-done.3 = bf16[8,512,128]{2,1,0:T(8,128)(2,1)S(1)} async-done(((bf16[8,512,128]{2,1,0:T(8,128)(2,1)}), bf16[8,512,128]{2,1,0:T(8,128)(2,1)S(1)}, u32[]{:S(2)}, u32[]{:S(2)}) %all-to-all-start.3) | async-done | bytes 1048608 | tf_op jit(solution)/shard_map/all_to_all | solution.py:302
  132.2 0.1 convert_reduce_fusion
  132.4 1.9 %collective-permute-start.7 = (bf16[512,128]{1,0:T(8,128)(2,1)S(1)}, bf16[512,128]{1,0:T(8,128)(2,1)S(1)}, u32[]{:S(2)}, u32[]{:S(2)}) collective-permute-start(bf16[512,128]{1,0:T(8,128)(2,1)S(1)} %fusion.4), channel_id=1, source_target_pairs={{0,8},{8,0},{1,9},{9,1},{2,10},{10,2},{3,11},{11,3},{4,12},{12,4},... | collective-permute-start | bytes 393224 | tf_op jit(solution)/shard_map/ppermute | solution.py:307
  134.3 0.0 collective-permute-done.5
  134.3 0.0 reduce-scatter.2.cloned.1.call-done
  134.3 1.9 %fusion.2 = bf16[128,1024]{1,0:T(8,128)(2,1)} fusion(bf16[128,1024]{1,0:T(8,128)(2,1)S(1)} %copy-done.5, bf16[128,1024]{1,0:T(8,128)(2,1)S(1)} %collective-permute-done.5, bf16[1,128,1024]{2,1,0:T(8,128)(2,1)} %reduce-scatter.2.cloned.1.call-done, f32[1024]{0:T(1024)S(1)} %bitcast.38, f32[128]{0:T(128)S(1)} %bitcast.33, pred[1024]{0:T(1024)(128)(4,1)S(1)} %compare_reduce_fusion), kind=kLoop, calls=%fused_computation.5 | loop fusion | flops 1572864 | bytes 1054208 | tf_op jit(solution)/shard_map/convert_element_type | solution.py:369
  136.3 9.9 %collective-permute-done.7 = bf16[512,128]{1,0:T(8,128)(2,1)S(1)} collective-permute-done((bf16[512,128]{1,0:T(8,128)(2,1)S(1)}, bf16[512,128]{1,0:T(8,128)(2,1)S(1)}, u32[]{:S(2)}, u32[]{:S(2)}) %collective-permute-start.7) | collective-permute-done | bytes 131104 | tf_op jit(solution)/shard_map/ppermute | solution.py:307
  146.1 0.7 fusion.3
  (20 shorter events, 0.1 us)
Async XLA Ops:
  7.2 49.6 %all-gather.3.cloned.1.call-start = ((), (), s32[]{:S(2)}) async-start(), calls=%async_computation.6 | async-start | bytes 1474560 | tf_op jit(solution)/shard_map/all_gather | solution.py:327
  7.3 1.6 %copy-start = (bf16[8192,128]{1,0:T(8,128)(2,1)S(1)}, bf16[8192,128]{1,0:T(8,128)(2,1)}, u32[]{:S(2)}) copy-start(bf16[8192,128]{1,0:T(8,128)(2,1)} %w_ref.5) | copy-start | bytes 6291460
  8.9 0.8 copy-start.6
  9.6 0.8 copy-start.8
  10.4 5.2 %copy-start.5 = (bf16[128,1024]{1,0:T(8,128)(2,1)S(1)}, bf16[128,1024]{1,0:T(8,128)(2,1)}, u32[]{:S(2)}) copy-start(bf16[128,1024]{1,0:T(8,128)(2,1)} %x_ref.1) | copy-start | bytes 786436
  10.4 5.2 %copy-start.10 = (f32[1,1024]{1,0:T(1,128)S(1)}, f32[1,1024]{1,0:T(1,128)}, u32[]{:S(2)}) copy-start(f32[1,1024]{1,0:T(1,128)} %scale_ref.1) | copy-start | bytes 12292
  13.6 3.8 %collective-permute-start = (bf16[4,128,512]{2,1,0:T(8,128)(2,1)S(1)}, bf16[4,128,512]{2,1,0:T(8,128)(2,1)S(1)}, u32[]{:S(2)}, u32[]{:S(2)}) collective-permute-start(bf16[4,128,512]{2,1,0:T(8,128)(2,1)S(1)} %get-tuple-element.20), channel_id=1, source_target_pairs={{0,1},{1,0},{2,3},{3,2},{4,5},{5,4},{6,7},{7,6},{8,9},{9,8},{10,11... | collective-permute-start | bytes 1572872 | tf_op jit(solution)/shard_map/ppermute | solution.py:307
  18.4 22.8 %all-to-all-start = ((bf16[4,128,512]{2,1,0:T(8,128)(2,1)}), bf16[4,128,512]{2,1,0:T(8,128)(2,1)S(1)}, u32[]{:S(2)}, u32[]{:S(2)}) async-start(bf16[4,128,512]{2,1,0:T(8,128)(2,1)} %add_convert_fusion), calls=%async_computation | async-start | bytes 1048576 | tf_op jit(solution)/shard_map/all_to_all | solution.py:302
  23.9 24.6 %copy-start.13 = (s32[1,128]{1,0:T(1,128)S(1)}, s32[1,128]{1,0:T(1,128)}, u32[]{:S(2)}) copy-start(s32[1,128]{1,0:T(1,128)} %param.13) | copy-start | bytes 1540
  23.9 24.9 %copy-start.1 = (bf16[8192,128]{1,0:T(8,128)(2,1)S(1)}, bf16[8192,128]{1,0:T(8,128)(2,1)}, u32[]{:S(2)}) copy-start(bf16[8192,128]{1,0:T(8,128)(2,1)} %w_ref.5) | copy-start | bytes 6291460
  23.9 24.9 %copy-start.7 = (bf16[128,128]{1,0:T(8,128)(2,1)S(1)}, bf16[128,128]{1,0:T(8,128)(2,1)}, u32[]{:S(2)}) copy-start(bf16[128,128]{1,0:T(8,128)(2,1)} %r2_ref.3) | copy-start | bytes 98308
  24.1 3.1 %collective-permute-start.1 = (f32[1,128]{1,0:T(1,128)S(1)}, f32[1,128]{1,0:T(1,128)S(1)}, u32[]{:S(2)}, u32[]{:S(2)}) collective-permute-start(f32[1,128]{1,0:T(1,128)S(1)} %bitcast.39), channel_id=1, source_target_pairs={{0,1},{1,0},{2,3},{3,2},{4,5},{5,4},{6,7},{7,6},{8,9},{9,8},{10,11... | collective-permute-start | bytes 1544 | tf_op jit(solution)/shard_map/ppermute | solution.py:307
  27.2 7.6 %collective-permute-start.2 = (f32[1,128]{1,0:T(1,128)S(1)}, f32[1,128]{1,0:T(1,128)S(1)}, u32[]{:S(2)}, u32[]{:S(2)}) collective-permute-start(f32[1,128]{1,0:T(1,128)S(1)} %bitcast_add_fusion), channel_id=1, source_target_pairs={{0,2},{2,0},{4,6},{6,4},{1,3},{3,1},{5,7},{7,5},{8,10},{10,8},{12,... | collective-permute-start | bytes 1544 | tf_op jit(solution)/shard_map/ppermute | solution.py:315
  34.8 6.3 %collective-permute-start.3 = (f32[1,128]{1,0:T(1,128)S(1)}, f32[1,128]{1,0:T(1,128)S(1)}, u32[]{:S(2)}, u32[]{:S(2)}) collective-permute-start(f32[1,128]{1,0:T(1,128)S(1)} %add.47), channel_id=1, source_target_pairs={{0,4},{2,6},{4,0},{6,2},{1,5},{3,7},{5,1},{7,3},{8,12},{10,14},{12... | collective-permute-start | bytes 1544 | tf_op jit(solution)/shard_map/ppermute | solution.py:315
  42.3 7.2 %copy-start.9 = (bf16[128,128]{1,0:T(8,128)(2,1)S(1)}, bf16[128,128]{1,0:T(8,128)(2,1)}, u32[]{:S(2)}) copy-start(bf16[128,128]{1,0:T(8,128)(2,1)} %dv_ref.5) | copy-start | bytes 98308
  42.3 20.4 %all-to-all-start.1 = ((bf16[8,128,512]{2,1,0:T(8,128)(2,1)}), bf16[8,128,512]{2,1,0:T(8,128)(2,1)S(1)}, u32[]{:S(2)}, u32[]{:S(2)}) async-start(bf16[8,128,512]{2,1,0:T(8,128)(2,1)} %broadcast_in_dim.20), calls=%async_computation.1 | async-start | bytes 2097152 | tf_op jit(solution)/shard_map/all_to_all | solution.py:302
  54.9 1.3 copy-start.2
  56.7 1.3 copy-start.11
  60.6 1.0 copy-start.3
  62.7 20.0 %all-to-all-start.2 = ((bf16[8,128,512]{2,1,0:T(8,128)(2,1)}), bf16[8,128,512]{2,1,0:T(8,128)(2,1)}, u32[]{:S(2)}, u32[]{:S(2)}) async-start(bf16[8,128,512]{2,1,0:T(8,128)(2,1)} %copy-done.3), calls=%async_computation.2 | async-start | bytes 2097152 | tf_op jit(solution)/shard_map/all_to_all | solution.py:302
  67.0 67.3 %reduce-scatter.2.cloned.1.call-start = ((), (), s32[]{:S(2)}) async-start(), calls=%async_computation.5 | async-start | bytes 2359296 | tf_op jit(solution)/shard_map/reduce_scatter | solution.py:350
  67.7 4.8 %collective-permute-start.4 = (bf16[8,128,512]{2,1,0:T(8,128)(2,1)}, bf16[8,128,512]{2,1,0:T(8,128)(2,1)S(1)}, u32[]{:S(2)}, u32[]{:S(2)}) collective-permute-start(bf16[8,128,512]{2,1,0:T(8,128)(2,1)} %copy-done.3), channel_id=1, source_target_pairs={{0,1},{1,0},{2,3},{3,2},{4,5},{5,4},{6,7},{7,6},{8,9},{9,8},{10,11... | collective-permute-start | bytes 3145736 | tf_op jit(solution)/shard_map/ppermute | solution.py:307
  72.5 1.2 copy-start.4
  82.7 5.3 %collective-permute-start.6 = (bf16[8,128,512]{2,1,0:T(8,128)(2,1)}, bf16[8,128,512]{2,1,0:T(8,128)(2,1)S(1)}, u32[]{:S(2)}, u32[]{:S(2)}) collective-permute-start(bf16[8,128,512]{2,1,0:T(8,128)(2,1)} %all-to-all-done.2), channel_id=1, source_target_pairs={{0,1},{1,0},{2,3},{3,2},{4,5},{5,4},{6,7},{7,6},{8,9},{9,8},{10,11... | collective-permute-start | bytes 3145736 | tf_op jit(solution)/shard_map/ppermute | solution.py:307
  90.3 9.9 %copy-start.12 = (bf16[128,1024]{1,0:T(8,128)(2,1)S(1)}, bf16[128,1024]{1,0:T(8,128)(2,1)}, u32[]{:S(2)}) copy-start(bf16[128,1024]{1,0:T(8,128)(2,1)} %param.8) | copy-start | bytes 786436
  90.3 41.9 %all-to-all-start.3 = ((bf16[8,512,128]{2,1,0:T(8,128)(2,1)}), bf16[8,512,128]{2,1,0:T(8,128)(2,1)S(1)}, u32[]{:S(2)}, u32[]{:S(2)}) async-start(bf16[8,512,128]{2,1,0:T(8,128)(2,1)} %outer_other.1), calls=%async_computation.4 | async-start | bytes 2097152 | tf_op jit(solution)/shard_map/all_to_all | solution.py:302
  100.3 34.0 %collective-permute-start.5 = (bf16[128,1024]{1,0:T(8,128)(2,1)S(1)}, bf16[128,1024]{1,0:T(8,128)(2,1)S(1)}, u32[]{:S(2)}, u32[]{:S(2)}) collective-permute-start(bf16[128,1024]{1,0:T(8,128)(2,1)S(1)} %copy-done.12), channel_id=1, source_target_pairs={{0,504},{8,0},{16,8},{24,16},{32,24},{40,32},{48,40},{56,48},{64,5... | collective-permute-start | bytes 786440 | tf_op jit(solution)/shard_map/ppermute | solution.py:357
  132.4 13.8 %collective-permute-start.7 = (bf16[512,128]{1,0:T(8,128)(2,1)S(1)}, bf16[512,128]{1,0:T(8,128)(2,1)S(1)}, u32[]{:S(2)}, u32[]{:S(2)}) collective-permute-start(bf16[512,128]{1,0:T(8,128)(2,1)S(1)} %fusion.4), channel_id=1, source_target_pairs={{0,8},{8,0},{1,9},{9,1},{2,10},{10,2},{3,11},{11,3},{4,12},{12,4},... | collective-permute-start | bytes 393224 | tf_op jit(solution)/shard_map/ppermute | solution.py:307
Sparse Core Ops, SparseCore 0:
  16.5 40.2 all-gather.2
  70.7 53.8 reduce-scatter.1

commit v5 on v4

--- a/solution.py
+++ b/solution.py
@@ -91,7 +91,7 @@
     rot = rotated_rows(w_ref, r2_ref)
     keep_top(top_ref, rot)
     for part in range(4):
-        prod = dot_nt(dv_ref[...], rot[part * 512 : (part + 1) * 512]).astype(jnp.bfloat16)
+        prod = dot_nt(rot[part * 512 : (part + 1) * 512], dv_ref[...]).astype(jnp.bfloat16)
 
         @pl.when(core == part % 2)
         def _():
@@ -104,7 +104,7 @@
 
 def frame_parts(core, weight, rotor, value_grad):
     whole = lambda i, core: (0, 0)
-    half = jax.ShapeDtypeStruct((4, 128, 512), jnp.bfloat16)
+    half = jax.ShapeDtypeStruct((4, 512, 128), jnp.bfloat16)
     return pl.pallas_call(
         frame_kernel,
         grid_spec=pltpu.PrefetchScalarGridSpec(
@@ -117,8 +117,8 @@
             ],
             out_specs=[
                 pl.BlockSpec((1, 128), whole),
-                pl.BlockSpec((2, 128, 512), lambda i, core: (i, 0, 0)),
-                pl.BlockSpec((2, 128, 512), lambda i, core: (i, 0, 0)),
+                pl.BlockSpec((2, 512, 128), lambda i, core: (i, 0, 0)),
+                pl.BlockSpec((2, 512, 128), lambda i, core: (i, 0, 0)),
             ],
         ),
         out_shape=[jax.ShapeDtypeStruct((1, 128), jnp.float32), half, half],
@@ -165,7 +165,7 @@
         out_specs=pl.BlockSpec((1, 128, 1024), lambda i: (i, 0, 0)),
         out_shape=jax.ShapeDtypeStruct((8, 128, 1024), jnp.bfloat16),
         compiler_params=pltpu.CompilerParams(vmem_limit_bytes=BIG),
-        cost_estimate=CHEAP,
+        cost_estimate=pl.CostEstimate(flops=10_350_000_000, bytes_accessed=1, transcendentals=0),
         name="weight_grad",
     )(weight, rotor, top_one, top_two, value_grad)
 
@@ -202,7 +202,7 @@
         ),
         out_shape=jax.ShapeDtypeStruct((8, 128, 512), jnp.bfloat16),
         compiler_params=pltpu.CompilerParams(vmem_limit_bytes=BIG),
-        cost_estimate=pl.CostEstimate(flops=10_350_000_000, bytes_accessed=1, transcendentals=0),
+        cost_estimate=pl.CostEstimate(flops=6_900_000_000, bytes_accessed=1, transcendentals=0),
         name="quantize",
     )(core, hidden_all, mask, inverse)
 
@@ -265,13 +265,15 @@
 
 
 def outer_kernel(place_ref, frame_ref, quant_ref, *rest):
-    out_ref, yh = rest[-1], place_ref[1]
-    prod = lax.dot_general(
-        frame_ref[...],
-        quant_ref[...],
-        (((0,), (0,)), ((), ())),
-        preferred_element_type=jnp.float32,
-    ).astype(jnp.bfloat16)
+    out_ref, left_ref, yh = rest[-2], rest[-1], place_ref[1]
+
+    @pl.when(pl.program_id(0) == 0)
+    def _():
+        for near in range(8):
+            left_ref[:, near * 128 : (near + 1) * 128] = frame_ref[near]
+
+    prod = jnp.dot(left_ref[...], quant_ref[...], preferred_element_type=jnp.float32)
+    prod = prod.astype(jnp.bfloat16)
     for part in range(2):
         out_ref[(part + yh) % 2] = prod[:, part * 128 : (part + 1) * 128]
 
@@ -284,11 +286,12 @@
             num_scalar_prefetch=1,
             grid=(2,),
             in_specs=[
-                pl.BlockSpec((1024, 512), lambda i, place: (0, 0)),
+                pl.BlockSpec((8, 512, 128), lambda i, place: (0, 0, 0)),
                 pl.BlockSpec((1024, 256), lambda i, place: (0, i)),
             ]
             + [pl.BlockSpec(memory_space=pl.ANY)] * len(more),
             out_specs=pl.BlockSpec((2, 512, 128), lambda i, place: (place[0] * 2 + i, 0, 0)),
+            scratch_shapes=[pltpu.VMEM((512, 1024), jnp.bfloat16)],
         ),
         out_shape=jax.ShapeDtypeStruct((8, 512, 128), jnp.bfloat16),
         input_output_aliases={3: 0} if more else {},
@@ -328,36 +331,36 @@
 
     top_one, frame_keep, frame_send = frame_parts(place, value_weight, rotation, value_grad)
     frame_pair = (wide(frame_keep) + wide(swap_core(frame_send))).astype(jnp.bfloat16)
-    frame_pair, hidden_two = tie((frame_pair, hidden_in))
+    frame_pair, rotor = tie((frame_pair, rotation))
     frame_terms = exchange(frame_pair, "yl")
+    top_two = rest_top(value_weight, rotor)
+    grad_parts = weight_grad(value_weight, rotor, top_one, top_two, value_grad)
+    frame_terms, grad_parts, hidden_two = tie((frame_terms, grad_parts, hidden_in))
+    frame = jnp.sum(wide(frame_terms), axis=0).astype(jnp.bfloat16)
+    frames = exchange(jnp.broadcast_to(frame[None], (8, 512, 128)), NEAR)
     squares = jnp.sum(wide(hidden_two) * wide(hidden_two), axis=1).reshape(1, 128)
     squares = squares + swap_core(squares)
     squares = squares + flipped(squares, 1)
     squares = squares + flipped(squares, 2)
     inverse = lax.rsqrt(squares / 8192.0 + NORM_EPS)
-    frame_terms, inverse, rotor = tie((frame_terms, inverse, rotation))
-    frame = jnp.sum(wide(frame_terms), axis=0).astype(jnp.bfloat16)
-    frames = exchange(jnp.broadcast_to(frame[None], (8, 128, 512)), NEAR).reshape(1024, 512)
-    top_two = rest_top(value_weight, rotor)
-    grad_parts = weight_grad(value_weight, rotor, top_one, top_two, value_grad)
 
     ids = outliers[0]
     blocks = (ids[None, :] // 128 == jnp.arange(64)[:, None]).astype(jnp.bfloat16)
     lanes = (ids[:, None] % 128 == jnp.arange(128)[None, :]).astype(jnp.bfloat16)
     mask = jnp.dot(blocks, lanes, preferred_element_type=jnp.float32).reshape(TP, 1, 1024)
 
-    hidden_all, mask, grad_parts = tie((hidden_all, mask, grad_parts))
+    hidden_all, mask, grad_parts, inverse = tie((hidden_all, mask, grad_parts, inverse))
     grad_sum = lax.psum_scatter(grad_parts, TPA, scatter_dimension=0, tiled=False)
     quant = quantize(place, hidden_all, mask, inverse)
     frames, quant = tie((frames, quant))
     quants = exchange(quant, NEAR)
-    r2_grad = rotor_grad(place, quant, swap_core(quant), value_weight, value_grad)
-    quants, r2_grad, grad_sent = tie((quants, r2_grad, grad_sent))
+    quants, quant, grad_sent = tie((quants, quant, grad_sent))
     quants_other = swap_core(quants).reshape(1024, 512)
     incoming = lax.ppermute(grad_sent, SEC, pairs)
     parts = outer(place, frames, quants.reshape(1024, 512), None, "outer")
     parts = outer(other, frames, quants_other, parts, "outer_other")
-    parts = exchange(parts, "zh").reshape(4, 2, 512, 128)
+    r2_grad = rotor_grad(place, quant, swap_core(quant), value_weight, value_grad)
+    parts, r2_grad = tie((exchange(parts, "zh").reshape(4, 2, 512, 128), r2_grad))
     sums = jnp.sum(wide(parts), axis=0)
     r1_grad = sums[0] + wide(shifted(sums[1].astype(jnp.bfloat16), "yh", 1))
 

time: 155 us -> 170 us (1.097)
  the two profiles are of different devices: /device:TPU:48 before, /device:TPU:128 now
where the time goes in v5:
time: 170 us; the launch traced here: 169 us
  starting transfers between devices  62.1 us (37%)
  waiting for transfers between devices  54.5 us (32%)
  Pallas kernels  22.4 us (13%)
  between operations  14.3 us (8%)
  local copies, waits for them, and re-layouts  8.81 us (5%)
  other arithmetic  6.6 us (4%)
    all_to_all x4, waiting for transfers between devices, exchange(): return lax.all_to_all(value, axes, split_axis=0, concat_axis=0, tiled=True)  41.1 us
    all_to_all x4, starting transfers between devices, exchange(): return lax.all_to_all(value, axes, split_axis=0, concat_axis=0, tiled=True)  28.4 us
    ppermute x5, starting transfers between devices, shifted(): lax.ppermute(value, axis, [(chip, (chip + turn) % count) for chip in rang...  21.4 us
    unnamed x28, local copies, waits for them, and re-layouts  7.69 us
    ppermute x1, starting transfers between devices, local(): incoming = lax.ppermute(grad_sent, SEC, pairs)  6.79 us
    ppermute x5, waiting for transfers between devices, shifted(): lax.ppermute(value, axis, [(chip, (chip + turn) % count) for chip in rang...  6.52 us
    ppermute x2, waiting for transfers between devices, flipped(): return lax.ppermute(value, 'yl', [(chip, chip ^ bit) for chip in range(4)])  6.09 us
    pallas_call x2, Pallas kernels, outer(): pl.pallas_call(outer_kernel, grid_spec=pltpu.PrefetchScalarGridSpec(num_s...  5.63 us
  transfers between devices with their start and end apart: 14, of which 9 were waited for; matrix products, arithmetic and copies ran while one was open for 4% of the time, Pallas kernels for 11%

profile of v5, /device:TPU:128, one launch (start us, length us, event | category | flops | bytes accessed | tf_op | source)
XLA Modules:
  0.0 168.9 jit_solution(17570794993929182436)
XLA Ops:
  7.2 0.0 all-gather.3.cloned.1.call-start
  7.2 0.1 pad_add_fusion.core_ref.place_ref
  7.3 1.6 copy-done
  8.9 0.8 copy-done.7
  9.6 0.8 copy-done.9
  10.4 3.2 %frame_parts.1 = (f32[1,128]{1,0:T(1,128)S(1)}, bf16[4,512,128]{2,1,0:T(8,128)(2,1)S(1)}, bf16[4,512,128]{2,1,0:T(8,128)(2,1)S(1)}) custom-call(s32[2]{0:T(128)S(1)} %pad_add_fusion.core_ref.place_ref, bf16[8192,128]{1,0:T(8,128)(2,1)S(1)} %copy-done, bf16[128,128]{1,0:T(8,128)(2,1)S(1)} %copy-done.7, bf16[128,128]{1,0:T(8,128)(2,1)S(1)} %copy-done.9), custom_call_target="tpu_custom_call" | custom-call | flops 23000000512 | bytes 1 | tf_op jit(solution)/shard_map/frame_parts/pallas_call | solution.py:108
  13.6 0.0 copy-start.1
  13.6 0.0 copy-start.8
  13.6 2.1 %collective-permute-start = (bf16[4,512,128]{2,1,0:T(8,128)(2,1)S(1)}, bf16[4,512,128]{2,1,0:T(8,128)(2,1)}, u32[]{:S(2)}, u32[]{:S(2)}) collective-permute-start(bf16[4,512,128]{2,1,0:T(8,128)(2,1)S(1)} %get-tuple-element.23), channel_id=1, source_target_pairs={{0,1},{1,0},{2,3},{3,2},{4,5},{5,4},{6,7},{7,6},{8,9},{9,8},{10,11... | collective-permute-start | bytes 1572872 | tf_op jit(solution)/shard_map/ppermute | solution.py:310
  15.7 0.0 copy-done.5
  15.7 0.0 copy-done.11
  15.7 0.8 prepare.1
  16.5 0.0 all-gather.3.cloned.1.call-update
  16.5 1.2 collective-permute-done
  17.7 2.0 %add_convert_fusion = bf16[4,512,128]{2,1,0:T(8,128)(2,1)} fusion(bf16[4,512,128]{2,1,0:T(8,128)(2,1)} %collective-permute-done, bf16[4,512,128]{2,1,0:T(8,128)(2,1)S(1)} %get-tuple-element.22), kind=kLoop, calls=%fused_computation.1 | loop fusion | flops 1048576 | bytes 1572864 | tf_op jit(solution)/shard_map/convert_element_type | solution.py:333
  19.7 0.0 copy-done.1
  19.7 0.0 copy-done.8
  19.7 0.7 rest_top.1.two_ref
  20.4 4.9 %all-to-all-start = ((bf16[4,512,128]{2,1,0:T(8,128)(2,1)}), bf16[4,512,128]{2,1,0:T(8,128)(2,1)S(1)}, u32[]{:S(2)}, u32[]{:S(2)}) async-start(bf16[4,512,128]{2,1,0:T(8,128)(2,1)} %add_convert_fusion), calls=%async_computation | async-start | bytes 1048576 | tf_op jit(solution)/shard_map/all_to_all | solution.py:305
  25.3 0.0 copy-done.10
  25.3 5.3 %weight_grad.1 = bf16[8,128,1024]{2,1,0:T(8,128)(2,1)S(1)} custom-call(bf16[8192,128]{1,0:T(8,128)(2,1)S(1)} %copy-done.1, bf16[128,128]{1,0:T(8,128)(2,1)S(1)} %copy-done.8, f32[1,128]{1,0:T(1,128)S(1)} %get-tuple-element.26.one_ref, f32[1,128]{1,0:T(1,128)S(1)} %rest_top.1.two_ref, bf16[128,128]{1,0:T(8,128)(2,1)S(1)} %copy-done.10), custom_call_target="tpu_custom_call" | custom-call | flops 10350000128 | bytes 1 | tf_op jit(solution)/shard_map/weight_grad/pallas_call | solution.py:161
  30.6 0.0 copy-start.6
  30.6 1.3 copy-done.6
  31.9 13.7 %all-to-all-done = bf16[4,512,128]{2,1,0:T(8,128)(2,1)S(1)} async-done(((bf16[4,512,128]{2,1,0:T(8,128)(2,1)}), bf16[4,512,128]{2,1,0:T(8,128)(2,1)S(1)}, u32[]{:S(2)}, u32[]{:S(2)}) %all-to-all-start) | async-done | bytes 524320 | tf_op jit(solution)/shard_map/all_to_all | solution.py:305
  45.6 0.1 reduce_sum.30
  45.7 1.1 broadcast_in_dim.20
  46.8 7.9 %all-to-all-start.1 = ((bf16[8,512,128]{2,1,0:T(8,128)(2,1)}), bf16[8,512,128]{2,1,0:T(8,128)(2,1)S(1)}, u32[]{:S(2)}, u32[]{:S(2)}) async-start(bf16[8,512,128]{2,1,0:T(8,128)(2,1)} %broadcast_in_dim.20), calls=%async_computation.1 | async-start | bytes 2097152 | tf_op jit(solution)/shard_map/all_to_all | solution.py:305
  54.7 0.1 multiply_reduce_fusion
  54.8 1.9 %collective-permute-start.1 = (f32[1,128]{1,0:T(1,128)S(1)}, f32[1,128]{1,0:T(1,128)S(1)}, u32[]{:S(2)}, u32[]{:S(2)}) collective-permute-start(f32[1,128]{1,0:T(1,128)S(1)} %bitcast.33), channel_id=1, source_target_pairs={{0,1},{1,0},{2,3},{3,2},{4,5},{5,4},{6,7},{7,6},{8,9},{9,8},{10,11... | collective-permute-start | bytes 1544 | tf_op jit(solution)/shard_map/ppermute | solution.py:310
  56.7 0.0 copy-done.13
  56.7 1.1 collective-permute-done.1
  57.8 1.9 %collective-permute-start.2 = (f32[1,128]{1,0:T(1,128)S(1)}, f32[1,128]{1,0:T(1,128)S(1)}, u32[]{:S(2)}, u32[]{:S(2)}) collective-permute-start(f32[1,128]{1,0:T(1,128)S(1)} %bitcast_add_fusion), channel_id=1, source_target_pairs={{0,2},{2,0},{4,6},{6,4},{1,3},{3,1},{5,7},{7,5},{8,10},{10,8},{12,... | collective-permute-start | bytes 1544 | tf_op jit(solution)/shard_map/ppermute | solution.py:318
  59.7 3.5 %collective-permute-done.2 = f32[1,128]{1,0:T(1,128)S(1)} collective-permute-done((f32[1,128]{1,0:T(1,128)S(1)}, f32[1,128]{1,0:T(1,128)S(1)}, u32[]{:S(2)}, u32[]{:S(2)}) %collective-permute-start.2) | collective-permute-done | bytes 544 | tf_op jit(solution)/shard_map/ppermute | solution.py:318
  63.2 3.5 %collective-permute-start.3 = (f32[1,128]{1,0:T(1,128)S(1)}, f32[1,128]{1,0:T(1,128)S(1)}, u32[]{:S(2)}, u32[]{:S(2)}) collective-permute-start(f32[1,128]{1,0:T(1,128)S(1)} %add.48), channel_id=1, source_target_pairs={{0,4},{2,6},{4,0},{6,2},{1,5},{3,7},{5,1},{7,3},{8,12},{10,14},{12... | collective-permute-start | bytes 1544 | tf_op jit(solution)/shard_map/ppermute | solution.py:318
  66.8 0.2 fusion.5
  67.0 2.6 %collective-permute-done.3 = f32[1,128]{1,0:T(1,128)S(1)} collective-permute-done((f32[1,128]{1,0:T(1,128)S(1)}, f32[1,128]{1,0:T(1,128)S(1)}, u32[]{:S(2)}, u32[]{:S(2)}) %collective-permute-start.3) | collective-permute-done | bytes 544 | tf_op jit(solution)/shard_map/ppermute | solution.py:318
  69.6 1.3 copy-done.12
  70.8 2.5 %quantize.1.mine_ref = bf16[8,128,512]{2,1,0:T(8,128)(2,1)S(1)} custom-call(s32[2]{0:T(128)S(1)} %pad_add_fusion.core_ref.place_ref, bf16[4,144,1024]{2,1,0:T(8,128)(2,1)S(1)} %bitcast.31, f32[8,1,1024]{2,1,0:T(1,128)S(1)} %bitcast.29, f32[1,128]{1,0:T(1,128)S(1)} %add_rsqrt_fusion.inv_ref), custom_call_target="tpu_custom_call" | custom-call | flops 6899999744 | bytes 1 | tf_op jit(solution)/shard_map/quantize/pallas_call | solution.py:191
  73.4 0.0 copy-start.3
  73.4 1.0 copy-done.3
  74.4 0.0 all-to-all-done.1.frame_ref
  74.4 5.7 %all-to-all-start.2 = ((bf16[8,128,512]{2,1,0:T(8,128)(2,1)}), bf16[8,128,512]{2,1,0:T(8,128)(2,1)}, u32[]{:S(2)}, u32[]{:S(2)}) async-start(bf16[8,128,512]{2,1,0:T(8,128)(2,1)} %copy-done.3), calls=%async_computation.2 | async-start | bytes 2097152 | tf_op jit(solution)/shard_map/all_to_all | solution.py:305
  80.1 0.0 reduce-scatter.2.cloned.1.call-start
  80.1 0.7 reduce-scatter.2.cloned.1.call-update
  80.8 13.5 %all-to-all-done.2 = bf16[8,128,512]{2,1,0:T(8,128)(2,1)} async-done(((bf16[8,128,512]{2,1,0:T(8,128)(2,1)}), bf16[8,128,512]{2,1,0:T(8,128)(2,1)}, u32[]{:S(2)}, u32[]{:S(2)}) %all-to-all-start.2) | async-done | bytes 1048608 | tf_op jit(solution)/shard_map/all_to_all | solution.py:305
  94.3 1.9 %collective-permute-start.5 = (bf16[8,128,512]{2,1,0:T(8,128)(2,1)}, bf16[8,128,512]{2,1,0:T(8,128)(2,1)}, u32[]{:S(2)}, u32[]{:S(2)}) collective-permute-start(bf16[8,128,512]{2,1,0:T(8,128)(2,1)} %all-to-all-done.2), channel_id=1, source_target_pairs={{0,1},{1,0},{2,3},{3,2},{4,5},{5,4},{6,7},{7,6},{8,9},{9,8},{10,11... | collective-permute-start | bytes 3145736 | tf_op jit(solution)/shard_map/ppermute | solution.py:310
  96.3 0.1 pad_add_fusion.1.place_ref
  96.3 2.8 %outer.1.rest_0_ = bf16[8,512,128]{2,1,0:T(8,128)(2,1)S(1)} custom-call(s32[2]{0:T(128)S(1)} %pad_add_fusion.core_ref.place_ref, bf16[8,512,128]{2,1,0:T(8,128)(2,1)S(1)} %all-to-all-done.1.frame_ref, bf16[1024,512]{1,0:T(8,128)(2,1)} %bitcast.12.quant_ref), custom_call_target="tpu_custom_call" | custom-call | flops 1 | bytes 1 | tf_op jit(solution)/shard_map/outer/pallas_call | solution.py:283
  99.2 0.1 collective-permute-done.5
  99.2 2.8 %outer_other.1 = bf16[8,512,128]{2,1,0:T(8,128)(2,1)S(1)} custom-call(s32[2]{0:T(128)S(1)} %pad_add_fusion.1.place_ref, bf16[8,512,128]{2,1,0:T(8,128)(2,1)S(1)} %all-to-all-done.1.frame_ref, bf16[1024,512]{1,0:T(8,128)(2,1)} %bitcast.11.quant_ref, bf16[8,512,128]{2,1,0:T(8,128)(2,1)S(1)} %outer.1.rest_0_), custom_call_target="tpu_custom_call", output_to_operand_aliasing={{}: (3, {})} | custom-call | flops 1 | bytes 1 | tf_op jit(solution)/shard_map/outer_other/pallas_call | solution.py:283
  102.1 1.0 copy-done.2
  103.0 10.0 %all-to-all-start.3 = ((bf16[8,512,128]{2,1,0:T(8,128)(2,1)}), bf16[8,512,128]{2,1,0:T(8,128)(2,1)}, u32[]{:S(2)}, u32[]{:S(2)}) async-start(bf16[8,512,128]{2,1,0:T(8,128)(2,1)} %copy-done.2), calls=%async_computation.4 | async-start | bytes 2097152 | tf_op jit(solution)/shard_map/all_to_all | solution.py:305
  113.0 1.9 %collective-permute-start.6 = (bf16[8,128,512]{2,1,0:T(8,128)(2,1)S(1)}, bf16[8,128,512]{2,1,0:T(8,128)(2,1)}, u32[]{:S(2)}, u32[]{:S(2)}) collective-permute-start(bf16[8,128,512]{2,1,0:T(8,128)(2,1)S(1)} %copy-done.4), channel_id=1, source_target_pairs={{0,1},{1,0},{2,3},{3,2},{4,5},{5,4},{6,7},{7,6},{8,9},{9,8},{10,11... | collective-permute-start | bytes 3145736 | tf_op jit(solution)/shard_map/ppermute | solution.py:310
  115.0 6.8 %collective-permute-start.4 = (bf16[128,1024]{1,0:T(8,128)(2,1)}, bf16[128,1024]{1,0:T(8,128)(2,1)}, u32[]{:S(2)}, u32[]{:S(2)}) collective-permute-start(bf16[128,1024]{1,0:T(8,128)(2,1)} %param.8), channel_id=1, source_target_pairs={{0,504},{8,0},{16,8},{24,16},{32,24},{40,32},{48,40},{56,48},{64,5... | collective-permute-start | bytes 786440 | tf_op jit(solution)/shard_map/ppermute | solution.py:359
  121.8 0.0 collective-permute-done.6.other_ref
  121.8 4.3 %rotor_grad.1 = f32[128,128]{1,0:T(8,128)} custom-call(s32[2]{0:T(128)S(1)} %pad_add_fusion.core_ref.place_ref, bf16[8,128,512]{2,1,0:T(8,128)(2,1)S(1)} %copy-done.4, bf16[8,128,512]{2,1,0:T(8,128)(2,1)} %collective-permute-done.6.other_ref, bf16[8,1024,128]{2,1,0:T(8,128)(2,1)S(1)} %bitcast.26, bf16[8,1024,128]{2,1,0:T(8,128)(2,1)S(1)} %bitcast.27, ...), custom_call_target="tpu_custom_call" | custom-call | flops 1 | bytes 1 | tf_op jit(solution)/shard_map/rotor_grad/pallas_call | solution.py:245
  126.1 13.9 %all-to-all-done.3 = bf16[8,512,128]{2,1,0:T(8,128)(2,1)} async-done(((bf16[8,512,128]{2,1,0:T(8,128)(2,1)}), bf16[8,512,128]{2,1,0:T(8,128)(2,1)}, u32[]{:S(2)}, u32[]{:S(2)}) %all-to-all-start.3) | async-done | bytes 1048608 | tf_op jit(solution)/shard_map/all_to_all | solution.py:305
  140.1 1.4 convert_reduce_fusion
  141.5 13.6 %collective-permute-start.7 = (bf16[512,128]{1,0:T(8,128)(2,1)S(1)}, bf16[512,128]{1,0:T(8,128)(2,1)S(1)}, u32[]{:S(2)}, u32[]{:S(2)}) collective-permute-start(bf16[512,128]{1,0:T(8,128)(2,1)S(1)} %fusion.4), channel_id=1, source_target_pairs={{0,8},{8,0},{1,9},{9,1},{2,10},{10,2},{3,11},{11,3},{4,12},{12,4},... | collective-permute-start | bytes 393224 | tf_op jit(solution)/shard_map/ppermute | solution.py:310
  155.1 0.0 collective-permute-done.4
  155.1 0.0 reduce-scatter.2.cloned.1.call-done
  155.1 2.0 %fusion.2 = bf16[128,1024]{1,0:T(8,128)(2,1)} fusion(bf16[128,1024]{1,0:T(8,128)(2,1)S(1)} %copy-done.5, bf16[128,1024]{1,0:T(8,128)(2,1)} %collective-permute-done.4, bf16[1,128,1024]{2,1,0:T(8,128)(2,1)} %reduce-scatter.2.cloned.1.call-done, f32[1024]{0:T(1024)S(1)} %bitcast.32, f32[128]{0:T(128)S(1)} %bitcast.28, pred[1024]{0:T(1024)(128)(4,1)S(1)} %compare_reduce_fusion), kind=kLoop, calls=%fused_computation.5 | loop fusion | flops 1572864 | bytes 1054208 | tf_op jit(solution)/shard_map/convert_element_type | solution.py:372
  157.1 4.2 %collective-permute-done.7 = bf16[512,128]{1,0:T(8,128)(2,1)S(1)} collective-permute-done((bf16[512,128]{1,0:T(8,128)(2,1)S(1)}, bf16[512,128]{1,0:T(8,128)(2,1)S(1)}, u32[]{:S(2)}, u32[]{:S(2)}) %collective-permute-start.7) | collective-permute-done | bytes 131104 | tf_op jit(solution)/shard_map/ppermute | solution.py:310
  161.3 0.7 fusion.3
  (20 shorter events, 0.1 us)
Async XLA Ops:
  7.2 62.4 %all-gather.3.cloned.1.call-start = ((), (), s32[]{:S(2)}) async-start(), calls=%async_computation.6 | async-start | bytes 1474560 | tf_op jit(solution)/shard_map/all_gather | solution.py:330
  7.3 1.6 copy-start
  8.9 0.8 copy-start.7
  9.6 0.8 copy-start.9
  10.4 5.3 %copy-start.5 = (bf16[128,1024]{1,0:T(8,128)(2,1)S(1)}, bf16[128,1024]{1,0:T(8,128)(2,1)}, u32[]{:S(2)}) copy-start(bf16[128,1024]{1,0:T(8,128)(2,1)} %x_ref.1) | copy-start | bytes 786436
  10.4 5.3 %copy-start.11 = (f32[1,1024]{1,0:T(1,128)S(1)}, f32[1,1024]{1,0:T(1,128)}, u32[]{:S(2)}) copy-start(f32[1,1024]{1,0:T(1,128)} %scale_ref.1) | copy-start | bytes 12292
  13.6 6.1 %copy-start.1 = (bf16[8192,128]{1,0:T(8,128)(2,1)S(1)}, bf16[8192,128]{1,0:T(8,128)(2,1)}, u32[]{:S(2)}) copy-start(bf16[8192,128]{1,0:T(8,128)(2,1)} %w_ref.5) | copy-start | bytes 6291460
  13.6 6.1 %copy-start.8 = (bf16[128,128]{1,0:T(8,128)(2,1)S(1)}, bf16[128,128]{1,0:T(8,128)(2,1)}, u32[]{:S(2)}) copy-start(bf16[128,128]{1,0:T(8,128)(2,1)} %r2_ref.3) | copy-start | bytes 98308
  13.6 4.1 %collective-permute-start = (bf16[4,512,128]{2,1,0:T(8,128)(2,1)S(1)}, bf16[4,512,128]{2,1,0:T(8,128)(2,1)}, u32[]{:S(2)}, u32[]{:S(2)}) collective-permute-start(bf16[4,512,128]{2,1,0:T(8,128)(2,1)S(1)} %get-tuple-element.23), channel_id=1, source_target_pairs={{0,1},{1,0},{2,3},{3,2},{4,5},{5,4},{6,7},{7,6},{8,9},{9,8},{10,11... | collective-permute-start | bytes 1572872 | tf_op jit(solution)/shard_map/ppermute | solution.py:310
  17.7 7.6 %copy-start.10 = (bf16[128,128]{1,0:T(8,128)(2,1)S(1)}, bf16[128,128]{1,0:T(8,128)(2,1)}, u32[]{:S(2)}) copy-start(bf16[128,128]{1,0:T(8,128)(2,1)} %dv_ref.5) | copy-start | bytes 98308
  20.4 25.2 %all-to-all-start = ((bf16[4,512,128]{2,1,0:T(8,128)(2,1)}), bf16[4,512,128]{2,1,0:T(8,128)(2,1)S(1)}, u32[]{:S(2)}, u32[]{:S(2)}) async-start(bf16[4,512,128]{2,1,0:T(8,128)(2,1)} %add_convert_fusion), calls=%async_computation | async-start | bytes 1048576 | tf_op jit(solution)/shard_map/all_to_all | solution.py:305
  30.6 1.3 copy-start.6
  31.9 24.8 %copy-start.13 = (s32[1,128]{1,0:T(1,128)S(1)}, s32[1,128]{1,0:T(1,128)}, u32[]{:S(2)}) copy-start(s32[1,128]{1,0:T(1,128)} %param.13) | copy-start | bytes 1540
  46.8 27.6 %all-to-all-start.1 = ((bf16[8,512,128]{2,1,0:T(8,128)(2,1)}), bf16[8,512,128]{2,1,0:T(8,128)(2,1)S(1)}, u32[]{:S(2)}, u32[]{:S(2)}) async-start(bf16[8,512,128]{2,1,0:T(8,128)(2,1)} %broadcast_in_dim.20), calls=%async_computation.1 | async-start | bytes 2097152 | tf_op jit(solution)/shard_map/all_to_all | solution.py:305
  54.8 3.0 %collective-permute-start.1 = (f32[1,128]{1,0:T(1,128)S(1)}, f32[1,128]{1,0:T(1,128)S(1)}, u32[]{:S(2)}, u32[]{:S(2)}) collective-permute-start(f32[1,128]{1,0:T(1,128)S(1)} %bitcast.33), channel_id=1, source_target_pairs={{0,1},{1,0},{2,3},{3,2},{4,5},{5,4},{6,7},{7,6},{8,9},{9,8},{10,11... | collective-permute-start | bytes 1544 | tf_op jit(solution)/shard_map/ppermute | solution.py:310
  57.8 5.4 %collective-permute-start.2 = (f32[1,128]{1,0:T(1,128)S(1)}, f32[1,128]{1,0:T(1,128)S(1)}, u32[]{:S(2)}, u32[]{:S(2)}) collective-permute-start(f32[1,128]{1,0:T(1,128)S(1)} %bitcast_add_fusion), channel_id=1, source_target_pairs={{0,2},{2,0},{4,6},{6,4},{1,3},{3,1},{5,7},{7,5},{8,10},{10,8},{12,... | collective-permute-start | bytes 1544 | tf_op jit(solution)/shard_map/ppermute | solution.py:318
  63.2 6.3 %collective-permute-start.3 = (f32[1,128]{1,0:T(1,128)S(1)}, f32[1,128]{1,0:T(1,128)S(1)}, u32[]{:S(2)}, u32[]{:S(2)}) collective-permute-start(f32[1,128]{1,0:T(1,128)S(1)} %add.48), channel_id=1, source_target_pairs={{0,4},{2,6},{4,0},{6,2},{1,5},{3,7},{5,1},{7,3},{8,12},{10,14},{12... | collective-permute-start | bytes 1544 | tf_op jit(solution)/shard_map/ppermute | solution.py:318
  69.6 1.3 copy-start.12
  73.4 1.0 copy-start.3
  74.4 20.0 %all-to-all-start.2 = ((bf16[8,128,512]{2,1,0:T(8,128)(2,1)}), bf16[8,128,512]{2,1,0:T(8,128)(2,1)}, u32[]{:S(2)}, u32[]{:S(2)}) async-start(bf16[8,128,512]{2,1,0:T(8,128)(2,1)} %copy-done.3), calls=%async_computation.2 | async-start | bytes 2097152 | tf_op jit(solution)/shard_map/all_to_all | solution.py:305
  80.1 75.0 %reduce-scatter.2.cloned.1.call-start = ((), (), s32[]{:S(2)}) async-start(), calls=%async_computation.5 | async-start | bytes 2359296 | tf_op jit(solution)/shard_map/reduce_scatter | solution.py:353
  94.3 4.9 %collective-permute-start.5 = (bf16[8,128,512]{2,1,0:T(8,128)(2,1)}, bf16[8,128,512]{2,1,0:T(8,128)(2,1)}, u32[]{:S(2)}, u32[]{:S(2)}) collective-permute-start(bf16[8,128,512]{2,1,0:T(8,128)(2,1)} %all-to-all-done.2), channel_id=1, source_target_pairs={{0,1},{1,0},{2,3},{3,2},{4,5},{5,4},{6,7},{7,6},{8,9},{9,8},{10,11... | collective-permute-start | bytes 3145736 | tf_op jit(solution)/shard_map/ppermute | solution.py:310
  102.0 1.0 copy-start.2
  103.0 10.0 %copy-start.4 = (bf16[8,128,512]{2,1,0:T(8,128)(2,1)S(1)}, bf16[8,128,512]{2,1,0:T(8,128)(2,1)}, u32[]{:S(2)}) copy-start(bf16[8,128,512]{2,1,0:T(8,128)(2,1)} %copy-done.3) | copy-start | bytes 3145732
  103.0 37.0 %all-to-all-start.3 = ((bf16[8,512,128]{2,1,0:T(8,128)(2,1)}), bf16[8,512,128]{2,1,0:T(8,128)(2,1)}, u32[]{:S(2)}, u32[]{:S(2)}) async-start(bf16[8,512,128]{2,1,0:T(8,128)(2,1)} %copy-done.2), calls=%async_computation.4 | async-start | bytes 2097152 | tf_op jit(solution)/shard_map/all_to_all | solution.py:305
  113.0 8.8 %collective-permute-start.6 = (bf16[8,128,512]{2,1,0:T(8,128)(2,1)S(1)}, bf16[8,128,512]{2,1,0:T(8,128)(2,1)}, u32[]{:S(2)}, u32[]{:S(2)}) collective-permute-start(bf16[8,128,512]{2,1,0:T(8,128)(2,1)S(1)} %copy-done.4), channel_id=1, source_target_pairs={{0,1},{1,0},{2,3},{3,2},{4,5},{5,4},{6,7},{7,6},{8,9},{9,8},{10,11... | collective-permute-start | bytes 3145736 | tf_op jit(solution)/shard_map/ppermute | solution.py:310
  115.0 40.1 %collective-permute-start.4 = (bf16[128,1024]{1,0:T(8,128)(2,1)}, bf16[128,1024]{1,0:T(8,128)(2,1)}, u32[]{:S(2)}, u32[]{:S(2)}) collective-permute-start(bf16[128,1024]{1,0:T(8,128)(2,1)} %param.8), channel_id=1, source_target_pairs={{0,504},{8,0},{16,8},{24,16},{32,24},{40,32},{48,40},{56,48},{64,5... | collective-permute-start | bytes 786440 | tf_op jit(solution)/shard_map/ppermute | solution.py:359
  141.5 19.8 %collective-permute-start.7 = (bf16[512,128]{1,0:T(8,128)(2,1)S(1)}, bf16[512,128]{1,0:T(8,128)(2,1)S(1)}, u32[]{:S(2)}, u32[]{:S(2)}) collective-permute-start(bf16[512,128]{1,0:T(8,128)(2,1)S(1)} %fusion.4), channel_id=1, source_target_pairs={{0,8},{8,0},{1,9},{9,1},{2,10},{10,2},{3,11},{11,3},{4,12},{12,4},... | collective-permute-start | bytes 393224 | tf_op jit(solution)/shard_map/ppermute | solution.py:310
Sparse Core Ops, SparseCore 0:
  16.6 42.1 all-gather.2
  83.8 56.3 reduce-scatter.1

commit v6 on v4

--- a/solution.py
+++ b/solution.py
@@ -13,6 +13,7 @@
 SCALE_FLOOR = 1e-06
 TP = 8
 BIG = 32 << 20
+WHOLE = 60 << 20
 CHEAP = pl.CostEstimate(flops=1, bytes_accessed=1, transcendentals=0)
 LONG = pl.CostEstimate(flops=23_000_000_000, bytes_accessed=1, transcendentals=0)
 SEC = ("x", "zh", "zl", "yh")
@@ -46,26 +47,49 @@
     )
 
 
-def prepare_kernel(x_ref, scale_ref, out_ref):
-    scale = scale_ref[...]
-    top = scale.astype(jnp.bfloat16).astype(jnp.float32)
-    rest = scale - top
-    mid = rest.astype(jnp.bfloat16).astype(jnp.float32)
-    low = rest - mid
-    row = lax.broadcasted_iota(jnp.int32, (16, scale.shape[1]), 0)
-    extra = jnp.where(row == 0, top, jnp.where(row == 1, mid, jnp.where(row == 2, low, 0.0)))
-    out_ref[0:128, :] = x_ref[...]
-    out_ref[128:144, :] = extra.astype(jnp.bfloat16)
-
-
-def prepare(hidden, scale):
+def prepare_kernel(core_ref, x_ref, scale_ref, w_ref, r2_ref, dv_ref, out_ref, send_ref):
+    step = pl.program_id(0)
+    send_ref[pl.ds(pl.multiple_of(step * 512, 512), 512), :] = w_ref[...]
+
+    @pl.when(step == 0)
+    def _():
+        scale = scale_ref[...]
+        top = scale.astype(jnp.bfloat16).astype(jnp.float32)
+        rest = scale - top
+        mid = rest.astype(jnp.bfloat16).astype(jnp.float32)
+        low = rest - mid
+        row = lax.broadcasted_iota(jnp.int32, (16, scale.shape[1]), 0)
+        extra = jnp.where(row == 0, top, jnp.where(row == 1, mid, jnp.where(row == 2, low, 0.0)))
+        out_ref[0:128, :] = x_ref[...]
+        out_ref[128:144, :] = extra.astype(jnp.bfloat16)
+        send_ref[2048:2176, :] = r2_ref[...]
+        send_ref[2176:2304, :] = dv_ref[...]
+
+
+def prepare(core, hidden, scale, weight, rotor, value_grad):
+    whole = lambda i, core: (0, 0)
     return pl.pallas_call(
         prepare_kernel,
-        out_shape=jax.ShapeDtypeStruct((144, 1024), jnp.bfloat16),
-        compiler_params=pltpu.CompilerParams(vmem_limit_bytes=BIG),
+        grid_spec=pltpu.PrefetchScalarGridSpec(
+            num_scalar_prefetch=1,
+            grid=(4,),
+            in_specs=[
+                pl.BlockSpec((128, 1024), whole),
+                pl.BlockSpec((1, 1024), whole),
+                pl.BlockSpec((512, 128), lambda i, core: (i * 2 + 1 - core[0], 0)),
+                pl.BlockSpec((128, 128), whole),
+                pl.BlockSpec((128, 128), whole),
+            ],
+            out_specs=[pl.BlockSpec((144, 1024), whole), pl.BlockSpec((2304, 128), whole)],
+        ),
+        out_shape=[
+            jax.ShapeDtypeStruct((144, 1024), jnp.bfloat16),
+            jax.ShapeDtypeStruct((2304, 128), jnp.bfloat16),
+        ],
+        compiler_params=pltpu.CompilerParams(vmem_limit_bytes=WHOLE),
         cost_estimate=CHEAP,
         name="prepare",
-    )(hidden, scale)
+    )(core, hidden, scale, weight, rotor, value_grad)
 
 
 def rotated_rows(w_ref, r2_ref):
@@ -86,88 +110,76 @@
         top_ref[...] = jnp.maximum(top_ref[...], top)
 
 
-def frame_kernel(core_ref, w_ref, r2_ref, dv_ref, top_ref, keep_ref, send_ref):
-    core = core_ref[0]
-    rot = rotated_rows(w_ref, r2_ref)
-    keep_top(top_ref, rot)
-    for part in range(4):
-        prod = dot_nt(dv_ref[...], rot[part * 512 : (part + 1) * 512]).astype(jnp.bfloat16)
-
-        @pl.when(core == part % 2)
-        def _():
-            keep_ref[part // 2] = prod
-
-        @pl.when(core != part % 2)
-        def _():
-            send_ref[part // 2] = prod
-
-
-def frame_parts(core, weight, rotor, value_grad):
-    whole = lambda i, core: (0, 0)
-    half = jax.ShapeDtypeStruct((4, 128, 512), jnp.bfloat16)
+def frame_kernel(core_ref, w_ref, r2_ref, dv_ref, w2_ref, r22_ref, dv2_ref, out_ref):
+    mine = dot_nt(dv_ref[...], rotated_rows(w_ref, r2_ref))
+    other = dot_nt(dv2_ref[...], rotated_rows(w2_ref, r22_ref))
+    out_ref[0] = (mine + other).astype(jnp.bfloat16)
+
+
+def frame_pairs(core, weight, rotor, value_grad, received):
+    whole = pl.BlockSpec((128, 128), lambda i, core: (0, 0))
     return pl.pallas_call(
         frame_kernel,
         grid_spec=pltpu.PrefetchScalarGridSpec(
             num_scalar_prefetch=1,
-            grid=(2,),
-            in_specs=[
-                pl.BlockSpec((2048, 128), lambda i, core: (i, 0)),
-                pl.BlockSpec((128, 128), whole),
-                pl.BlockSpec((128, 128), whole),
+            grid=(4,),
+            in_specs=[
+                pl.BlockSpec((512, 128), lambda i, core: (i * 2 + core[0], 0)),
+                whole,
+                whole,
+                pl.BlockSpec((512, 128), lambda i, core: (i, 0)),
+                pl.BlockSpec((128, 128), lambda i, core: (16, 0)),
+                pl.BlockSpec((128, 128), lambda i, core: (17, 0)),
             ],
-            out_specs=[
-                pl.BlockSpec((1, 128), whole),
-                pl.BlockSpec((2, 128, 512), lambda i, core: (i, 0, 0)),
-                pl.BlockSpec((2, 128, 512), lambda i, core: (i, 0, 0)),
-            ],
-        ),
-        out_shape=[jax.ShapeDtypeStruct((1, 128), jnp.float32), half, half],
+            out_specs=pl.BlockSpec((1, 128, 512), lambda i, core: (i, 0, 0)),
+        ),
+        out_shape=jax.ShapeDtypeStruct((4, 128, 512), jnp.bfloat16),
         compiler_params=pltpu.CompilerParams(vmem_limit_bytes=BIG),
         cost_estimate=LONG,
-        name="frame_parts",
-    )(core, weight, rotor, value_grad)
+        name="frame_pairs",
+    )(core, weight, rotor, value_grad, received, received, received)
 
 
 def top_kernel(w_ref, r2_ref, top_ref):
     keep_top(top_ref, rotated_rows(w_ref, r2_ref))
 
 
-def rest_top(weight, rotor):
+def rotated_top(weight, rotor):
     return pl.pallas_call(
         top_kernel,
-        grid=(2,),
+        grid=(4,),
         in_specs=[
-            pl.BlockSpec((2048, 128), lambda i: (i + 2, 0)),
+            pl.BlockSpec((2048, 128), lambda i: (i, 0)),
             pl.BlockSpec((128, 128), lambda i: (0, 0)),
         ],
         out_specs=pl.BlockSpec((1, 128), lambda i: (0, 0)),
         out_shape=jax.ShapeDtypeStruct((1, 128), jnp.float32),
         compiler_params=pltpu.CompilerParams(vmem_limit_bytes=BIG),
         cost_estimate=CHEAP,
-        name="rest_top",
+        name="rotated_top",
     )(weight, rotor)
 
 
-def weight_grad_kernel(w_ref, r2_ref, one_ref, two_ref, dv_ref, out_ref):
-    step = jnp.maximum(one_ref[...], two_ref[...]) / 7.0 + SCALE_FLOOR
+def weight_grad_kernel(w_ref, r2_ref, top_ref, dv_ref, out_ref):
+    step = top_ref[...] / 7.0 + SCALE_FLOOR
     rot = rotated_rows(w_ref, r2_ref).astype(jnp.float32)
     quant = soft_quant(rot, 1.0 / step, step * 7.0)
     out_ref[0] = dot_nt(dv_ref[...], quant.astype(jnp.bfloat16)).astype(jnp.bfloat16)
 
 
-def weight_grad(weight, rotor, top_one, top_two, value_grad):
+def weight_grad(weight, rotor, top, value_grad):
     small = pl.BlockSpec((128, 128), lambda i: (0, 0))
     row = pl.BlockSpec((1, 128), lambda i: (0, 0))
     return pl.pallas_call(
         weight_grad_kernel,
         grid=(8,),
-        in_specs=[pl.BlockSpec((1024, 128), lambda i: (i, 0)), small, row, row, small],
+        in_specs=[pl.BlockSpec((1024, 128), lambda i: (i, 0)), small, row, small],
         out_specs=pl.BlockSpec((1, 128, 1024), lambda i: (i, 0, 0)),
         out_shape=jax.ShapeDtypeStruct((8, 128, 1024), jnp.bfloat16),
         compiler_params=pltpu.CompilerParams(vmem_limit_bytes=BIG),
         cost_estimate=CHEAP,
         name="weight_grad",
-    )(weight, rotor, top_one, top_two, value_grad)
+    )(weight, rotor, top, value_grad)
 
 
 def quant_kernel(core_ref, all_ref, mask_ref, inv_ref, quant_ref):
@@ -324,10 +336,10 @@
     wide = lambda value: value.astype(jnp.float32)
     tie = lax.optimization_barrier
 
-    hidden_all = lax.all_gather(prepare(hidden_in, act_scale), "yl", axis=0)
-
-    top_one, frame_keep, frame_send = frame_parts(place, value_weight, rotation, value_grad)
-    frame_pair = (wide(frame_keep) + wide(swap_core(frame_send))).astype(jnp.bfloat16)
+    packed, inputs = prepare(place, hidden_in, act_scale, value_weight, rotation, value_grad)
+    hidden_all = lax.all_gather(packed, "yl", axis=0)
+
+    frame_pair = frame_pairs(place, value_weight, rotation, value_grad, swap_core(inputs))
     frame_pair, hidden_two = tie((frame_pair, hidden_in))
     frame_terms = exchange(frame_pair, "yl")
     squares = jnp.sum(wide(hidden_two) * wide(hidden_two), axis=1).reshape(1, 128)
@@ -338,8 +350,8 @@
     frame_terms, inverse, rotor = tie((frame_terms, inverse, rotation))
     frame = jnp.sum(wide(frame_terms), axis=0).astype(jnp.bfloat16)
     frames = exchange(jnp.broadcast_to(frame[None], (8, 128, 512)), NEAR).reshape(1024, 512)
-    top_two = rest_top(value_weight, rotor)
-    grad_parts = weight_grad(value_weight, rotor, top_one, top_two, value_grad)
+    top = rotated_top(value_weight, rotor)
+    grad_parts = weight_grad(value_weight, rotor, top, value_grad)
 
     ids = outliers[0]
     blocks = (ids[None, :] // 128 == jnp.arange(64)[:, None]).astype(jnp.bfloat16)
@@ -351,13 +363,13 @@
     quant = quantize(place, hidden_all, mask, inverse)
     frames, quant = tie((frames, quant))
     quants = exchange(quant, NEAR)
-    r2_grad = rotor_grad(place, quant, swap_core(quant), value_weight, value_grad)
-    quants, r2_grad, grad_sent = tie((quants, r2_grad, grad_sent))
+    quants, quant, grad_sent = tie((quants, quant, grad_sent))
     quants_other = swap_core(quants).reshape(1024, 512)
     incoming = lax.ppermute(grad_sent, SEC, pairs)
     parts = outer(place, frames, quants.reshape(1024, 512), None, "outer")
     parts = outer(other, frames, quants_other, parts, "outer_other")
-    parts = exchange(parts, "zh").reshape(4, 2, 512, 128)
+    r2_grad = rotor_grad(place, quant, swap_core(quant), value_weight, value_grad)
+    parts, r2_grad = tie((exchange(parts, "zh").reshape(4, 2, 512, 128), r2_grad))
     sums = jnp.sum(wide(parts), axis=0)
     r1_grad = sums[0] + wide(shifted(sums[1].astype(jnp.bfloat16), "yh", 1))
 

time: 155 us -> 160 us (1.032)
  Pallas kernels: 20.9 us -> 25.7 us
  starting transfers between devices: 44.1 us -> 47.6 us
  local copies, waits for them, and re-layouts: 9.02 us -> 5.66 us
    all_to_all x4, starting transfers between devices: 26 us -> 30.8 us  [exchange(): return lax.all_to_all(value, axes, split_axis=0, concat_axis=0, tiled=True)]
    pallas_call x3, Pallas kernels: 4.65 us -> 8.35 us  [the longest x1 3.85 us: prepare(): pl.pallas_call(prepare_kernel, grid_spec=pltpu.PrefetchScalarGridSpec(num...]
    unnamed x28 -> x24, local copies, waits for them, and re-layouts: 7.94 us -> 4.59 us
    pallas_call x1, Pallas kernels: 2.7 us -> 4.31 us  [rotor_grad(): pl.pallas_call(rotor_grad_kernel, grid_spec=pltpu.PrefetchScalarGridSpec(...]
  transfers between devices with their start and end apart: 14 -> 14, of which waited for: 10 -> 9; matrix products, arithmetic and copies ran while one was open for 3% -> 3% of each run, Pallas kernels for 11% -> 14%
where the time goes in v6:
time: 160 us
  waiting for transfers between devices  60.8 us (38%)
  starting transfers between devices  47.6 us (30%)
  Pallas kernels  25.7 us (16%)
  between operations  14.3 us (9%)
  local copies, waits for them, and re-layouts  5.66 us (4%)
  other arithmetic  5.13 us (3%)
    all_to_all x4, waiting for transfers between devices, exchange(): return lax.all_to_all(value, axes, split_axis=0, concat_axis=0, tiled=True)  35.8 us
    all_to_all x4, starting transfers between devices, exchange(): return lax.all_to_all(value, axes, split_axis=0, concat_axis=0, tiled=True)  30.8 us
    ppermute x5, waiting for transfers between devices, shifted(): lax.ppermute(value, axis, [(chip, (chip + turn) % count) for chip in rang...  14.2 us
    ppermute x2, waiting for transfers between devices, flipped(): return lax.ppermute(value, 'yl', [(chip, chip ^ bit) for chip in range(4)])  10.1 us
    ppermute x5, starting transfers between devices, shifted(): lax.ppermute(value, axis, [(chip, (chip + turn) % count) for chip in rang...  9.56 us
    pallas_call x1, Pallas kernels, weight_grad(): pl.pallas_call(weight_grad_kernel, grid=(8,), in_specs=[pl.BlockSpec((102...  5.34 us
    ppermute x2, starting transfers between devices, flipped(): return lax.ppermute(value, 'yl', [(chip, chip ^ bit) for chip in range(4)])  5.27 us
    pallas_call x2, Pallas kernels, outer(): pl.pallas_call(outer_kernel, grid_spec=pltpu.PrefetchScalarGridSpec(num_s...  5.21 us
  transfers between devices with their start and end apart: 14, of which 9 were waited for; matrix products, arithmetic and copies ran while one was open for 3% of the time, Pallas kernels for 14%

profile of v6, /device:TPU:48, one launch (start us, length us, event | category | flops | bytes accessed | tf_op | source)
XLA Modules:
  0.0 159.5 jit_solution(18266964511299051792)
XLA Ops:
  7.2 0.0 copy-start
  7.2 0.0 copy-start.6
  7.2 0.0 copy-start.5
  7.2 0.0 all-gather.3.cloned.1.call-start
  7.3 0.6 pad_add_fusion.core_ref.place_ref
  7.8 3.9 %prepare.1 = (bf16[144,1024]{1,0:T(8,128)(2,1)}, bf16[2304,128]{1,0:T(8,128)(2,1)}) custom-call(s32[2]{0:T(128)} %pad_add_fusion.core_ref.place_ref, bf16[128,1024]{1,0:T(8,128)(2,1)} %x_ref.1, f32[1,1024]{1,0:T(1,128)} %scale_ref.1, bf16[8192,128]{1,0:T(8,128)(2,1)} %w_ref.7, bf16[128,128]{1,0:T(8,128)(2,1)} %r2_ref.5, bf16[128,128]{1,0:T(8,128)(2,1)} %dv_ref.7), custom_call_target="tpu_custom_call" | custom-call | flops 1 | bytes 1 | tf_op jit(solution)/shard_map/prepare/pallas_call | solution.py:71
  11.7 1.9 %collective-permute-start = (bf16[2304,128]{1,0:T(8,128)(2,1)}, bf16[2304,128]{1,0:T(8,128)(2,1)S(1)}, u32[]{:S(2)}, u32[]{:S(2)}) collective-permute-start(bf16[2304,128]{1,0:T(8,128)(2,1)} %get-tuple-element.20), channel_id=1, source_target_pairs={{0,1},{1,0},{2,3},{3,2},{4,5},{5,4},{6,7},{7,6},{8,9},{9,8},{10,11... | collective-permute-start | bytes 1769480 | tf_op jit(solution)/shard_map/ppermute | solution.py:319
  13.6 0.0 all-gather.3.cloned.1.call-update
  13.6 0.0 copy-start.9
  13.6 2.1 %collective-permute-done.w2_ref.r22_ref.dv2_ref = bf16[2304,128]{1,0:T(8,128)(2,1)S(1)} collective-permute-done((bf16[2304,128]{1,0:T(8,128)(2,1)}, bf16[2304,128]{1,0:T(8,128)(2,1)S(1)}, u32[]{:S(2)}, u32[]{:S(2)}) %collective-permute-start) | collective-permute-done | bytes 589856 | tf_op jit(solution)/shard_map/ppermute | solution.py:319
  15.8 0.0 copy-done
  15.8 0.0 copy-done.6
  15.8 0.0 copy-done.5
  15.8 0.0 copy-done.7
  15.8 3.2 %frame_pairs.1 = bf16[4,128,512]{2,1,0:T(8,128)(2,1)} custom-call(s32[2]{0:T(128)S(1)} %copy-done.7, bf16[8192,128]{1,0:T(8,128)(2,1)S(1)} %copy-done, bf16[128,128]{1,0:T(8,128)(2,1)S(1)} %copy-done.5, bf16[128,128]{1,0:T(8,128)(2,1)S(1)} %copy-done.6, bf16[2304,128]{1,0:T(8,128)(2,1)S(1)} %collective-permute-done.w2_ref.r22_ref.dv2_ref, ...), custom_call_target="tpu_custom_call" | custom-call | flops 23000000512 | bytes 1 | tf_op jit(solution)/shard_map/frame_pairs/pallas_call | solution.py:121
  19.0 5.6 %all-to-all-start = ((bf16[4,128,512]{2,1,0:T(8,128)(2,1)}), bf16[4,128,512]{2,1,0:T(8,128)(2,1)S(1)}, u32[]{:S(2)}, u32[]{:S(2)}) async-start(bf16[4,128,512]{2,1,0:T(8,128)(2,1)} %frame_pairs.1), calls=%async_computation | async-start | bytes 1048576 | tf_op jit(solution)/shard_map/all_to_all | solution.py:314
  24.5 0.0 copy-done.9
  24.5 0.1 multiply_reduce_fusion
  24.7 1.9 %collective-permute-start.1 = (f32[1,128]{1,0:T(1,128)S(1)}, f32[1,128]{1,0:T(1,128)S(1)}, u32[]{:S(2)}, u32[]{:S(2)}) collective-permute-start(f32[1,128]{1,0:T(1,128)S(1)} %bitcast.36), channel_id=1, source_target_pairs={{0,1},{1,0},{2,3},{3,2},{4,5},{5,4},{6,7},{7,6},{8,9},{9,8},{10,11... | collective-permute-start | bytes 1544 | tf_op jit(solution)/shard_map/ppermute | solution.py:319
  26.6 1.1 collective-permute-done.1
  27.7 3.4 %collective-permute-start.2 = (f32[1,128]{1,0:T(1,128)S(1)}, f32[1,128]{1,0:T(1,128)S(1)}, u32[]{:S(2)}, u32[]{:S(2)}) collective-permute-start(f32[1,128]{1,0:T(1,128)S(1)} %bitcast_add_fusion), channel_id=1, source_target_pairs={{0,2},{2,0},{4,6},{6,4},{1,3},{3,1},{5,7},{7,5},{8,10},{10,8},{12,... | collective-permute-start | bytes 1544 | tf_op jit(solution)/shard_map/ppermute | solution.py:327
  31.1 5.7 %collective-permute-done.2 = f32[1,128]{1,0:T(1,128)S(1)} collective-permute-done((f32[1,128]{1,0:T(1,128)S(1)}, f32[1,128]{1,0:T(1,128)S(1)}, u32[]{:S(2)}, u32[]{:S(2)}) %collective-permute-start.2) | collective-permute-done | bytes 544 | tf_op jit(solution)/shard_map/ppermute | solution.py:327
  36.8 1.9 %collective-permute-start.3 = (f32[1,128]{1,0:T(1,128)S(1)}, f32[1,128]{1,0:T(1,128)S(1)}, u32[]{:S(2)}, u32[]{:S(2)}) collective-permute-start(f32[1,128]{1,0:T(1,128)S(1)} %add.43), channel_id=1, source_target_pairs={{0,4},{2,6},{4,0},{6,2},{1,5},{3,7},{5,1},{7,3},{8,12},{10,14},{12... | collective-permute-start | bytes 1544 | tf_op jit(solution)/shard_map/ppermute | solution.py:327
  38.7 4.4 %collective-permute-done.3 = f32[1,128]{1,0:T(1,128)S(1)} collective-permute-done((f32[1,128]{1,0:T(1,128)S(1)}, f32[1,128]{1,0:T(1,128)S(1)}, u32[]{:S(2)}, u32[]{:S(2)}) %collective-permute-start.3) | collective-permute-done | bytes 544 | tf_op jit(solution)/shard_map/ppermute | solution.py:327
  43.1 0.0 all-to-all-done
  43.1 0.1 reduce_sum.31
  43.2 1.1 broadcast_in_dim.20
  44.3 6.9 %all-to-all-start.1 = ((bf16[8,128,512]{2,1,0:T(8,128)(2,1)}), bf16[8,128,512]{2,1,0:T(8,128)(2,1)S(1)}, u32[]{:S(2)}, u32[]{:S(2)}) async-start(bf16[8,128,512]{2,1,0:T(8,128)(2,1)} %broadcast_in_dim.20), calls=%async_computation.1 | async-start | bytes 2097152 | tf_op jit(solution)/shard_map/all_to_all | solution.py:314
  51.2 0.0 copy-done.11
  51.2 1.3 rotated_top.1.top_ref
  52.6 0.2 fusion.5
  52.8 5.3 %weight_grad.1 = bf16[8,128,1024]{2,1,0:T(8,128)(2,1)S(1)} custom-call(bf16[8192,128]{1,0:T(8,128)(2,1)S(1)} %copy-done, bf16[128,128]{1,0:T(8,128)(2,1)S(1)} %copy-done.5, f32[1,128]{1,0:T(1,128)S(1)} %rotated_top.1.top_ref, bf16[128,128]{1,0:T(8,128)(2,1)S(1)} %copy-done.6), custom_call_target="tpu_custom_call" | custom-call | flops 1 | bytes 1 | tf_op jit(solution)/shard_map/weight_grad/pallas_call | solution.py:173
  58.1 0.0 copy-start.2
  58.1 1.3 copy-done.2
  59.5 1.3 copy-done.8
  60.7 2.5 %quantize.1.mine_ref = bf16[8,128,512]{2,1,0:T(8,128)(2,1)S(1)} custom-call(s32[2]{0:T(128)S(1)} %copy-done.7, bf16[4,144,1024]{2,1,0:T(8,128)(2,1)S(1)} %bitcast.34, f32[8,1,1024]{2,1,0:T(1,128)S(1)} %bitcast.32, f32[1,128]{1,0:T(1,128)S(1)} %add_rsqrt_fusion.inv_ref), custom_call_target="tpu_custom_call" | custom-call | flops 10350000128 | bytes 1 | tf_op jit(solution)/shard_map/quantize/pallas_call | solution.py:203
  63.3 0.0 copy-start.3
  63.3 1.0 copy-done.3
  64.2 0.0 all-to-all-done.1
  64.2 5.7 %all-to-all-start.2 = ((bf16[8,128,512]{2,1,0:T(8,128)(2,1)}), bf16[8,128,512]{2,1,0:T(8,128)(2,1)}, u32[]{:S(2)}, u32[]{:S(2)}) async-start(bf16[8,128,512]{2,1,0:T(8,128)(2,1)} %copy-done.3), calls=%async_computation.2 | async-start | bytes 2097152 | tf_op jit(solution)/shard_map/all_to_all | solution.py:314
  69.9 0.0 reduce-scatter.2.cloned.1.call-start
  70.0 0.7 reduce-scatter.2.cloned.1.call-update
  70.7 12.9 %all-to-all-done.2 = bf16[8,128,512]{2,1,0:T(8,128)(2,1)} async-done(((bf16[8,128,512]{2,1,0:T(8,128)(2,1)}), bf16[8,128,512]{2,1,0:T(8,128)(2,1)}, u32[]{:S(2)}, u32[]{:S(2)}) %all-to-all-start.2) | async-done | bytes 1048608 | tf_op jit(solution)/shard_map/all_to_all | solution.py:314
  83.6 1.9 %collective-permute-start.5 = (bf16[8,128,512]{2,1,0:T(8,128)(2,1)}, bf16[8,128,512]{2,1,0:T(8,128)(2,1)}, u32[]{:S(2)}, u32[]{:S(2)}) collective-permute-start(bf16[8,128,512]{2,1,0:T(8,128)(2,1)} %all-to-all-done.2), channel_id=1, source_target_pairs={{0,1},{1,0},{2,3},{3,2},{4,5},{5,4},{6,7},{7,6},{8,9},{9,8},{10,11... | collective-permute-start | bytes 3145736 | tf_op jit(solution)/shard_map/ppermute | solution.py:319
  85.6 0.1 pad_add_fusion.1.place_ref
  85.6 2.6 %outer.1.rest_0_ = bf16[8,512,128]{2,1,0:T(8,128)(2,1)S(1)} custom-call(s32[2]{0:T(128)S(1)} %copy-done.7, bf16[1024,512]{1,0:T(8,128)(2,1)S(1)} %bitcast.29, bf16[1024,512]{1,0:T(8,128)(2,1)} %bitcast.13.quant_ref), custom_call_target="tpu_custom_call" | custom-call | flops 1 | bytes 1 | tf_op jit(solution)/shard_map/outer/pallas_call | solution.py:293
  88.2 0.3 collective-permute-done.5
  88.5 2.6 %outer_other.1 = bf16[8,512,128]{2,1,0:T(8,128)(2,1)S(1)} custom-call(s32[2]{0:T(128)S(1)} %pad_add_fusion.1.place_ref, bf16[1024,512]{1,0:T(8,128)(2,1)S(1)} %bitcast.30, bf16[1024,512]{1,0:T(8,128)(2,1)} %bitcast.12.quant_ref, bf16[8,512,128]{2,1,0:T(8,128)(2,1)S(1)} %outer.1.rest_0_), custom_call_target="tpu_custom_call", output_to_operand_aliasing={{}: (3, {})} | custom-call | flops 1 | bytes 1 | tf_op jit(solution)/shard_map/outer_other/pallas_call | solution.py:293
  91.1 0.0 copy-start.1
  91.1 1.0 copy-done.1
  92.1 12.6 %all-to-all-start.3 = ((bf16[8,512,128]{2,1,0:T(8,128)(2,1)}), bf16[8,512,128]{2,1,0:T(8,128)(2,1)}, u32[]{:S(2)}, u32[]{:S(2)}) async-start(bf16[8,512,128]{2,1,0:T(8,128)(2,1)} %copy-done.1), calls=%async_computation.4 | async-start | bytes 2097152 | tf_op jit(solution)/shard_map/all_to_all | solution.py:314
  104.8 1.9 %collective-permute-start.6 = (bf16[8,128,512]{2,1,0:T(8,128)(2,1)S(1)}, bf16[8,128,512]{2,1,0:T(8,128)(2,1)}, u32[]{:S(2)}, u32[]{:S(2)}) collective-permute-start(bf16[8,128,512]{2,1,0:T(8,128)(2,1)S(1)} %copy-done.4), channel_id=1, source_target_pairs={{0,1},{1,0},{2,3},{3,2},{4,5},{5,4},{6,7},{7,6},{8,9},{9,8},{10,11... | collective-permute-start | bytes 3145736 | tf_op jit(solution)/shard_map/ppermute | solution.py:319
  106.7 0.0 copy-done.10
  106.7 1.9 %collective-permute-start.4 = (bf16[128,1024]{1,0:T(8,128)(2,1)}, bf16[128,1024]{1,0:T(8,128)(2,1)}, u32[]{:S(2)}, u32[]{:S(2)}) collective-permute-start(bf16[128,1024]{1,0:T(8,128)(2,1)} %param.8), channel_id=1, source_target_pairs={{0,504},{8,0},{16,8},{24,16},{32,24},{40,32},{48,40},{56,48},{64,5... | collective-permute-start | bytes 786440 | tf_op jit(solution)/shard_map/ppermute | solution.py:368
  108.7 0.8 collective-permute-done.6.other_ref
  109.4 4.3 %rotor_grad.1 = f32[128,128]{1,0:T(8,128)} custom-call(s32[2]{0:T(128)S(1)} %copy-done.7, bf16[8,128,512]{2,1,0:T(8,128)(2,1)S(1)} %copy-done.4, bf16[8,128,512]{2,1,0:T(8,128)(2,1)} %collective-permute-done.6.other_ref, bf16[8,1024,128]{2,1,0:T(8,128)(2,1)S(1)} %bitcast.27, bf16[8,1024,128]{2,1,0:T(8,128)(2,1)S(1)} %bitcast.28, bf16[128,128]{1,0:T(8,128)(2,1)S(1)} %copy-done.6), custom_call_target="tpu_custom_call" | custom-call | flops 1 | bytes 1 | tf_op jit(solution)/shard_map/rotor_grad/pallas_call | solution.py:257
  113.7 22.8 %all-to-all-done.3 = bf16[8,512,128]{2,1,0:T(8,128)(2,1)} async-done(((bf16[8,512,128]{2,1,0:T(8,128)(2,1)}), bf16[8,512,128]{2,1,0:T(8,128)(2,1)}, u32[]{:S(2)}, u32[]{:S(2)}) %all-to-all-start.3) | async-done | bytes 1048608 | tf_op jit(solution)/shard_map/all_to_all | solution.py:314
  136.6 1.4 convert_reduce_fusion
  138.0 1.9 %collective-permute-start.7 = (bf16[512,128]{1,0:T(8,128)(2,1)S(1)}, bf16[512,128]{1,0:T(8,128)(2,1)S(1)}, u32[]{:S(2)}, u32[]{:S(2)}) collective-permute-start(bf16[512,128]{1,0:T(8,128)(2,1)S(1)} %fusion.4), channel_id=1, source_target_pairs={{0,8},{8,0},{1,9},{9,1},{2,10},{10,2},{3,11},{11,3},{4,12},{12,4},... | collective-permute-start | bytes 393224 | tf_op jit(solution)/shard_map/ppermute | solution.py:319
  140.0 0.0 collective-permute-done.4
  140.0 0.0 reduce-scatter.2.cloned.1.call-done
  140.0 2.0 %fusion.2 = bf16[128,1024]{1,0:T(8,128)(2,1)} fusion(bf16[128,1024]{1,0:T(8,128)(2,1)S(1)} %copy-done.9, bf16[128,1024]{1,0:T(8,128)(2,1)} %collective-permute-done.4, bf16[1,128,1024]{2,1,0:T(8,128)(2,1)} %reduce-scatter.2.cloned.1.call-done, f32[1024]{0:T(1024)S(1)} %bitcast.35, f32[128]{0:T(128)S(1)} %bitcast.31, pred[1024]{0:T(1024)(128)(4,1)S(1)} %compare_reduce_fusion), kind=kLoop, calls=%fused_computation.4 | loop fusion | flops 1572864 | bytes 1054208 | tf_op jit(solution)/shard_map/convert_element_type | solution.py:381
  142.0 9.9 %collective-permute-done.7 = bf16[512,128]{1,0:T(8,128)(2,1)S(1)} collective-permute-done((bf16[512,128]{1,0:T(8,128)(2,1)S(1)}, bf16[512,128]{1,0:T(8,128)(2,1)S(1)}, u32[]{:S(2)}, u32[]{:S(2)}) %collective-permute-start.7) | collective-permute-done | bytes 131104 | tf_op jit(solution)/shard_map/ppermute | solution.py:319
  152.0 0.7 fusion.3
  (15 shorter events, 0.1 us)
Async XLA Ops:
  7.2 8.6 %copy-start = (bf16[8192,128]{1,0:T(8,128)(2,1)S(1)}, bf16[8192,128]{1,0:T(8,128)(2,1)}, u32[]{:S(2)}) copy-start(bf16[8192,128]{1,0:T(8,128)(2,1)} %w_ref.7) | copy-start | bytes 6291460
  7.2 8.6 %copy-start.6 = (bf16[128,128]{1,0:T(8,128)(2,1)S(1)}, bf16[128,128]{1,0:T(8,128)(2,1)}, u32[]{:S(2)}) copy-start(bf16[128,128]{1,0:T(8,128)(2,1)} %dv_ref.7) | copy-start | bytes 98308
  7.2 8.6 %copy-start.5 = (bf16[128,128]{1,0:T(8,128)(2,1)S(1)}, bf16[128,128]{1,0:T(8,128)(2,1)}, u32[]{:S(2)}) copy-start(bf16[128,128]{1,0:T(8,128)(2,1)} %r2_ref.5) | copy-start | bytes 98308
  7.2 52.2 %all-gather.3.cloned.1.call-start = ((), (), s32[]{:S(2)}) async-start(), calls=%async_computation.6 | async-start | bytes 1474560 | tf_op jit(solution)/shard_map/all_gather | solution.py:340
  7.8 8.0 %copy-start.7 = (s32[2]{0:T(128)S(1)}, s32[2]{0:T(128)}, u32[]{:S(2)}) copy-start(s32[2]{0:T(128)} %pad_add_fusion.core_ref.place_ref) | copy-start | bytes 28
  11.7 4.1 %collective-permute-start = (bf16[2304,128]{1,0:T(8,128)(2,1)}, bf16[2304,128]{1,0:T(8,128)(2,1)S(1)}, u32[]{:S(2)}, u32[]{:S(2)}) collective-permute-start(bf16[2304,128]{1,0:T(8,128)(2,1)} %get-tuple-element.20), channel_id=1, source_target_pairs={{0,1},{1,0},{2,3},{3,2},{4,5},{5,4},{6,7},{7,6},{8,9},{9,8},{10,11... | collective-permute-start | bytes 1769480 | tf_op jit(solution)/shard_map/ppermute | solution.py:319
  13.6 10.9 %copy-start.9 = (bf16[128,1024]{1,0:T(8,128)(2,1)S(1)}, bf16[128,1024]{1,0:T(8,128)(2,1)}, u32[]{:S(2)}) copy-start(bf16[128,1024]{1,0:T(8,128)(2,1)} %x_ref.1) | copy-start | bytes 786436
  19.0 24.1 %all-to-all-start = ((bf16[4,128,512]{2,1,0:T(8,128)(2,1)}), bf16[4,128,512]{2,1,0:T(8,128)(2,1)S(1)}, u32[]{:S(2)}, u32[]{:S(2)}) async-start(bf16[4,128,512]{2,1,0:T(8,128)(2,1)} %frame_pairs.1), calls=%async_computation | async-start | bytes 1048576 | tf_op jit(solution)/shard_map/all_to_all | solution.py:314
  24.5 26.6 %copy-start.11 = (s32[1,128]{1,0:T(1,128)S(1)}, s32[1,128]{1,0:T(1,128)}, u32[]{:S(2)}) copy-start(s32[1,128]{1,0:T(1,128)} %param.13) | copy-start | bytes 1540
  24.7 3.0 %collective-permute-start.1 = (f32[1,128]{1,0:T(1,128)S(1)}, f32[1,128]{1,0:T(1,128)S(1)}, u32[]{:S(2)}, u32[]{:S(2)}) collective-permute-start(f32[1,128]{1,0:T(1,128)S(1)} %bitcast.36), channel_id=1, source_target_pairs={{0,1},{1,0},{2,3},{3,2},{4,5},{5,4},{6,7},{7,6},{8,9},{9,8},{10,11... | collective-permute-start | bytes 1544 | tf_op jit(solution)/shard_map/ppermute | solution.py:319
  27.7 9.1 %collective-permute-start.2 = (f32[1,128]{1,0:T(1,128)S(1)}, f32[1,128]{1,0:T(1,128)S(1)}, u32[]{:S(2)}, u32[]{:S(2)}) collective-permute-start(f32[1,128]{1,0:T(1,128)S(1)} %bitcast_add_fusion), channel_id=1, source_target_pairs={{0,2},{2,0},{4,6},{6,4},{1,3},{3,1},{5,7},{7,5},{8,10},{10,8},{12,... | collective-permute-start | bytes 1544 | tf_op jit(solution)/shard_map/ppermute | solution.py:327
  36.8 6.3 %collective-permute-start.3 = (f32[1,128]{1,0:T(1,128)S(1)}, f32[1,128]{1,0:T(1,128)S(1)}, u32[]{:S(2)}, u32[]{:S(2)}) collective-permute-start(f32[1,128]{1,0:T(1,128)S(1)} %add.43), channel_id=1, source_target_pairs={{0,4},{2,6},{4,0},{6,2},{1,5},{3,7},{5,1},{7,3},{8,12},{10,14},{12... | collective-permute-start | bytes 1544 | tf_op jit(solution)/shard_map/ppermute | solution.py:327
  44.3 20.0 %all-to-all-start.1 = ((bf16[8,128,512]{2,1,0:T(8,128)(2,1)}), bf16[8,128,512]{2,1,0:T(8,128)(2,1)S(1)}, u32[]{:S(2)}, u32[]{:S(2)}) async-start(bf16[8,128,512]{2,1,0:T(8,128)(2,1)} %broadcast_in_dim.20), calls=%async_computation.1 | async-start | bytes 2097152 | tf_op jit(solution)/shard_map/all_to_all | solution.py:314
  58.1 1.3 copy-start.2
  59.4 1.3 copy-start.8
  63.3 1.0 copy-start.3
  64.2 19.4 %all-to-all-start.2 = ((bf16[8,128,512]{2,1,0:T(8,128)(2,1)}), bf16[8,128,512]{2,1,0:T(8,128)(2,1)}, u32[]{:S(2)}, u32[]{:S(2)}) async-start(bf16[8,128,512]{2,1,0:T(8,128)(2,1)} %copy-done.3), calls=%async_computation.2 | async-start | bytes 2097152 | tf_op jit(solution)/shard_map/all_to_all | solution.py:314
  69.9 70.1 %reduce-scatter.2.cloned.1.call-start = ((), (), s32[]{:S(2)}) async-start(), calls=%async_computation.5 | async-start | bytes 2359296 | tf_op jit(solution)/shard_map/reduce_scatter | solution.py:362
  83.6 4.9 %collective-permute-start.5 = (bf16[8,128,512]{2,1,0:T(8,128)(2,1)}, bf16[8,128,512]{2,1,0:T(8,128)(2,1)}, u32[]{:S(2)}, u32[]{:S(2)}) collective-permute-start(bf16[8,128,512]{2,1,0:T(8,128)(2,1)} %all-to-all-done.2), channel_id=1, source_target_pairs={{0,1},{1,0},{2,3},{3,2},{4,5},{5,4},{6,7},{7,6},{8,9},{9,8},{10,11... | collective-permute-start | bytes 3145736 | tf_op jit(solution)/shard_map/ppermute | solution.py:319
  91.1 1.0 copy-start.1
  92.1 12.6 %copy-start.4 = (bf16[8,128,512]{2,1,0:T(8,128)(2,1)S(1)}, bf16[8,128,512]{2,1,0:T(8,128)(2,1)}, u32[]{:S(2)}) copy-start(bf16[8,128,512]{2,1,0:T(8,128)(2,1)} %copy-done.3) | copy-start | bytes 3145732
  92.1 14.6 %copy-start.10 = (f32[1,1024]{1,0:T(1,128)S(1)}, f32[1,1024]{1,0:T(1,128)}, u32[]{:S(2)}) copy-start(f32[1,1024]{1,0:T(1,128)} %scale_ref.1) | copy-start | bytes 12292
  92.1 44.5 %all-to-all-start.3 = ((bf16[8,512,128]{2,1,0:T(8,128)(2,1)}), bf16[8,512,128]{2,1,0:T(8,128)(2,1)}, u32[]{:S(2)}, u32[]{:S(2)}) async-start(bf16[8,512,128]{2,1,0:T(8,128)(2,1)} %copy-done.1), calls=%async_computation.4 | async-start | bytes 2097152 | tf_op jit(solution)/shard_map/all_to_all | solution.py:314
  104.8 4.7 %collective-permute-start.6 = (bf16[8,128,512]{2,1,0:T(8,128)(2,1)S(1)}, bf16[8,128,512]{2,1,0:T(8,128)(2,1)}, u32[]{:S(2)}, u32[]{:S(2)}) collective-permute-start(bf16[8,128,512]{2,1,0:T(8,128)(2,1)S(1)} %copy-done.4), channel_id=1, source_target_pairs={{0,1},{1,0},{2,3},{3,2},{4,5},{5,4},{6,7},{7,6},{8,9},{9,8},{10,11... | collective-permute-start | bytes 3145736 | tf_op jit(solution)/shard_map/ppermute | solution.py:319
  106.7 33.2 %collective-permute-start.4 = (bf16[128,1024]{1,0:T(8,128)(2,1)}, bf16[128,1024]{1,0:T(8,128)(2,1)}, u32[]{:S(2)}, u32[]{:S(2)}) collective-permute-start(bf16[128,1024]{1,0:T(8,128)(2,1)} %param.8), channel_id=1, source_target_pairs={{0,504},{8,0},{16,8},{24,16},{32,24},{40,32},{48,40},{56,48},{64,5... | collective-permute-start | bytes 786440 | tf_op jit(solution)/shard_map/ppermute | solution.py:368
  138.0 13.9 %collective-permute-start.7 = (bf16[512,128]{1,0:T(8,128)(2,1)S(1)}, bf16[512,128]{1,0:T(8,128)(2,1)S(1)}, u32[]{:S(2)}, u32[]{:S(2)}) collective-permute-start(bf16[512,128]{1,0:T(8,128)(2,1)S(1)} %fusion.4), channel_id=1, source_target_pairs={{0,8},{8,0},{1,9},{9,1},{2,10},{10,2},{3,11},{11,3},{4,12},{12,4},... | collective-permute-start | bytes 393224 | tf_op jit(solution)/shard_map/ppermute | solution.py:319
Sparse Core Ops, SparseCore 0:
  13.8 42.8 all-gather.2
  73.6 56.4 reduce-scatter.1

commit v7 on v6

--- a/solution.py
+++ b/solution.py
@@ -47,49 +47,84 @@
     )
 
 
-def prepare_kernel(core_ref, x_ref, scale_ref, w_ref, r2_ref, dv_ref, out_ref, send_ref):
+def three_terms(value):
+    top = value.astype(jnp.bfloat16).astype(jnp.float32)
+    rest = value - top
+    mid = rest.astype(jnp.bfloat16).astype(jnp.float32)
+    return top, mid, rest - mid
+
+
+def in_rows(terms, width):
+    row = lax.broadcasted_iota(jnp.int32, (16, width), 0)
+    out = jnp.zeros((16, width), jnp.float32)
+    for index, term in enumerate(terms):
+        out = jnp.where(row == index, term, out)
+    return out.astype(jnp.bfloat16)
+
+
+def inputs_kernel(core_ref, x_ref, w_ref, r2_ref, dv_ref, send_ref):
     step = pl.program_id(0)
     send_ref[pl.ds(pl.multiple_of(step * 512, 512), 512), :] = w_ref[...]
 
     @pl.when(step == 0)
     def _():
-        scale = scale_ref[...]
-        top = scale.astype(jnp.bfloat16).astype(jnp.float32)
-        rest = scale - top
-        mid = rest.astype(jnp.bfloat16).astype(jnp.float32)
-        low = rest - mid
-        row = lax.broadcasted_iota(jnp.int32, (16, scale.shape[1]), 0)
-        extra = jnp.where(row == 0, top, jnp.where(row == 1, mid, jnp.where(row == 2, low, 0.0)))
-        out_ref[0:128, :] = x_ref[...]
-        out_ref[128:144, :] = extra.astype(jnp.bfloat16)
+        squares = jnp.zeros((128, 128), jnp.float32)
+        for lane in range(8):
+            x = x_ref[:, lane * 128 : (lane + 1) * 128].astype(jnp.float32)
+            squares += x * x
+        squares = jnp.sum(jnp.transpose(squares), axis=0, keepdims=True)
         send_ref[2048:2176, :] = r2_ref[...]
         send_ref[2176:2304, :] = dv_ref[...]
-
-
-def prepare(core, hidden, scale, weight, rotor, value_grad):
+        send_ref[2304:2320, :] = in_rows(three_terms(squares), 128)
+
+
+def core_inputs(core, hidden, weight, rotor, value_grad):
     whole = lambda i, core: (0, 0)
     return pl.pallas_call(
-        prepare_kernel,
+        inputs_kernel,
         grid_spec=pltpu.PrefetchScalarGridSpec(
             num_scalar_prefetch=1,
             grid=(4,),
             in_specs=[
                 pl.BlockSpec((128, 1024), whole),
-                pl.BlockSpec((1, 1024), whole),
                 pl.BlockSpec((512, 128), lambda i, core: (i * 2 + 1 - core[0], 0)),
                 pl.BlockSpec((128, 128), whole),
                 pl.BlockSpec((128, 128), whole),
             ],
-            out_specs=[pl.BlockSpec((144, 1024), whole), pl.BlockSpec((2304, 128), whole)],
+            out_specs=pl.BlockSpec((2320, 128), whole),
         ),
-        out_shape=[
-            jax.ShapeDtypeStruct((144, 1024), jnp.bfloat16),
-            jax.ShapeDtypeStruct((2304, 128), jnp.bfloat16),
+        out_shape=jax.ShapeDtypeStruct((2320, 128), jnp.bfloat16),
+        compiler_params=pltpu.CompilerParams(vmem_limit_bytes=WHOLE),
+        cost_estimate=CHEAP,
+        name="core_inputs",
+    )(core, hidden, weight, rotor, value_grad)
+
+
+def pack_kernel(x_ref, scale_ref, mine_ref, other_ref, out_ref):
+    terms = mine_ref[...].astype(jnp.float32), other_ref[...].astype(jnp.float32)
+    sums = [term[0:1] + term[1:2] + term[2:3] for term in terms]
+    squares = jnp.concatenate([sums[0] + sums[1], jnp.zeros((1, 896), jnp.float32)], axis=1)
+    out_ref[0:128, :] = x_ref[...]
+    out_ref[128:144, :] = in_rows(three_terms(scale_ref[...]) + three_terms(squares), 1024)
+
+
+def pack(hidden, scale, mine, other):
+    whole = lambda i: (0, 0)
+    return pl.pallas_call(
+        pack_kernel,
+        grid=(1,),
+        in_specs=[
+            pl.BlockSpec((128, 1024), whole),
+            pl.BlockSpec((1, 1024), whole),
+            pl.BlockSpec((16, 128), lambda i: (144, 0)),
+            pl.BlockSpec((16, 128), lambda i: (144, 0)),
         ],
-        compiler_params=pltpu.CompilerParams(vmem_limit_bytes=WHOLE),
-        cost_estimate=CHEAP,
-        name="prepare",
-    )(core, hidden, scale, weight, rotor, value_grad)
+        out_specs=pl.BlockSpec((144, 1024), whole),
+        out_shape=jax.ShapeDtypeStruct((144, 1024), jnp.bfloat16),
+        compiler_params=pltpu.CompilerParams(vmem_limit_bytes=BIG),
+        cost_estimate=CHEAP,
+        name="pack",
+    )(hidden, scale, mine, other)
 
 
 def rotated_rows(w_ref, r2_ref):
@@ -182,8 +217,12 @@
     )(weight, rotor, top, value_grad)
 
 
-def quant_kernel(core_ref, all_ref, mask_ref, inv_ref, quant_ref):
-    inverse = jnp.transpose(jnp.broadcast_to(inv_ref[...], (128, 128)))
+def quant_kernel(core_ref, all_ref, sum_ref, mask_ref, quant_ref, inv_ref):
+    squares = jnp.sum(sum_ref[...].astype(jnp.float32), axis=0)
+    squares = squares[3:4] + squares[4:5] + squares[5:6]
+    inverse = lax.rsqrt(squares / 8192.0 + NORM_EPS)
+    inv_ref[...] = inverse
+    inverse = jnp.transpose(jnp.broadcast_to(inverse, (128, 128)))
     mask = mask_ref[0]
     scale = all_ref[0, 128:144, :].astype(jnp.float32)
     scale = scale[0:1] + scale[1:2] + scale[2:3]
@@ -199,7 +238,7 @@
         quant_ref[zl, :, place * 128 : (place + 1) * 128] = quant
 
 
-def quantize(core, hidden_all, mask, inverse):
+def quantize(core, hidden_all, mask):
     return pl.pallas_call(
         quant_kernel,
         grid_spec=pltpu.PrefetchScalarGridSpec(
@@ -207,16 +246,22 @@
             grid=(4,),
             in_specs=[
                 pl.BlockSpec((1, 144, 1024), lambda i, core: (i, 0, 0)),
+                pl.BlockSpec((4, 16, 128), lambda i, core: (0, 8, 0)),
                 pl.BlockSpec((1, 1, 1024), lambda i, core: (i * 2 + core[0], 0, 0)),
+            ],
+            out_specs=[
+                pl.BlockSpec((2, 128, 512), lambda i, core: (i, 0, 0)),
                 pl.BlockSpec((1, 128), lambda i, core: (0, 0)),
             ],
-            out_specs=pl.BlockSpec((2, 128, 512), lambda i, core: (i, 0, 0)),
         ),
-        out_shape=jax.ShapeDtypeStruct((8, 128, 512), jnp.bfloat16),
+        out_shape=[
+            jax.ShapeDtypeStruct((8, 128, 512), jnp.bfloat16),
+            jax.ShapeDtypeStruct((1, 128), jnp.float32),
+        ],
         compiler_params=pltpu.CompilerParams(vmem_limit_bytes=BIG),
         cost_estimate=pl.CostEstimate(flops=10_350_000_000, bytes_accessed=1, transcendentals=0),
         name="quantize",
-    )(core, hidden_all, mask, inverse)
+    )(core, hidden_all, hidden_all, mask)
 
 
 def rotor_grad_kernel(core_ref, mine_ref, other_ref, wm_ref, wo_ref, dv_ref, r2_ref, total_ref):
@@ -323,10 +368,6 @@
     return shifted(value, "c", 1)
 
 
-def flipped(value, bit):
-    return lax.ppermute(value, "yl", [(chip, chip ^ bit) for chip in range(4)])
-
-
 def local(hidden_in, grad_sent, value_grad, value_weight, rotation, act_scale, outliers):
     sections = 64
     pairs = [(source, (source - 1) % sections) for source in range(sections)]
@@ -336,22 +377,19 @@
     wide = lambda value: value.astype(jnp.float32)
     tie = lax.optimization_barrier
 
-    packed, inputs = prepare(place, hidden_in, act_scale, value_weight, rotation, value_grad)
+    inputs = core_inputs(place, hidden_in, value_weight, rotation, value_grad)
+    received = swap_core(inputs)
+    packed = pack(hidden_in, act_scale, inputs, received)
     hidden_all = lax.all_gather(packed, "yl", axis=0)
 
-    frame_pair = frame_pairs(place, value_weight, rotation, value_grad, swap_core(inputs))
-    frame_pair, hidden_two = tie((frame_pair, hidden_in))
+    frame_pair = frame_pairs(place, value_weight, rotation, value_grad, received)
+    frame_pair, rotor = tie((frame_pair, rotation))
     frame_terms = exchange(frame_pair, "yl")
-    squares = jnp.sum(wide(hidden_two) * wide(hidden_two), axis=1).reshape(1, 128)
-    squares = squares + swap_core(squares)
-    squares = squares + flipped(squares, 1)
-    squares = squares + flipped(squares, 2)
-    inverse = lax.rsqrt(squares / 8192.0 + NORM_EPS)
-    frame_terms, inverse, rotor = tie((frame_terms, inverse, rotation))
+    top = rotated_top(value_weight, rotor)
+    grad_parts = weight_grad(value_weight, rotor, top, value_grad)
+    frame_terms, grad_parts = tie((frame_terms, grad_parts))
     frame = jnp.sum(wide(frame_terms), axis=0).astype(jnp.bfloat16)
     frames = exchange(jnp.broadcast_to(frame[None], (8, 128, 512)), NEAR).reshape(1024, 512)
-    top = rotated_top(value_weight, rotor)
-    grad_parts = weight_grad(value_weight, rotor, top, value_grad)
 
     ids = outliers[0]
     blocks = (ids[None, :] // 128 == jnp.arange(64)[:, None]).astype(jnp.bfloat16)
@@ -360,7 +398,7 @@
 
     hidden_all, mask, grad_parts = tie((hidden_all, mask, grad_parts))
     grad_sum = lax.psum_scatter(grad_parts, TPA, scatter_dimension=0, tiled=False)
-    quant = quantize(place, hidden_all, mask, inverse)
+    quant, inverse = quantize(place, hidden_all, mask)
     frames, quant = tie((frames, quant))
     quants = exchange(quant, NEAR)
     quants, quant, grad_sent = tie((quants, quant, grad_sent))

time: 160 us -> 159 us (level)
  the two profiles are of different devices: /device:TPU:48 before, /device:TPU:41 now
where the time goes in v7:
time: 159 us; the launch traced here: 158 us
  waiting for transfers between devices  66.7 us (42%)
  starting transfers between devices  38.7 us (24%)
  Pallas kernels  25.6 us (16%)
  between operations  14.3 us (9%)
  local copies, waits for them, and re-layouts  7.52 us (5%)
  other arithmetic  4.96 us (3%)
    all_to_all x4, waiting for transfers between devices, exchange(): return lax.all_to_all(value, axes, split_axis=0, concat_axis=0, tiled=True)  39.6 us
    all_to_all x4, starting transfers between devices, exchange(): return lax.all_to_all(value, axes, split_axis=0, concat_axis=0, tiled=True)  25.4 us
    all_gather x1, waiting for transfers between devices, local(): hidden_all = lax.all_gather(packed, 'yl', axis=0)  14.7 us
    ppermute x4, waiting for transfers between devices, shifted(): lax.ppermute(value, axis, [(chip, (chip + turn) % count) for chip in rang...  11.6 us
    ppermute x4, starting transfers between devices, shifted(): lax.ppermute(value, axis, [(chip, (chip + turn) % count) for chip in rang...  10.4 us
    unnamed x28, local copies, waits for them, and re-layouts  6.45 us
    pallas_call x1, Pallas kernels, weight_grad(): pl.pallas_call(weight_grad_kernel, grid=(8,), in_specs=[pl.BlockSpec((102...  5.35 us
    pallas_call x2, Pallas kernels, outer(): pl.pallas_call(outer_kernel, grid_spec=pltpu.PrefetchScalarGridSpec(num_s...  5.22 us
  transfers between devices with their start and end apart: 11, of which 6 were waited for; matrix products, arithmetic and copies ran while one was open for 3% of the time, Pallas kernels for 13%

profile of v7, /device:TPU:41, one launch (start us, length us, event | category | flops | bytes accessed | tf_op | source)
XLA Modules:
  0.0 158.1 jit_solution(10213657503094063244)
XLA Ops:
  7.2 0.0 copy-start.6
  7.2 0.0 copy-start.10
  7.2 0.0 all-gather.3.cloned.1.call-start
  7.2 0.6 pad_add_fusion.core_ref.place_ref
  7.8 0.0 copy-start
  7.8 0.0 copy-start.8
  7.8 0.0 copy-start.9
  7.8 3.8 %core_inputs.1.mine_ref = bf16[2320,128]{1,0:T(8,128)(2,1)} custom-call(s32[2]{0:T(128)} %pad_add_fusion.core_ref.place_ref, bf16[128,1024]{1,0:T(8,128)(2,1)} %x_ref.3, bf16[8192,128]{1,0:T(8,128)(2,1)} %w_ref.7, bf16[128,128]{1,0:T(8,128)(2,1)} %r2_ref.5, bf16[128,128]{1,0:T(8,128)(2,1)} %dv_ref.7), custom_call_target="tpu_custom_call" | custom-call | flops 1 | bytes 1 | tf_op jit(solution)/shard_map/core_inputs/pallas_call | solution.py:83
  11.7 2.6 %collective-permute-start = (bf16[2320,128]{1,0:T(8,128)(2,1)}, bf16[2320,128]{1,0:T(8,128)(2,1)S(1)}, u32[]{:S(2)}, u32[]{:S(2)}) collective-permute-start(bf16[2320,128]{1,0:T(8,128)(2,1)} %core_inputs.1.mine_ref), channel_id=1, source_target_pairs={{0,1},{1,0},{2,3},{3,2},{4,5},{5,4},{6,7},{7,6},{8,9},{9,8},{10,11... | collective-permute-start | bytes 1781768 | tf_op jit(solution)/shard_map/ppermute | solution.py:364
  14.2 1.8 %collective-permute-done.w2_ref.r22_ref.dv2_ref.other_ref = bf16[2320,128]{1,0:T(8,128)(2,1)S(1)} collective-permute-done((bf16[2320,128]{1,0:T(8,128)(2,1)}, bf16[2320,128]{1,0:T(8,128)(2,1)S(1)}, u32[]{:S(2)}, u32[]{:S(2)}) %collective-permute-start) | collective-permute-done | bytes 593952 | tf_op jit(solution)/shard_map/ppermute | solution.py:364
  16.1 0.0 copy-done.6
  16.1 0.0 copy-done.10
  16.1 1.1 copy-done.5
  17.1 0.8 pack.1
  17.9 0.0 all-gather.3.cloned.1.call-update
  17.9 0.0 copy-done
  17.9 0.0 copy-done.8
  18.0 0.0 copy-done.9
  18.0 0.0 copy-done.11
  18.0 2.3 %frame_pairs.1 = bf16[4,128,512]{2,1,0:T(8,128)(2,1)S(1)} custom-call(s32[2]{0:T(128)S(1)} %copy-done.11, bf16[8192,128]{1,0:T(8,128)(2,1)S(1)} %copy-done, bf16[128,128]{1,0:T(8,128)(2,1)S(1)} %copy-done.8, bf16[128,128]{1,0:T(8,128)(2,1)S(1)} %copy-done.9, bf16[2320,128]{1,0:T(8,128)(2,1)S(1)} %collective-permute-done.w2_ref.r22_ref.dv2_ref.other_ref, ...), custom_call_target="tpu_custom_call" | custom-call | flops 23000000512 | bytes 1 | tf_op jit(solution)/shard_map/frame_pairs/pallas_call | solution.py:156
  20.2 0.0 copy-start.7
  20.2 0.8 copy-done.7
  21.1 4.5 %all-to-all-start = ((bf16[4,128,512]{2,1,0:T(8,128)(2,1)}), bf16[4,128,512]{2,1,0:T(8,128)(2,1)S(1)}, u32[]{:S(2)}, u32[]{:S(2)}) async-start(bf16[4,128,512]{2,1,0:T(8,128)(2,1)} %copy-done.7), calls=%async_computation | async-start | bytes 1048576 | tf_op jit(solution)/shard_map/all_to_all | solution.py:359
  25.6 1.3 rotated_top.1.top_ref
  26.9 5.3 %weight_grad.1 = bf16[8,128,1024]{2,1,0:T(8,128)(2,1)S(1)} custom-call(bf16[8192,128]{1,0:T(8,128)(2,1)S(1)} %copy-done, bf16[128,128]{1,0:T(8,128)(2,1)S(1)} %copy-done.8, f32[1,128]{1,0:T(1,128)S(1)} %rotated_top.1.top_ref, bf16[128,128]{1,0:T(8,128)(2,1)S(1)} %copy-done.9), custom_call_target="tpu_custom_call" | custom-call | flops 1 | bytes 1 | tf_op jit(solution)/shard_map/weight_grad/pallas_call | solution.py:208
  32.3 0.0 copy-start.2
  32.3 1.3 copy-done.2
  33.6 3.2 %all-to-all-done = bf16[4,128,512]{2,1,0:T(8,128)(2,1)S(1)} async-done(((bf16[4,128,512]{2,1,0:T(8,128)(2,1)}), bf16[4,128,512]{2,1,0:T(8,128)(2,1)S(1)}, u32[]{:S(2)}, u32[]{:S(2)}) %all-to-all-start) | async-done | bytes 524320 | tf_op jit(solution)/shard_map/all_to_all | solution.py:359
  36.8 0.1 reduce_sum.21
  36.9 1.1 broadcast_in_dim.20
  38.0 5.8 %all-to-all-start.1 = ((bf16[8,128,512]{2,1,0:T(8,128)(2,1)}), bf16[8,128,512]{2,1,0:T(8,128)(2,1)S(1)}, u32[]{:S(2)}, u32[]{:S(2)}) async-start(bf16[8,128,512]{2,1,0:T(8,128)(2,1)} %broadcast_in_dim.20), calls=%async_computation.1 | async-start | bytes 2097152 | tf_op jit(solution)/shard_map/all_to_all | solution.py:359
  43.8 0.0 copy-done.13
  43.8 0.2 fusion.5
  44.0 14.7 %all-gather.3.cloned.1.call-done = bf16[576,1024]{1,0:T(8,128)(2,1)} async-done(((bf16[144,1024]{1,0:T(8,128)(2,1)}), bf16[576,1024]{1,0:T(8,128)(2,1)}) %all-gather.3.cloned.1.call-update) | async-done | bytes 1179664 | tf_op jit(solution)/shard_map/all_gather | solution.py:383
  58.7 1.3 copy-done.12
  60.0 2.6 %quantize.1 = (bf16[8,128,512]{2,1,0:T(8,128)(2,1)S(1)}, f32[1,128]{1,0:T(1,128)S(1)}) custom-call(s32[2]{0:T(128)S(1)} %copy-done.11, bf16[4,144,1024]{2,1,0:T(8,128)(2,1)S(1)} %bitcast.32, bf16[4,144,1024]{2,1,0:T(8,128)(2,1)S(1)} %bitcast.33, f32[8,1,1024]{2,1,0:T(1,128)S(1)} %bitcast.30), custom_call_target="tpu_custom_call" | custom-call | flops 10350000128 | bytes 1 | tf_op jit(solution)/shard_map/quantize/pallas_call | solution.py:242
  62.6 0.0 copy-start.3
  62.6 1.0 copy-done.3
  63.6 0.0 all-to-all-done.1
  63.6 5.8 %all-to-all-start.2 = ((bf16[8,128,512]{2,1,0:T(8,128)(2,1)}), bf16[8,128,512]{2,1,0:T(8,128)(2,1)}, u32[]{:S(2)}, u32[]{:S(2)}) async-start(bf16[8,128,512]{2,1,0:T(8,128)(2,1)} %copy-done.3), calls=%async_computation.2 | async-start | bytes 2097152 | tf_op jit(solution)/shard_map/all_to_all | solution.py:359
  69.4 0.0 reduce-scatter.2.cloned.1.call-start
  69.4 0.7 reduce-scatter.2.cloned.1.call-update
  70.1 14.4 %all-to-all-done.2 = bf16[8,128,512]{2,1,0:T(8,128)(2,1)} async-done(((bf16[8,128,512]{2,1,0:T(8,128)(2,1)}), bf16[8,128,512]{2,1,0:T(8,128)(2,1)}, u32[]{:S(2)}, u32[]{:S(2)}) %all-to-all-start.2) | async-done | bytes 1048608 | tf_op jit(solution)/shard_map/all_to_all | solution.py:359
  84.6 3.5 %collective-permute-start.2 = (bf16[8,128,512]{2,1,0:T(8,128)(2,1)}, bf16[8,128,512]{2,1,0:T(8,128)(2,1)}, u32[]{:S(2)}, u32[]{:S(2)}) collective-permute-start(bf16[8,128,512]{2,1,0:T(8,128)(2,1)} %all-to-all-done.2), channel_id=1, source_target_pairs={{0,1},{1,0},{2,3},{3,2},{4,5},{5,4},{6,7},{7,6},{8,9},{9,8},{10,11... | collective-permute-start | bytes 3145736 | tf_op jit(solution)/shard_map/ppermute | solution.py:364
  88.1 0.1 pad_add_fusion.1.place_ref
  88.2 2.6 %outer.1.rest_0_ = bf16[8,512,128]{2,1,0:T(8,128)(2,1)S(1)} custom-call(s32[2]{0:T(128)S(1)} %copy-done.11, bf16[1024,512]{1,0:T(8,128)(2,1)S(1)} %bitcast.27, bf16[1024,512]{1,0:T(8,128)(2,1)} %bitcast.12.quant_ref), custom_call_target="tpu_custom_call" | custom-call | flops 1 | bytes 1 | tf_op jit(solution)/shard_map/outer/pallas_call | solution.py:338
  90.8 0.0 collective-permute-done.2
  90.8 2.6 %outer_other.1 = bf16[8,512,128]{2,1,0:T(8,128)(2,1)S(1)} custom-call(s32[2]{0:T(128)S(1)} %pad_add_fusion.1.place_ref, bf16[1024,512]{1,0:T(8,128)(2,1)S(1)} %bitcast.28, bf16[1024,512]{1,0:T(8,128)(2,1)} %bitcast.11.quant_ref, bf16[8,512,128]{2,1,0:T(8,128)(2,1)S(1)} %outer.1.rest_0_), custom_call_target="tpu_custom_call", output_to_operand_aliasing={{}: (3, {})} | custom-call | flops 1 | bytes 1 | tf_op jit(solution)/shard_map/outer_other/pallas_call | solution.py:338
  93.4 0.0 copy-start.1
  93.4 1.0 copy-done.1
  94.4 9.3 %all-to-all-start.3 = ((bf16[8,512,128]{2,1,0:T(8,128)(2,1)}), bf16[8,512,128]{2,1,0:T(8,128)(2,1)}, u32[]{:S(2)}, u32[]{:S(2)}) async-start(bf16[8,512,128]{2,1,0:T(8,128)(2,1)} %copy-done.1), calls=%async_computation.4 | async-start | bytes 2097152 | tf_op jit(solution)/shard_map/all_to_all | solution.py:359
  103.7 0.0 copy-done.4
  103.7 2.4 %collective-permute-start.3 = (bf16[8,128,512]{2,1,0:T(8,128)(2,1)S(1)}, bf16[8,128,512]{2,1,0:T(8,128)(2,1)}, u32[]{:S(2)}, u32[]{:S(2)}) collective-permute-start(bf16[8,128,512]{2,1,0:T(8,128)(2,1)S(1)} %copy-done.4), channel_id=1, source_target_pairs={{0,1},{1,0},{2,3},{3,2},{4,5},{5,4},{6,7},{7,6},{8,9},{9,8},{10,11... | collective-permute-start | bytes 3145736 | tf_op jit(solution)/shard_map/ppermute | solution.py:364
  106.2 2.9 %collective-permute-start.1 = (bf16[128,1024]{1,0:T(8,128)(2,1)}, bf16[128,1024]{1,0:T(8,128)(2,1)}, u32[]{:S(2)}, u32[]{:S(2)}) collective-permute-start(bf16[128,1024]{1,0:T(8,128)(2,1)} %param.8), channel_id=1, source_target_pairs={{0,504},{8,0},{16,8},{24,16},{32,24},{40,32},{48,40},{56,48},{64,5... | collective-permute-start | bytes 786440 | tf_op jit(solution)/shard_map/ppermute | solution.py:406
  109.0 0.0 collective-permute-done.3.other_ref
  109.0 4.3 %rotor_grad.1 = f32[128,128]{1,0:T(8,128)} custom-call(s32[2]{0:T(128)S(1)} %copy-done.11, bf16[8,128,512]{2,1,0:T(8,128)(2,1)S(1)} %copy-done.4, bf16[8,128,512]{2,1,0:T(8,128)(2,1)} %collective-permute-done.3.other_ref, bf16[8,1024,128]{2,1,0:T(8,128)(2,1)S(1)} %bitcast.25, bf16[8,1024,128]{2,1,0:T(8,128)(2,1)S(1)} %bitcast.26, bf16[128,128]{1,0:T(8,128)(2,1)S(1)} %copy-done.9), custom_call_target="tpu_custom_call" | custom-call | flops 1 | bytes 1 | tf_op jit(solution)/shard_map/rotor_grad/pallas_call | solution.py:302
  113.4 22.0 %all-to-all-done.3 = bf16[8,512,128]{2,1,0:T(8,128)(2,1)} async-done(((bf16[8,512,128]{2,1,0:T(8,128)(2,1)}), bf16[8,512,128]{2,1,0:T(8,128)(2,1)}, u32[]{:S(2)}, u32[]{:S(2)}) %all-to-all-start.3) | async-done | bytes 1048608 | tf_op jit(solution)/shard_map/all_to_all | solution.py:359
  135.3 1.4 convert_reduce_fusion
  136.8 1.9 %collective-permute-start.4 = (bf16[512,128]{1,0:T(8,128)(2,1)S(1)}, bf16[512,128]{1,0:T(8,128)(2,1)S(1)}, u32[]{:S(2)}, u32[]{:S(2)}) collective-permute-start(bf16[512,128]{1,0:T(8,128)(2,1)S(1)} %fusion.4), channel_id=1, source_target_pairs={{0,8},{8,0},{1,9},{9,1},{2,10},{10,2},{3,11},{11,3},{4,12},{12,4},... | collective-permute-start | bytes 393224 | tf_op jit(solution)/shard_map/ppermute | solution.py:364
  138.7 0.0 collective-permute-done.1
  138.7 0.0 reduce-scatter.2.cloned.1.call-done
  138.7 2.0 %fusion.2 = bf16[128,1024]{1,0:T(8,128)(2,1)} fusion(bf16[128,1024]{1,0:T(8,128)(2,1)S(1)} %copy-done.6, bf16[128,1024]{1,0:T(8,128)(2,1)} %collective-permute-done.1, bf16[1,128,1024]{2,1,0:T(8,128)(2,1)} %reduce-scatter.2.cloned.1.call-done, f32[1024]{0:T(1024)S(1)} %bitcast.34, f32[128]{0:T(128)S(1)} %bitcast.29, pred[1024]{0:T(1024)(128)(4,1)S(1)} %compare_reduce_fusion), kind=kLoop, calls=%fused_computation.4 | loop fusion | flops 1572864 | bytes 1054208 | tf_op jit(solution)/shard_map/convert_element_type | solution.py:419
  140.8 9.7 %collective-permute-done.4 = bf16[512,128]{1,0:T(8,128)(2,1)S(1)} collective-permute-done((bf16[512,128]{1,0:T(8,128)(2,1)S(1)}, bf16[512,128]{1,0:T(8,128)(2,1)S(1)}, u32[]{:S(2)}, u32[]{:S(2)}) %collective-permute-start.4) | collective-permute-done | bytes 131104 | tf_op jit(solution)/shard_map/ppermute | solution.py:364
  150.5 0.7 fusion.3
  (10 shorter events, 0.1 us)
Async XLA Ops:
  7.2 8.9 %copy-start.6 = (bf16[128,1024]{1,0:T(8,128)(2,1)S(1)}, bf16[128,1024]{1,0:T(8,128)(2,1)}, u32[]{:S(2)}) copy-start(bf16[128,1024]{1,0:T(8,128)(2,1)} %x_ref.3) | copy-start | bytes 786436
  7.2 8.9 %copy-start.10 = (f32[1,1024]{1,0:T(1,128)S(1)}, f32[1,1024]{1,0:T(1,128)}, u32[]{:S(2)}) copy-start(f32[1,1024]{1,0:T(1,128)} %scale_ref.1) | copy-start | bytes 12292
  7.2 51.5 %all-gather.3.cloned.1.call-start = ((), (), s32[]{:S(2)}) async-start(), calls=%async_computation.6 | async-start | bytes 1474560 | tf_op jit(solution)/shard_map/all_gather | solution.py:383
  7.8 10.1 %copy-start = (bf16[8192,128]{1,0:T(8,128)(2,1)S(1)}, bf16[8192,128]{1,0:T(8,128)(2,1)}, u32[]{:S(2)}) copy-start(bf16[8192,128]{1,0:T(8,128)(2,1)} %w_ref.7) | copy-start | bytes 6291460
  7.8 10.1 %copy-start.8 = (bf16[128,128]{1,0:T(8,128)(2,1)S(1)}, bf16[128,128]{1,0:T(8,128)(2,1)}, u32[]{:S(2)}) copy-start(bf16[128,128]{1,0:T(8,128)(2,1)} %r2_ref.5) | copy-start | bytes 98308
  7.8 10.1 %copy-start.9 = (bf16[128,128]{1,0:T(8,128)(2,1)S(1)}, bf16[128,128]{1,0:T(8,128)(2,1)}, u32[]{:S(2)}) copy-start(bf16[128,128]{1,0:T(8,128)(2,1)} %dv_ref.7) | copy-start | bytes 98308
  7.8 10.1 %copy-start.11 = (s32[2]{0:T(128)S(1)}, s32[2]{0:T(128)}, u32[]{:S(2)}) copy-start(s32[2]{0:T(128)} %pad_add_fusion.core_ref.place_ref) | copy-start | bytes 28
  11.7 4.4 %collective-permute-start = (bf16[2320,128]{1,0:T(8,128)(2,1)}, bf16[2320,128]{1,0:T(8,128)(2,1)S(1)}, u32[]{:S(2)}, u32[]{:S(2)}) collective-permute-start(bf16[2320,128]{1,0:T(8,128)(2,1)} %core_inputs.1.mine_ref), channel_id=1, source_target_pairs={{0,1},{1,0},{2,3},{3,2},{4,5},{5,4},{6,7},{7,6},{8,9},{9,8},{10,11... | collective-permute-start | bytes 1781768 | tf_op jit(solution)/shard_map/ppermute | solution.py:364
  16.1 1.1 copy-start.5
  20.2 0.8 copy-start.7
  21.1 15.8 %all-to-all-start = ((bf16[4,128,512]{2,1,0:T(8,128)(2,1)}), bf16[4,128,512]{2,1,0:T(8,128)(2,1)S(1)}, u32[]{:S(2)}, u32[]{:S(2)}) async-start(bf16[4,128,512]{2,1,0:T(8,128)(2,1)} %copy-done.7), calls=%async_computation | async-start | bytes 1048576 | tf_op jit(solution)/shard_map/all_to_all | solution.py:359
  32.3 1.3 copy-start.2
  33.6 10.2 %copy-start.13 = (s32[1,128]{1,0:T(1,128)S(1)}, s32[1,128]{1,0:T(1,128)}, u32[]{:S(2)}) copy-start(s32[1,128]{1,0:T(1,128)} %param.13) | copy-start | bytes 1540
  38.0 25.6 %all-to-all-start.1 = ((bf16[8,128,512]{2,1,0:T(8,128)(2,1)}), bf16[8,128,512]{2,1,0:T(8,128)(2,1)S(1)}, u32[]{:S(2)}, u32[]{:S(2)}) async-start(bf16[8,128,512]{2,1,0:T(8,128)(2,1)} %broadcast_in_dim.20), calls=%async_computation.1 | async-start | bytes 2097152 | tf_op jit(solution)/shard_map/all_to_all | solution.py:359
  58.7 1.3 copy-start.12
  62.6 1.0 copy-start.3
  63.6 21.0 %all-to-all-start.2 = ((bf16[8,128,512]{2,1,0:T(8,128)(2,1)}), bf16[8,128,512]{2,1,0:T(8,128)(2,1)}, u32[]{:S(2)}, u32[]{:S(2)}) async-start(bf16[8,128,512]{2,1,0:T(8,128)(2,1)} %copy-done.3), calls=%async_computation.2 | async-start | bytes 2097152 | tf_op jit(solution)/shard_map/all_to_all | solution.py:359
  69.4 69.3 %reduce-scatter.2.cloned.1.call-start = ((), (), s32[]{:S(2)}) async-start(), calls=%async_computation.5 | async-start | bytes 2359296 | tf_op jit(solution)/shard_map/reduce_scatter | solution.py:400
  84.6 6.2 %collective-permute-start.2 = (bf16[8,128,512]{2,1,0:T(8,128)(2,1)}, bf16[8,128,512]{2,1,0:T(8,128)(2,1)}, u32[]{:S(2)}, u32[]{:S(2)}) collective-permute-start(bf16[8,128,512]{2,1,0:T(8,128)(2,1)} %all-to-all-done.2), channel_id=1, source_target_pairs={{0,1},{1,0},{2,3},{3,2},{4,5},{5,4},{6,7},{7,6},{8,9},{9,8},{10,11... | collective-permute-start | bytes 3145736 | tf_op jit(solution)/shard_map/ppermute | solution.py:364
  93.4 1.0 copy-start.1
  94.4 9.3 %copy-start.4 = (bf16[8,128,512]{2,1,0:T(8,128)(2,1)S(1)}, bf16[8,128,512]{2,1,0:T(8,128)(2,1)}, u32[]{:S(2)}) copy-start(bf16[8,128,512]{2,1,0:T(8,128)(2,1)} %copy-done.3) | copy-start | bytes 3145732
  94.4 40.9 %all-to-all-start.3 = ((bf16[8,512,128]{2,1,0:T(8,128)(2,1)}), bf16[8,512,128]{2,1,0:T(8,128)(2,1)}, u32[]{:S(2)}, u32[]{:S(2)}) async-start(bf16[8,512,128]{2,1,0:T(8,128)(2,1)} %copy-done.1), calls=%async_computation.4 | async-start | bytes 2097152 | tf_op jit(solution)/shard_map/all_to_all | solution.py:359
  103.7 5.4 %collective-permute-start.3 = (bf16[8,128,512]{2,1,0:T(8,128)(2,1)S(1)}, bf16[8,128,512]{2,1,0:T(8,128)(2,1)}, u32[]{:S(2)}, u32[]{:S(2)}) collective-permute-start(bf16[8,128,512]{2,1,0:T(8,128)(2,1)S(1)} %copy-done.4), channel_id=1, source_target_pairs={{0,1},{1,0},{2,3},{3,2},{4,5},{5,4},{6,7},{7,6},{8,9},{9,8},{10,11... | collective-permute-start | bytes 3145736 | tf_op jit(solution)/shard_map/ppermute | solution.py:364
  106.2 32.5 %collective-permute-start.1 = (bf16[128,1024]{1,0:T(8,128)(2,1)}, bf16[128,1024]{1,0:T(8,128)(2,1)}, u32[]{:S(2)}, u32[]{:S(2)}) collective-permute-start(bf16[128,1024]{1,0:T(8,128)(2,1)} %param.8), channel_id=1, source_target_pairs={{0,504},{8,0},{16,8},{24,16},{32,24},{40,32},{48,40},{56,48},{64,5... | collective-permute-start | bytes 786440 | tf_op jit(solution)/shard_map/ppermute | solution.py:406
  136.8 13.7 %collective-permute-start.4 = (bf16[512,128]{1,0:T(8,128)(2,1)S(1)}, bf16[512,128]{1,0:T(8,128)(2,1)S(1)}, u32[]{:S(2)}, u32[]{:S(2)}) collective-permute-start(bf16[512,128]{1,0:T(8,128)(2,1)S(1)} %fusion.4), channel_id=1, source_target_pairs={{0,8},{8,0},{1,9},{9,1},{2,10},{10,2},{3,11},{11,3},{4,12},{12,4},... | collective-permute-start | bytes 393224 | tf_op jit(solution)/shard_map/ppermute | solution.py:364
Sparse Core Ops, SparseCore 0:
  18.1 40.6 all-gather.2
  73.1 49.0 reduce-scatter.1

commit v8 on v7

--- a/solution.py
+++ b/solution.py
@@ -100,33 +100,6 @@
     )(core, hidden, weight, rotor, value_grad)
 
 
-def pack_kernel(x_ref, scale_ref, mine_ref, other_ref, out_ref):
-    terms = mine_ref[...].astype(jnp.float32), other_ref[...].astype(jnp.float32)
-    sums = [term[0:1] + term[1:2] + term[2:3] for term in terms]
-    squares = jnp.concatenate([sums[0] + sums[1], jnp.zeros((1, 896), jnp.float32)], axis=1)
-    out_ref[0:128, :] = x_ref[...]
-    out_ref[128:144, :] = in_rows(three_terms(scale_ref[...]) + three_terms(squares), 1024)
-
-
-def pack(hidden, scale, mine, other):
-    whole = lambda i: (0, 0)
-    return pl.pallas_call(
-        pack_kernel,
-        grid=(1,),
-        in_specs=[
-            pl.BlockSpec((128, 1024), whole),
-            pl.BlockSpec((1, 1024), whole),
-            pl.BlockSpec((16, 128), lambda i: (144, 0)),
-            pl.BlockSpec((16, 128), lambda i: (144, 0)),
-        ],
-        out_specs=pl.BlockSpec((144, 1024), whole),
-        out_shape=jax.ShapeDtypeStruct((144, 1024), jnp.bfloat16),
-        compiler_params=pltpu.CompilerParams(vmem_limit_bytes=BIG),
-        cost_estimate=CHEAP,
-        name="pack",
-    )(hidden, scale, mine, other)
-
-
 def rotated_rows(w_ref, r2_ref):
     rot = jnp.dot(w_ref[...], r2_ref[...], preferred_element_type=jnp.float32)
     return rot.astype(jnp.bfloat16)
@@ -145,14 +118,23 @@
         top_ref[...] = jnp.maximum(top_ref[...], top)
 
 
-def frame_kernel(core_ref, w_ref, r2_ref, dv_ref, w2_ref, r22_ref, dv2_ref, out_ref):
+def frame_kernel(
+    core_ref, w_ref, r2_ref, dv_ref, w2_ref, r22_ref, dv2_ref, scale_ref, sq_ref, sq2_ref, out_ref
+):
     mine = dot_nt(dv_ref[...], rotated_rows(w_ref, r2_ref))
     other = dot_nt(dv2_ref[...], rotated_rows(w2_ref, r22_ref))
-    out_ref[0] = (mine + other).astype(jnp.bfloat16)
-
-
-def frame_pairs(core, weight, rotor, value_grad, received):
+    out_ref[0, 0:128, :] = (mine + other).astype(jnp.bfloat16)
+    squares = sq_ref[...].astype(jnp.float32), sq2_ref[...].astype(jnp.float32)
+    squares = [term[0:1] + term[1:2] + term[2:3] for term in squares]
+    squares = jnp.concatenate([squares[0] + squares[1], jnp.zeros((1, 384), jnp.float32)], axis=1)
+    scale = scale_ref[...]
+    terms = three_terms(scale[:, :512]) + three_terms(scale[:, 512:]) + three_terms(squares)
+    out_ref[0, 128:144, :] = in_rows(terms, 512)
+
+
+def frame_pairs(core, weight, rotor, value_grad, scale, inputs, received):
     whole = pl.BlockSpec((128, 128), lambda i, core: (0, 0))
+    sums = pl.BlockSpec((16, 128), lambda i, core: (144, 0))
     return pl.pallas_call(
         frame_kernel,
         grid_spec=pltpu.PrefetchScalarGridSpec(
@@ -165,14 +147,17 @@
                 pl.BlockSpec((512, 128), lambda i, core: (i, 0)),
                 pl.BlockSpec((128, 128), lambda i, core: (16, 0)),
                 pl.BlockSpec((128, 128), lambda i, core: (17, 0)),
+                pl.BlockSpec((1, 1024), lambda i, core: (0, 0)),
+                sums,
+                sums,
             ],
-            out_specs=pl.BlockSpec((1, 128, 512), lambda i, core: (i, 0, 0)),
+            out_specs=pl.BlockSpec((1, 144, 512), lambda i, core: (i, 0, 0)),
         ),
-        out_shape=jax.ShapeDtypeStruct((4, 128, 512), jnp.bfloat16),
+        out_shape=jax.ShapeDtypeStruct((4, 144, 512), jnp.bfloat16),
         compiler_params=pltpu.CompilerParams(vmem_limit_bytes=BIG),
         cost_estimate=LONG,
         name="frame_pairs",
-    )(core, weight, rotor, value_grad, received, received, received)
+    )(core, weight, rotor, value_grad, received, received, received, scale, inputs, received)
 
 
 def top_kernel(w_ref, r2_ref, top_ref):
@@ -217,15 +202,17 @@
     )(weight, rotor, top, value_grad)
 
 
-def quant_kernel(core_ref, all_ref, sum_ref, mask_ref, quant_ref, inv_ref):
-    squares = jnp.sum(sum_ref[...].astype(jnp.float32), axis=0)
-    squares = squares[3:4] + squares[4:5] + squares[5:6]
+def quant_kernel(core_ref, all_ref, term_ref, sum_ref, mask_ref, quant_ref, inv_ref):
+    squares = jnp.sum(sum_ref[:, :, 0:128].astype(jnp.float32), axis=0)
+    squares = squares[6:7] + squares[7:8] + squares[8:9]
     inverse = lax.rsqrt(squares / 8192.0 + NORM_EPS)
     inv_ref[...] = inverse
     inverse = jnp.transpose(jnp.broadcast_to(inverse, (128, 128)))
     mask = mask_ref[0]
-    scale = all_ref[0, 128:144, :].astype(jnp.float32)
-    scale = scale[0:1] + scale[1:2] + scale[2:3]
+    terms = term_ref[0].astype(jnp.float32)
+    scale = jnp.concatenate(
+        [terms[0:1] + terms[1:2] + terms[2:3], terms[3:4] + terms[4:5] + terms[5:6]], axis=1
+    )
     recip = 1.0 / scale
     scale7 = scale * 7.0
     for lane in range(8):
@@ -238,15 +225,16 @@
         quant_ref[zl, :, place * 128 : (place + 1) * 128] = quant
 
 
-def quantize(core, hidden_all, mask):
+def quantize(core, hidden_all, terms, mask):
     return pl.pallas_call(
         quant_kernel,
         grid_spec=pltpu.PrefetchScalarGridSpec(
             num_scalar_prefetch=1,
             grid=(4,),
             in_specs=[
-                pl.BlockSpec((1, 144, 1024), lambda i, core: (i, 0, 0)),
-                pl.BlockSpec((4, 16, 128), lambda i, core: (0, 8, 0)),
+                pl.BlockSpec((1, 128, 1024), lambda i, core: (i, 0, 0)),
+                pl.BlockSpec((1, 16, 512), lambda i, core: (i, 8, 0)),
+                pl.BlockSpec((4, 16, 512), lambda i, core: (0, 8, 0)),
                 pl.BlockSpec((1, 1, 1024), lambda i, core: (i * 2 + core[0], 0, 0)),
             ],
             out_specs=[
@@ -259,9 +247,9 @@
             jax.ShapeDtypeStruct((1, 128), jnp.float32),
         ],
         compiler_params=pltpu.CompilerParams(vmem_limit_bytes=BIG),
-        cost_estimate=pl.CostEstimate(flops=10_350_000_000, bytes_accessed=1, transcendentals=0),
+        cost_estimate=pl.CostEstimate(flops=17_250_000_000, bytes_accessed=1, transcendentals=0),
         name="quantize",
-    )(core, hidden_all, hidden_all, mask)
+    )(core, hidden_all, terms, terms, mask)
 
 
 def rotor_grad_kernel(core_ref, mine_ref, other_ref, wm_ref, wo_ref, dv_ref, r2_ref, total_ref):
@@ -329,8 +317,9 @@
         (((0,), (0,)), ((), ())),
         preferred_element_type=jnp.float32,
     ).astype(jnp.bfloat16)
-    for part in range(2):
-        out_ref[(part + yh) % 2] = prod[:, part * 128 : (part + 1) * 128]
+    for part in range(4):
+        place = part // 2 * 2 + (part + yh) % 2
+        out_ref[place] = prod[:, part * 128 : (part + 1) * 128]
 
 
 def outer(place, frames, quants, into, name):
@@ -339,13 +328,13 @@
         outer_kernel,
         grid_spec=pltpu.PrefetchScalarGridSpec(
             num_scalar_prefetch=1,
-            grid=(2,),
+            grid=(1,),
             in_specs=[
                 pl.BlockSpec((1024, 512), lambda i, place: (0, 0)),
-                pl.BlockSpec((1024, 256), lambda i, place: (0, i)),
+                pl.BlockSpec((1024, 512), lambda i, place: (0, 0)),
             ]
             + [pl.BlockSpec(memory_space=pl.ANY)] * len(more),
-            out_specs=pl.BlockSpec((2, 512, 128), lambda i, place: (place[0] * 2 + i, 0, 0)),
+            out_specs=pl.BlockSpec((4, 512, 128), lambda i, place: (place[0], 0, 0)),
         ),
         out_shape=jax.ShapeDtypeStruct((8, 512, 128), jnp.bfloat16),
         input_output_aliases={3: 0} if more else {},
@@ -377,18 +366,19 @@
     wide = lambda value: value.astype(jnp.float32)
     tie = lax.optimization_barrier
 
+    hidden_all = lax.all_gather(hidden_in, "yl", axis=0)
+
     inputs = core_inputs(place, hidden_in, value_weight, rotation, value_grad)
     received = swap_core(inputs)
-    packed = pack(hidden_in, act_scale, inputs, received)
-    hidden_all = lax.all_gather(packed, "yl", axis=0)
-
-    frame_pair = frame_pairs(place, value_weight, rotation, value_grad, received)
+    frame_pair = frame_pairs(
+        place, value_weight, rotation, value_grad, act_scale, inputs, received
+    )
     frame_pair, rotor = tie((frame_pair, rotation))
     frame_terms = exchange(frame_pair, "yl")
     top = rotated_top(value_weight, rotor)
     grad_parts = weight_grad(value_weight, rotor, top, value_grad)
     frame_terms, grad_parts = tie((frame_terms, grad_parts))
-    frame = jnp.sum(wide(frame_terms), axis=0).astype(jnp.bfloat16)
+    frame = jnp.sum(wide(frame_terms[:, :128]), axis=0).astype(jnp.bfloat16)
     frames = exchange(jnp.broadcast_to(frame[None], (8, 128, 512)), NEAR).reshape(1024, 512)
 
     ids = outliers[0]
@@ -398,7 +388,7 @@
 
     hidden_all, mask, grad_parts = tie((hidden_all, mask, grad_parts))
     grad_sum = lax.psum_scatter(grad_parts, TPA, scatter_dimension=0, tiled=False)
-    quant, inverse = quantize(place, hidden_all, mask)
+    quant, inverse = quantize(place, hidden_all, frame_terms, mask)
     frames, quant = tie((frames, quant))
     quants = exchange(quant, NEAR)
     quants, quant, grad_sent = tie((quants, quant, grad_sent))

time: 159 us -> 165 us (1.038)
  the two profiles are of different devices: /device:TPU:41 before, /device:TPU:1 now
where the time goes in v8:
time: 165 us; the launch traced here: 164 us
  starting transfers between devices  62.5 us (38%)
  waiting for transfers between devices  47.3 us (29%)
  Pallas kernels  27 us (16%)
  between operations  14.3 us (9%)
  local copies, waits for them, and re-layouts  7.8 us (5%)
  other arithmetic  4.97 us (3%)
    all_to_all x4, waiting for transfers between devices, exchange(): return lax.all_to_all(value, axes, split_axis=0, concat_axis=0, tiled=True)  40.4 us
    ppermute x4, starting transfers between devices, shifted(): lax.ppermute(value, axis, [(chip, (chip + turn) % count) for chip in rang...  33.4 us
    all_to_all x4, starting transfers between devices, exchange(): return lax.all_to_all(value, axes, split_axis=0, concat_axis=0, tiled=True)  18.8 us
    ppermute x1, starting transfers between devices, local(): incoming = lax.ppermute(grad_sent, SEC, pairs)  10.1 us
    unnamed x30, local copies, waits for them, and re-layouts  6.66 us
    ppermute x4, waiting for transfers between devices, shifted(): lax.ppermute(value, axis, [(chip, (chip + turn) % count) for chip in rang...  5.79 us
    pallas_call x1, Pallas kernels, weight_grad(): pl.pallas_call(weight_grad_kernel, grid=(8,), in_specs=[pl.BlockSpec((102...  5.35 us
    pallas_call x2, Pallas kernels, outer(): pl.pallas_call(outer_kernel, grid_spec=pltpu.PrefetchScalarGridSpec(num_s...  5.05 us
  transfers between devices with their start and end apart: 11, of which 7 were waited for; matrix products, arithmetic and copies ran while one was open for 3% of the time, Pallas kernels for 14%

profile of v8, /device:TPU:1, one launch (start us, length us, event | category | flops | bytes accessed | tf_op | source)
XLA Modules:
  0.0 164.1 jit_solution(1815144255806876018)
XLA Ops:
  7.2 0.0 copy-start
  7.2 0.0 copy-start.9
  7.2 0.0 copy-start.8
  7.2 0.0 copy-start.11
  7.2 0.0 all-gather.3.cloned.1.call-start
  7.3 0.6 pad_add_fusion.core_ref.place_ref
  7.9 3.8 %core_inputs.1.sq_ref = bf16[2320,128]{1,0:T(8,128)(2,1)} custom-call(s32[2]{0:T(128)} %pad_add_fusion.core_ref.place_ref, bf16[128,1024]{1,0:T(8,128)(2,1)} %x_ref.1, bf16[8192,128]{1,0:T(8,128)(2,1)} %w_ref.7, bf16[128,128]{1,0:T(8,128)(2,1)} %r2_ref.5, bf16[128,128]{1,0:T(8,128)(2,1)} %dv_ref.7), custom_call_target="tpu_custom_call" | custom-call | flops 1 | bytes 1 | tf_op jit(solution)/shard_map/core_inputs/pallas_call | solution.py:83
  11.7 8.8 %collective-permute-start = (bf16[2320,128]{1,0:T(8,128)(2,1)}, bf16[2320,128]{1,0:T(8,128)(2,1)}, u32[]{:S(2)}, u32[]{:S(2)}) collective-permute-start(bf16[2320,128]{1,0:T(8,128)(2,1)} %core_inputs.1.sq_ref), channel_id=1, source_target_pairs={{0,1},{1,0},{2,3},{3,2},{4,5},{5,4},{6,7},{7,6},{8,9},{9,8},{10,11... | collective-permute-start | bytes 1781768 | tf_op jit(solution)/shard_map/ppermute | solution.py:353
  20.5 0.0 all-gather.3.cloned.1.call-update
  20.5 1.9 %collective-permute-done.w2_ref.r22_ref.dv2_ref.sq2_ref = bf16[2320,128]{1,0:T(8,128)(2,1)} collective-permute-done((bf16[2320,128]{1,0:T(8,128)(2,1)}, bf16[2320,128]{1,0:T(8,128)(2,1)}, u32[]{:S(2)}, u32[]{:S(2)}) %collective-permute-start) | collective-permute-done | bytes 593952 | tf_op jit(solution)/shard_map/ppermute | solution.py:353
  22.4 0.0 copy-done
  22.4 0.0 copy-done.9
  22.4 0.0 copy-done.8
  22.4 0.0 copy-done.11
  22.4 0.0 copy-done.10
  22.4 0.0 copy-start.7
  22.5 1.1 copy-done.7
  23.5 4.5 %frame_pairs.1 = bf16[4,144,512]{2,1,0:T(8,128)(2,1)} custom-call(s32[2]{0:T(128)S(1)} %copy-done.10, bf16[8192,128]{1,0:T(8,128)(2,1)S(1)} %copy-done, bf16[128,128]{1,0:T(8,128)(2,1)S(1)} %copy-done.8, bf16[128,128]{1,0:T(8,128)(2,1)S(1)} %copy-done.9, bf16[2320,128]{1,0:T(8,128)(2,1)} %collective-permute-done.w2_ref.r22_ref.dv2_ref.sq2_ref, ...), custom_call_target="tpu_custom_call" | custom-call | flops 23000000512 | bytes 1 | tf_op jit(solution)/shard_map/frame_pairs/pallas_call | solution.py:138
  28.1 3.5 %all-to-all-start = ((bf16[4,144,512]{2,1,0:T(8,128)(2,1)}), bf16[4,144,512]{2,1,0:T(8,128)(2,1)S(1)}, u32[]{:S(2)}, u32[]{:S(2)}) async-start(bf16[4,144,512]{2,1,0:T(8,128)(2,1)} %frame_pairs.1), calls=%async_computation | async-start | bytes 1179648 | tf_op jit(solution)/shard_map/all_to_all | solution.py:348
  31.5 0.0 copy-done.14
  31.6 1.3 rotated_top.1.top_ref
  32.9 5.3 %weight_grad.1 = bf16[8,128,1024]{2,1,0:T(8,128)(2,1)S(1)} custom-call(bf16[8192,128]{1,0:T(8,128)(2,1)S(1)} %copy-done, bf16[128,128]{1,0:T(8,128)(2,1)S(1)} %copy-done.8, f32[1,128]{1,0:T(1,128)S(1)} %rotated_top.1.top_ref, bf16[128,128]{1,0:T(8,128)(2,1)S(1)} %copy-done.9), custom_call_target="tpu_custom_call" | custom-call | flops 1 | bytes 1 | tf_op jit(solution)/shard_map/weight_grad/pallas_call | solution.py:193
  38.3 0.0 copy-start.2
  38.3 1.3 copy-done.2
  39.6 18.3 %all-to-all-done.term_ref.sum_ref = bf16[4,144,512]{2,1,0:T(8,128)(2,1)S(1)} async-done(((bf16[4,144,512]{2,1,0:T(8,128)(2,1)}), bf16[4,144,512]{2,1,0:T(8,128)(2,1)S(1)}, u32[]{:S(2)}, u32[]{:S(2)}) %all-to-all-start) | async-done | bytes 589856 | tf_op jit(solution)/shard_map/all_to_all | solution.py:348
  57.9 0.1 slice_reduce_fusion
  58.0 1.1 broadcast_in_dim.20
  59.1 0.0 copy-done.5
  59.1 3.6 %all-to-all-start.1 = ((bf16[8,128,512]{2,1,0:T(8,128)(2,1)}), bf16[8,128,512]{2,1,0:T(8,128)(2,1)S(1)}, u32[]{:S(2)}, u32[]{:S(2)}) async-start(bf16[8,128,512]{2,1,0:T(8,128)(2,1)} %broadcast_in_dim.20), calls=%async_computation.1 | async-start | bytes 2097152 | tf_op jit(solution)/shard_map/all_to_all | solution.py:348
  62.7 0.2 fusion.5
  62.9 0.4 all-gather.3.cloned.1.call-done
  63.3 1.1 copy-done.6
  64.4 1.2 copy-done.12
  65.6 2.6 %quantize.1 = (bf16[8,128,512]{2,1,0:T(8,128)(2,1)S(1)}, f32[1,128]{1,0:T(1,128)S(1)}) custom-call(s32[2]{0:T(128)S(1)} %copy-done.10, bf16[4,128,1024]{2,1,0:T(8,128)(2,1)S(1)} %bitcast.32, bf16[4,144,512]{2,1,0:T(8,128)(2,1)S(1)} %copy-done.6, bf16[4,144,512]{2,1,0:T(8,128)(2,1)S(1)} %copy-done.6, f32[8,1,1024]{2,1,0:T(1,128)S(1)} %bitcast.30), custom_call_target="tpu_custom_call" | custom-call | flops 17250000896 | bytes 1 | tf_op jit(solution)/shard_map/quantize/pallas_call | solution.py:229
  68.2 0.0 copy-start.3
  68.2 1.0 copy-done.3
  69.2 4.4 %all-to-all-done.1 = bf16[8,128,512]{2,1,0:T(8,128)(2,1)S(1)} async-done(((bf16[8,128,512]{2,1,0:T(8,128)(2,1)}), bf16[8,128,512]{2,1,0:T(8,128)(2,1)S(1)}, u32[]{:S(2)}, u32[]{:S(2)}) %all-to-all-start.1) | async-done | bytes 1048608 | tf_op jit(solution)/shard_map/all_to_all | solution.py:348
  73.5 4.2 %all-to-all-start.2 = ((bf16[8,128,512]{2,1,0:T(8,128)(2,1)}), bf16[8,128,512]{2,1,0:T(8,128)(2,1)}, u32[]{:S(2)}, u32[]{:S(2)}) async-start(bf16[8,128,512]{2,1,0:T(8,128)(2,1)} %copy-done.3), calls=%async_computation.2 | async-start | bytes 2097152 | tf_op jit(solution)/shard_map/all_to_all | solution.py:348
  77.8 0.0 reduce-scatter.2.cloned.1.call-start
  77.8 0.7 reduce-scatter.2.cloned.1.call-update
  78.5 9.7 %all-to-all-done.2 = bf16[8,128,512]{2,1,0:T(8,128)(2,1)} async-done(((bf16[8,128,512]{2,1,0:T(8,128)(2,1)}), bf16[8,128,512]{2,1,0:T(8,128)(2,1)}, u32[]{:S(2)}, u32[]{:S(2)}) %all-to-all-start.2) | async-done | bytes 1048608 | tf_op jit(solution)/shard_map/all_to_all | solution.py:348
  88.2 9.0 %collective-permute-start.2 = (bf16[8,128,512]{2,1,0:T(8,128)(2,1)}, bf16[8,128,512]{2,1,0:T(8,128)(2,1)}, u32[]{:S(2)}, u32[]{:S(2)}) collective-permute-start(bf16[8,128,512]{2,1,0:T(8,128)(2,1)} %all-to-all-done.2), channel_id=1, source_target_pairs={{0,1},{1,0},{2,3},{3,2},{4,5},{5,4},{6,7},{7,6},{8,9},{9,8},{10,11... | collective-permute-start | bytes 3145736 | tf_op jit(solution)/shard_map/ppermute | solution.py:353
  97.3 0.1 pad_add_fusion.1.place_ref
  97.3 2.5 %outer.1.rest_0_ = bf16[8,512,128]{2,1,0:T(8,128)(2,1)S(1)} custom-call(s32[2]{0:T(128)S(1)} %copy-done.10, bf16[1024,512]{1,0:T(8,128)(2,1)S(1)} %bitcast.27, bf16[1024,512]{1,0:T(8,128)(2,1)} %bitcast.12.quant_ref), custom_call_target="tpu_custom_call" | custom-call | flops 1 | bytes 1 | tf_op jit(solution)/shard_map/outer/pallas_call | solution.py:327
  99.9 0.0 collective-permute-done.2
  99.9 2.5 %outer_other.1 = bf16[8,512,128]{2,1,0:T(8,128)(2,1)S(1)} custom-call(s32[2]{0:T(128)S(1)} %pad_add_fusion.1.place_ref, bf16[1024,512]{1,0:T(8,128)(2,1)S(1)} %bitcast.28, bf16[1024,512]{1,0:T(8,128)(2,1)} %bitcast.11.quant_ref, bf16[8,512,128]{2,1,0:T(8,128)(2,1)S(1)} %outer.1.rest_0_), custom_call_target="tpu_custom_call", output_to_operand_aliasing={{}: (3, {})} | custom-call | flops 1 | bytes 1 | tf_op jit(solution)/shard_map/outer_other/pallas_call | solution.py:327
  102.4 0.0 copy-start.1
  102.4 1.0 copy-done.1
  103.4 7.5 %all-to-all-start.3 = ((bf16[8,512,128]{2,1,0:T(8,128)(2,1)}), bf16[8,512,128]{2,1,0:T(8,128)(2,1)}, u32[]{:S(2)}, u32[]{:S(2)}) async-start(bf16[8,512,128]{2,1,0:T(8,128)(2,1)} %copy-done.1), calls=%async_computation.4 | async-start | bytes 2097152 | tf_op jit(solution)/shard_map/all_to_all | solution.py:348
  110.9 0.0 copy-done.4
  111.0 2.5 %collective-permute-start.3 = (bf16[8,128,512]{2,1,0:T(8,128)(2,1)S(1)}, bf16[8,128,512]{2,1,0:T(8,128)(2,1)}, u32[]{:S(2)}, u32[]{:S(2)}) collective-permute-start(bf16[8,128,512]{2,1,0:T(8,128)(2,1)S(1)} %copy-done.4), channel_id=1, source_target_pairs={{0,1},{1,0},{2,3},{3,2},{4,5},{5,4},{6,7},{7,6},{8,9},{9,8},{10,11... | collective-permute-start | bytes 3145736 | tf_op jit(solution)/shard_map/ppermute | solution.py:353
  113.5 10.1 %collective-permute-start.1 = (bf16[128,1024]{1,0:T(8,128)(2,1)}, bf16[128,1024]{1,0:T(8,128)(2,1)}, u32[]{:S(2)}, u32[]{:S(2)}) collective-permute-start(bf16[128,1024]{1,0:T(8,128)(2,1)} %param.8), channel_id=1, source_target_pairs={{0,504},{8,0},{16,8},{24,16},{32,24},{40,32},{48,40},{56,48},{64,5... | collective-permute-start | bytes 786440 | tf_op jit(solution)/shard_map/ppermute | solution.py:396
  123.7 0.0 collective-permute-done.3.other_ref
  123.7 0.0 copy-start.13
  123.7 4.3 %rotor_grad.1 = f32[128,128]{1,0:T(8,128)} custom-call(s32[2]{0:T(128)S(1)} %copy-done.10, bf16[8,128,512]{2,1,0:T(8,128)(2,1)S(1)} %copy-done.4, bf16[8,128,512]{2,1,0:T(8,128)(2,1)} %collective-permute-done.3.other_ref, bf16[8,1024,128]{2,1,0:T(8,128)(2,1)S(1)} %bitcast.25, bf16[8,1024,128]{2,1,0:T(8,128)(2,1)S(1)} %bitcast.26, bf16[128,128]{1,0:T(8,128)(2,1)S(1)} %copy-done.9), custom_call_target="tpu_custom_call" | custom-call | flops 1 | bytes 1 | tf_op jit(solution)/shard_map/rotor_grad/pallas_call | solution.py:290
  128.0 8.0 %all-to-all-done.3 = bf16[8,512,128]{2,1,0:T(8,128)(2,1)} async-done(((bf16[8,512,128]{2,1,0:T(8,128)(2,1)}), bf16[8,512,128]{2,1,0:T(8,128)(2,1)}, u32[]{:S(2)}, u32[]{:S(2)}) %all-to-all-start.3) | async-done | bytes 1048608 | tf_op jit(solution)/shard_map/all_to_all | solution.py:348
  136.0 1.4 convert_reduce_fusion
  137.5 13.1 %collective-permute-start.4 = (bf16[512,128]{1,0:T(8,128)(2,1)S(1)}, bf16[512,128]{1,0:T(8,128)(2,1)S(1)}, u32[]{:S(2)}, u32[]{:S(2)}) collective-permute-start(bf16[512,128]{1,0:T(8,128)(2,1)S(1)} %fusion.4), channel_id=1, source_target_pairs={{0,8},{8,0},{1,9},{9,1},{2,10},{10,2},{3,11},{11,3},{4,12},{12,4},... | collective-permute-start | bytes 393224 | tf_op jit(solution)/shard_map/ppermute | solution.py:353
  150.6 0.0 collective-permute-done.1
  150.6 0.0 reduce-scatter.2.cloned.1.call-done
  150.6 0.0 copy-done.13
  150.6 2.0 %fusion.2 = bf16[128,1024]{1,0:T(8,128)(2,1)} fusion(bf16[128,1024]{1,0:T(8,128)(2,1)S(1)} %copy-done.13, bf16[128,1024]{1,0:T(8,128)(2,1)} %collective-permute-done.1, bf16[1,128,1024]{2,1,0:T(8,128)(2,1)} %reduce-scatter.2.cloned.1.call-done, f32[1024]{0:T(1024)S(1)} %bitcast.33, f32[128]{0:T(128)S(1)} %bitcast.29, pred[1024]{0:T(1024)(128)(4,1)S(1)} %compare_reduce_fusion), kind=kLoop, calls=%fused_computation.4 | loop fusion | flops 1572864 | bytes 1054208 | tf_op jit(solution)/shard_map/convert_element_type | solution.py:409
  152.6 3.8 %collective-permute-done.4 = bf16[512,128]{1,0:T(8,128)(2,1)S(1)} collective-permute-done((bf16[512,128]{1,0:T(8,128)(2,1)S(1)}, bf16[512,128]{1,0:T(8,128)(2,1)S(1)}, u32[]{:S(2)}, u32[]{:S(2)}) %collective-permute-start.4) | collective-permute-done | bytes 131104 | tf_op jit(solution)/shard_map/ppermute | solution.py:353
  156.5 0.7 fusion.3
  (11 shorter events, 0.1 us)
Async XLA Ops:
  7.2 15.3 %copy-start = (bf16[8192,128]{1,0:T(8,128)(2,1)S(1)}, bf16[8192,128]{1,0:T(8,128)(2,1)}, u32[]{:S(2)}) copy-start(bf16[8192,128]{1,0:T(8,128)(2,1)} %w_ref.7) | copy-start | bytes 6291460
  7.2 15.3 %copy-start.9 = (bf16[128,128]{1,0:T(8,128)(2,1)S(1)}, bf16[128,128]{1,0:T(8,128)(2,1)}, u32[]{:S(2)}) copy-start(bf16[128,128]{1,0:T(8,128)(2,1)} %dv_ref.7) | copy-start | bytes 98308
  7.2 15.2 %copy-start.8 = (bf16[128,128]{1,0:T(8,128)(2,1)S(1)}, bf16[128,128]{1,0:T(8,128)(2,1)}, u32[]{:S(2)}) copy-start(bf16[128,128]{1,0:T(8,128)(2,1)} %r2_ref.5) | copy-start | bytes 98308
  7.2 15.2 %copy-start.11 = (f32[1,1024]{1,0:T(1,128)S(1)}, f32[1,1024]{1,0:T(1,128)}, u32[]{:S(2)}) copy-start(f32[1,1024]{1,0:T(1,128)} %scale_ref.1) | copy-start | bytes 12292
  7.2 56.1 %all-gather.3.cloned.1.call-start = ((), (), s32[]{:S(2)}) async-start(), calls=%async_computation.6 | async-start | bytes 1310720 | tf_op jit(solution)/shard_map/all_gather | solution.py:369
  7.8 14.6 %copy-start.10 = (s32[2]{0:T(128)S(1)}, s32[2]{0:T(128)}, u32[]{:S(2)}) copy-start(s32[2]{0:T(128)} %pad_add_fusion.core_ref.place_ref) | copy-start | bytes 28
  11.7 10.7 %collective-permute-start = (bf16[2320,128]{1,0:T(8,128)(2,1)}, bf16[2320,128]{1,0:T(8,128)(2,1)}, u32[]{:S(2)}, u32[]{:S(2)}) collective-permute-start(bf16[2320,128]{1,0:T(8,128)(2,1)} %core_inputs.1.sq_ref), channel_id=1, source_target_pairs={{0,1},{1,0},{2,3},{3,2},{4,5},{5,4},{6,7},{7,6},{8,9},{9,8},{10,11... | collective-permute-start | bytes 1781768 | tf_op jit(solution)/shard_map/ppermute | solution.py:353
  22.4 1.1 copy-start.7
  23.5 8.0 %copy-start.14 = (s32[1,128]{1,0:T(1,128)S(1)}, s32[1,128]{1,0:T(1,128)}, u32[]{:S(2)}) copy-start(s32[1,128]{1,0:T(1,128)} %param.13) | copy-start | bytes 1540
  28.1 29.9 %all-to-all-start = ((bf16[4,144,512]{2,1,0:T(8,128)(2,1)}), bf16[4,144,512]{2,1,0:T(8,128)(2,1)S(1)}, u32[]{:S(2)}, u32[]{:S(2)}) async-start(bf16[4,144,512]{2,1,0:T(8,128)(2,1)} %frame_pairs.1), calls=%async_computation | async-start | bytes 1179648 | tf_op jit(solution)/shard_map/all_to_all | solution.py:348
  38.3 1.3 copy-start.2
  57.9 1.2 copy-start.5
  59.1 14.4 %all-to-all-start.1 = ((bf16[8,128,512]{2,1,0:T(8,128)(2,1)}), bf16[8,128,512]{2,1,0:T(8,128)(2,1)S(1)}, u32[]{:S(2)}, u32[]{:S(2)}) async-start(bf16[8,128,512]{2,1,0:T(8,128)(2,1)} %broadcast_in_dim.20), calls=%async_computation.1 | async-start | bytes 2097152 | tf_op jit(solution)/shard_map/all_to_all | solution.py:348
  63.3 1.1 copy-start.6
  64.4 1.2 copy-start.12
  68.2 1.0 copy-start.3
  73.5 14.7 %all-to-all-start.2 = ((bf16[8,128,512]{2,1,0:T(8,128)(2,1)}), bf16[8,128,512]{2,1,0:T(8,128)(2,1)}, u32[]{:S(2)}, u32[]{:S(2)}) async-start(bf16[8,128,512]{2,1,0:T(8,128)(2,1)} %copy-done.3), calls=%async_computation.2 | async-start | bytes 2097152 | tf_op jit(solution)/shard_map/all_to_all | solution.py:348
  77.8 72.8 %reduce-scatter.2.cloned.1.call-start = ((), (), s32[]{:S(2)}) async-start(), calls=%async_computation.5 | async-start | bytes 2359296 | tf_op jit(solution)/shard_map/reduce_scatter | solution.py:390
  88.2 11.7 %collective-permute-start.2 = (bf16[8,128,512]{2,1,0:T(8,128)(2,1)}, bf16[8,128,512]{2,1,0:T(8,128)(2,1)}, u32[]{:S(2)}, u32[]{:S(2)}) collective-permute-start(bf16[8,128,512]{2,1,0:T(8,128)(2,1)} %all-to-all-done.2), channel_id=1, source_target_pairs={{0,1},{1,0},{2,3},{3,2},{4,5},{5,4},{6,7},{7,6},{8,9},{9,8},{10,11... | collective-permute-start | bytes 3145736 | tf_op jit(solution)/shard_map/ppermute | solution.py:353
  102.4 1.0 copy-start.1
  103.4 7.6 %copy-start.4 = (bf16[8,128,512]{2,1,0:T(8,128)(2,1)S(1)}, bf16[8,128,512]{2,1,0:T(8,128)(2,1)}, u32[]{:S(2)}) copy-start(bf16[8,128,512]{2,1,0:T(8,128)(2,1)} %copy-done.3) | copy-start | bytes 3145732
  103.4 32.6 %all-to-all-start.3 = ((bf16[8,512,128]{2,1,0:T(8,128)(2,1)}), bf16[8,512,128]{2,1,0:T(8,128)(2,1)}, u32[]{:S(2)}, u32[]{:S(2)}) async-start(bf16[8,512,128]{2,1,0:T(8,128)(2,1)} %copy-done.1), calls=%async_computation.4 | async-start | bytes 2097152 | tf_op jit(solution)/shard_map/all_to_all | solution.py:348
  111.0 12.7 %collective-permute-start.3 = (bf16[8,128,512]{2,1,0:T(8,128)(2,1)S(1)}, bf16[8,128,512]{2,1,0:T(8,128)(2,1)}, u32[]{:S(2)}, u32[]{:S(2)}) collective-permute-start(bf16[8,128,512]{2,1,0:T(8,128)(2,1)S(1)} %copy-done.4), channel_id=1, source_target_pairs={{0,1},{1,0},{2,3},{3,2},{4,5},{5,4},{6,7},{7,6},{8,9},{9,8},{10,11... | collective-permute-start | bytes 3145736 | tf_op jit(solution)/shard_map/ppermute | solution.py:353
  113.5 37.0 %collective-permute-start.1 = (bf16[128,1024]{1,0:T(8,128)(2,1)}, bf16[128,1024]{1,0:T(8,128)(2,1)}, u32[]{:S(2)}, u32[]{:S(2)}) collective-permute-start(bf16[128,1024]{1,0:T(8,128)(2,1)} %param.8), channel_id=1, source_target_pairs={{0,504},{8,0},{16,8},{24,16},{32,24},{40,32},{48,40},{56,48},{64,5... | collective-permute-start | bytes 786440 | tf_op jit(solution)/shard_map/ppermute | solution.py:396
  123.7 26.9 %copy-start.13 = (bf16[128,1024]{1,0:T(8,128)(2,1)S(1)}, bf16[128,1024]{1,0:T(8,128)(2,1)}, u32[]{:S(2)}) copy-start(bf16[128,1024]{1,0:T(8,128)(2,1)} %x_ref.1) | copy-start | bytes 786436
  137.5 19.0 %collective-permute-start.4 = (bf16[512,128]{1,0:T(8,128)(2,1)S(1)}, bf16[512,128]{1,0:T(8,128)(2,1)S(1)}, u32[]{:S(2)}, u32[]{:S(2)}) collective-permute-start(bf16[512,128]{1,0:T(8,128)(2,1)S(1)} %fusion.4), channel_id=1, source_target_pairs={{0,8},{8,0},{1,9},{9,1},{2,10},{10,2},{3,11},{11,3},{4,12},{12,4},... | collective-permute-start | bytes 393224 | tf_op jit(solution)/shard_map/ppermute | solution.py:353
Sparse Core Ops, SparseCore 0:
  20.6 42.6 all-gather.2
  81.5 55.1 reduce-scatter.1

commit v9 on v4

--- a/solution.py
+++ b/solution.py
@@ -13,6 +13,7 @@
 SCALE_FLOOR = 1e-06
 TP = 8
 BIG = 32 << 20
+WHOLE = 60 << 20
 CHEAP = pl.CostEstimate(flops=1, bytes_accessed=1, transcendentals=0)
 LONG = pl.CostEstimate(flops=23_000_000_000, bytes_accessed=1, transcendentals=0)
 SEC = ("x", "zh", "zl", "yh")
@@ -122,7 +123,7 @@
             ],
         ),
         out_shape=[jax.ShapeDtypeStruct((1, 128), jnp.float32), half, half],
-        compiler_params=pltpu.CompilerParams(vmem_limit_bytes=BIG),
+        compiler_params=pltpu.CompilerParams(vmem_limit_bytes=WHOLE),
         cost_estimate=LONG,
         name="frame_parts",
     )(core, weight, rotor, value_grad)

time: 155 us -> 156 us (level)
  local copies, waits for them, and re-layouts: 9.02 us -> 5.92 us
  Pallas kernels: 20.9 us -> 22.9 us
    unnamed x28 -> x26, local copies, waits for them, and re-layouts: 7.94 us -> 4.86 us
    pallas_call x1, Pallas kernels: 3.21 us -> 5.31 us  [frame_parts(): pl.pallas_call(frame_kernel, grid_spec=pltpu.PrefetchScalarGridSpec(num_s...]
  transfers between devices with their start and end apart: 14 -> 14, of which waited for: 10 -> 9; matrix products, arithmetic and copies ran while one was open for 3% -> 4% of each run, Pallas kernels for 11% -> 11%
where the time goes in v9:
time: 156 us; the launch traced here: 155 us
  waiting for transfers between devices  61.5 us (39%)
  starting transfers between devices  44.7 us (29%)
  Pallas kernels  22.9 us (15%)
  between operations  14.3 us (9%)
  local copies, waits for them, and re-layouts  5.92 us (4%)
  other arithmetic  5.72 us (4%)
    all_to_all x4, waiting for transfers between devices, exchange(): return lax.all_to_all(value, axes, split_axis=0, concat_axis=0, tiled=True)  36.8 us
    all_to_all x4, starting transfers between devices, exchange(): return lax.all_to_all(value, axes, split_axis=0, concat_axis=0, tiled=True)  27 us
    ppermute x5, waiting for transfers between devices, shifted(): lax.ppermute(value, axis, [(chip, (chip + turn) % count) for chip in rang...  15.3 us
    ppermute x5, starting transfers between devices, shifted(): lax.ppermute(value, axis, [(chip, (chip + turn) % count) for chip in rang...  9.7 us
    ppermute x2, waiting for transfers between devices, flipped(): return lax.ppermute(value, 'yl', [(chip, chip ^ bit) for chip in range(4)])  8.63 us
    pallas_call x2, Pallas kernels, outer(): pl.pallas_call(outer_kernel, grid_spec=pltpu.PrefetchScalarGridSpec(num_s...  5.6 us
    pallas_call x1, Pallas kernels, weight_grad(): pl.pallas_call(weight_grad_kernel, grid=(8,), in_specs=[pl.BlockSpec((102...  5.35 us
    pallas_call x1, Pallas kernels, frame_parts(): pl.pallas_call(frame_kernel, grid_spec=pltpu.PrefetchScalarGridSpec(num_s...  5.31 us
  transfers between devices with their start and end apart: 14, of which 9 were waited for; matrix products, arithmetic and copies ran while one was open for 4% of the time, Pallas kernels for 11%

profile of v9, /device:TPU:48, one launch (start us, length us, event | category | flops | bytes accessed | tf_op | source)
XLA Modules:
  0.0 155.2 jit_solution(8707428126151450107)
XLA Ops:
  7.2 0.0 all-gather.3.cloned.1.call-start
  7.2 0.6 pad_add_fusion.core_ref.place_ref
  7.8 0.0 copy-start.4
  7.8 5.3 %frame_parts.1 = (f32[1,128]{1,0:T(1,128)}, bf16[4,128,512]{2,1,0:T(8,128)(2,1)}, bf16[4,128,512]{2,1,0:T(8,128)(2,1)}) custom-call(s32[2]{0:T(128)} %pad_add_fusion.core_ref.place_ref, bf16[8192,128]{1,0:T(8,128)(2,1)} %w_ref.5, bf16[128,128]{1,0:T(8,128)(2,1)} %r2_ref.3, bf16[128,128]{1,0:T(8,128)(2,1)} %dv_ref.5), custom_call_target="tpu_custom_call" | custom-call | flops 23000000512 | bytes 1 | tf_op jit(solution)/shard_map/frame_parts/pallas_call | solution.py:109
  13.1 1.9 %collective-permute-start = (bf16[4,128,512]{2,1,0:T(8,128)(2,1)}, bf16[4,128,512]{2,1,0:T(8,128)(2,1)S(1)}, u32[]{:S(2)}, u32[]{:S(2)}) collective-permute-start(bf16[4,128,512]{2,1,0:T(8,128)(2,1)} %get-tuple-element.20), channel_id=1, source_target_pairs={{0,1},{1,0},{2,3},{3,2},{4,5},{5,4},{6,7},{7,6},{8,9},{9,8},{10,11... | collective-permute-start | bytes 1572872 | tf_op jit(solution)/shard_map/ppermute | solution.py:308
  15.0 0.0 copy-done.4
  15.0 0.0 copy-done.7
  15.0 0.8 prepare.1
  15.8 0.0 all-gather.3.cloned.1.call-update
  15.8 1.3 collective-permute-done
  17.1 2.0 %add_convert_fusion = bf16[4,128,512]{2,1,0:T(8,128)(2,1)} fusion(bf16[4,128,512]{2,1,0:T(8,128)(2,1)S(1)} %collective-permute-done, bf16[4,128,512]{2,1,0:T(8,128)(2,1)} %get-tuple-element.19), kind=kLoop, calls=%fused_computation.1 | loop fusion | flops 1048576 | bytes 1572864 | tf_op jit(solution)/shard_map/convert_element_type | solution.py:331
  19.1 5.6 %all-to-all-start = ((bf16[4,128,512]{2,1,0:T(8,128)(2,1)}), bf16[4,128,512]{2,1,0:T(8,128)(2,1)S(1)}, u32[]{:S(2)}, u32[]{:S(2)}) async-start(bf16[4,128,512]{2,1,0:T(8,128)(2,1)} %add_convert_fusion), calls=%async_computation | async-start | bytes 1048576 | tf_op jit(solution)/shard_map/all_to_all | solution.py:303
  24.7 0.1 multiply_reduce_fusion
  24.8 2.0 %collective-permute-start.1 = (f32[1,128]{1,0:T(1,128)S(1)}, f32[1,128]{1,0:T(1,128)S(1)}, u32[]{:S(2)}, u32[]{:S(2)}) collective-permute-start(f32[1,128]{1,0:T(1,128)S(1)} %bitcast.39), channel_id=1, source_target_pairs={{0,1},{1,0},{2,3},{3,2},{4,5},{5,4},{6,7},{7,6},{8,9},{9,8},{10,11... | collective-permute-start | bytes 1544 | tf_op jit(solution)/shard_map/ppermute | solution.py:308
  26.8 1.1 collective-permute-done.1
  27.9 3.4 %collective-permute-start.2 = (f32[1,128]{1,0:T(1,128)S(1)}, f32[1,128]{1,0:T(1,128)S(1)}, u32[]{:S(2)}, u32[]{:S(2)}) collective-permute-start(f32[1,128]{1,0:T(1,128)S(1)} %bitcast_add_fusion), channel_id=1, source_target_pairs={{0,2},{2,0},{4,6},{6,4},{1,3},{3,1},{5,7},{7,5},{8,10},{10,8},{12,... | collective-permute-start | bytes 1544 | tf_op jit(solution)/shard_map/ppermute | solution.py:316
  31.3 4.2 %collective-permute-done.2 = f32[1,128]{1,0:T(1,128)S(1)} collective-permute-done((f32[1,128]{1,0:T(1,128)S(1)}, f32[1,128]{1,0:T(1,128)S(1)}, u32[]{:S(2)}, u32[]{:S(2)}) %collective-permute-start.2) | collective-permute-done | bytes 544 | tf_op jit(solution)/shard_map/ppermute | solution.py:316
  35.5 1.9 %collective-permute-start.3 = (f32[1,128]{1,0:T(1,128)S(1)}, f32[1,128]{1,0:T(1,128)S(1)}, u32[]{:S(2)}, u32[]{:S(2)}) collective-permute-start(f32[1,128]{1,0:T(1,128)S(1)} %add.47), channel_id=1, source_target_pairs={{0,4},{2,6},{4,0},{6,2},{1,5},{3,7},{5,1},{7,3},{8,12},{10,14},{12... | collective-permute-start | bytes 1544 | tf_op jit(solution)/shard_map/ppermute | solution.py:316
  37.5 4.4 %collective-permute-done.3 = f32[1,128]{1,0:T(1,128)S(1)} collective-permute-done((f32[1,128]{1,0:T(1,128)S(1)}, f32[1,128]{1,0:T(1,128)S(1)}, u32[]{:S(2)}, u32[]{:S(2)}) %collective-permute-start.3) | collective-permute-done | bytes 544 | tf_op jit(solution)/shard_map/ppermute | solution.py:316
  41.9 0.0 all-to-all-done
  41.9 0.1 reduce_sum.31
  42.0 1.0 broadcast_in_dim.20
  43.0 6.2 %all-to-all-start.1 = ((bf16[8,128,512]{2,1,0:T(8,128)(2,1)}), bf16[8,128,512]{2,1,0:T(8,128)(2,1)S(1)}, u32[]{:S(2)}, u32[]{:S(2)}) async-start(bf16[8,128,512]{2,1,0:T(8,128)(2,1)} %broadcast_in_dim.20), calls=%async_computation.1 | async-start | bytes 2097152 | tf_op jit(solution)/shard_map/all_to_all | solution.py:303
  49.2 0.0 copy-done.12
  49.3 0.2 fusion.5
  49.5 0.0 copy-done
  49.5 0.0 copy-done.5
  49.5 0.7 rest_top.1.two_ref
  50.2 0.0 copy-done.6
  50.2 0.0 copy-done.9
  50.2 0.0 copy-start.8
  50.2 5.3 %weight_grad.1 = bf16[8,128,1024]{2,1,0:T(8,128)(2,1)S(1)} custom-call(bf16[8192,128]{1,0:T(8,128)(2,1)S(1)} %copy-done, bf16[128,128]{1,0:T(8,128)(2,1)S(1)} %copy-done.5, f32[1,128]{1,0:T(1,128)S(1)} %copy-done.9, f32[1,128]{1,0:T(1,128)S(1)} %rest_top.1.two_ref, bf16[128,128]{1,0:T(8,128)(2,1)S(1)} %copy-done.6), custom_call_target="tpu_custom_call" | custom-call | flops 1 | bytes 1 | tf_op jit(solution)/shard_map/weight_grad/pallas_call | solution.py:162
  55.6 0.0 copy-start.1
  55.6 1.3 copy-done.1
  56.9 0.0 copy-done.8
  56.9 1.3 copy-done.10
  58.2 2.5 %quantize.1.mine_ref = bf16[8,128,512]{2,1,0:T(8,128)(2,1)S(1)} custom-call(s32[2]{0:T(128)S(1)} %copy-done.8, bf16[4,144,1024]{2,1,0:T(8,128)(2,1)S(1)} %bitcast.36, f32[8,1,1024]{2,1,0:T(1,128)S(1)} %bitcast.34, f32[1,128]{1,0:T(1,128)S(1)} %add_rsqrt_fusion.inv_ref), custom_call_target="tpu_custom_call" | custom-call | flops 10350000128 | bytes 1 | tf_op jit(solution)/shard_map/quantize/pallas_call | solution.py:192
  60.7 0.0 copy-start.2
  60.7 1.0 copy-done.2
  61.7 1.7 %all-to-all-done.1 = bf16[8,128,512]{2,1,0:T(8,128)(2,1)S(1)} async-done(((bf16[8,128,512]{2,1,0:T(8,128)(2,1)}), bf16[8,128,512]{2,1,0:T(8,128)(2,1)S(1)}, u32[]{:S(2)}, u32[]{:S(2)}) %all-to-all-start.1) | async-done | bytes 1048608 | tf_op jit(solution)/shard_map/all_to_all | solution.py:303
  63.4 4.2 %all-to-all-start.2 = ((bf16[8,128,512]{2,1,0:T(8,128)(2,1)}), bf16[8,128,512]{2,1,0:T(8,128)(2,1)}, u32[]{:S(2)}, u32[]{:S(2)}) async-start(bf16[8,128,512]{2,1,0:T(8,128)(2,1)} %copy-done.2), calls=%async_computation.2 | async-start | bytes 2097152 | tf_op jit(solution)/shard_map/all_to_all | solution.py:303
  67.7 0.0 reduce-scatter.2.cloned.1.call-start
  67.7 0.7 reduce-scatter.2.cloned.1.call-update
  68.4 1.9 %collective-permute-start.4 = (bf16[8,128,512]{2,1,0:T(8,128)(2,1)}, bf16[8,128,512]{2,1,0:T(8,128)(2,1)S(1)}, u32[]{:S(2)}, u32[]{:S(2)}) collective-permute-start(bf16[8,128,512]{2,1,0:T(8,128)(2,1)} %copy-done.2), channel_id=1, source_target_pairs={{0,1},{1,0},{2,3},{3,2},{4,5},{5,4},{6,7},{7,6},{8,9},{9,8},{10,11... | collective-permute-start | bytes 3145736 | tf_op jit(solution)/shard_map/ppermute | solution.py:308
  70.4 2.8 %collective-permute-done.4.other_ref = bf16[8,128,512]{2,1,0:T(8,128)(2,1)S(1)} collective-permute-done((bf16[8,128,512]{2,1,0:T(8,128)(2,1)}, bf16[8,128,512]{2,1,0:T(8,128)(2,1)S(1)}, u32[]{:S(2)}, u32[]{:S(2)}) %collective-permute-start.4) | collective-permute-done | bytes 1048608 | tf_op jit(solution)/shard_map/ppermute | solution.py:308
  73.2 1.2 copy-done.3
  74.4 2.7 %rotor_grad.1 = f32[128,128]{1,0:T(8,128)} custom-call(s32[2]{0:T(128)S(1)} %copy-done.8, bf16[8,128,512]{2,1,0:T(8,128)(2,1)S(1)} %copy-done.3, bf16[8,128,512]{2,1,0:T(8,128)(2,1)S(1)} %collective-permute-done.4.other_ref, bf16[8,1024,128]{2,1,0:T(8,128)(2,1)S(1)} %bitcast.28, bf16[8,1024,128]{2,1,0:T(8,128)(2,1)S(1)} %bitcast.29, ...), custom_call_target="tpu_custom_call" | custom-call | flops 1 | bytes 1 | tf_op jit(solution)/shard_map/rotor_grad/pallas_call | solution.py:246
  77.1 5.8 %all-to-all-done.2 = bf16[8,128,512]{2,1,0:T(8,128)(2,1)} async-done(((bf16[8,128,512]{2,1,0:T(8,128)(2,1)}), bf16[8,128,512]{2,1,0:T(8,128)(2,1)}, u32[]{:S(2)}, u32[]{:S(2)}) %all-to-all-start.2) | async-done | bytes 1048608 | tf_op jit(solution)/shard_map/all_to_all | solution.py:303
  82.9 1.9 %collective-permute-start.6 = (bf16[8,128,512]{2,1,0:T(8,128)(2,1)}, bf16[8,128,512]{2,1,0:T(8,128)(2,1)S(1)}, u32[]{:S(2)}, u32[]{:S(2)}) collective-permute-start(bf16[8,128,512]{2,1,0:T(8,128)(2,1)} %all-to-all-done.2), channel_id=1, source_target_pairs={{0,1},{1,0},{2,3},{3,2},{4,5},{5,4},{6,7},{7,6},{8,9},{9,8},{10,11... | collective-permute-start | bytes 3145736 | tf_op jit(solution)/shard_map/ppermute | solution.py:308
  84.8 0.1 pad_add_fusion.1.place_ref
  84.9 3.3 %outer.1.rest_0_ = bf16[8,512,128]{2,1,0:T(8,128)(2,1)} custom-call(s32[2]{0:T(128)S(1)} %copy-done.8, bf16[1024,512]{1,0:T(8,128)(2,1)S(1)} %bitcast.30, bf16[1024,512]{1,0:T(8,128)(2,1)} %bitcast.14.quant_ref), custom_call_target="tpu_custom_call" | custom-call | flops 1 | bytes 1 | tf_op jit(solution)/shard_map/outer/pallas_call | solution.py:282
  88.2 0.0 collective-permute-done.6
  88.2 2.3 %outer_other.1 = bf16[8,512,128]{2,1,0:T(8,128)(2,1)} custom-call(s32[2]{0:T(128)S(1)} %pad_add_fusion.1.place_ref, bf16[1024,512]{1,0:T(8,128)(2,1)S(1)} %bitcast.31, bf16[1024,512]{1,0:T(8,128)(2,1)S(1)} %bitcast.32, bf16[8,512,128]{2,1,0:T(8,128)(2,1)} %outer.1.rest_0_), custom_call_target="tpu_custom_call", output_to_operand_aliasing={{}: (3, {})} | custom-call | flops 1 | bytes 1 | tf_op jit(solution)/shard_map/outer_other/pallas_call | solution.py:282
  90.5 10.9 %all-to-all-start.3 = ((bf16[8,512,128]{2,1,0:T(8,128)(2,1)}), bf16[8,512,128]{2,1,0:T(8,128)(2,1)S(1)}, u32[]{:S(2)}, u32[]{:S(2)}) async-start(bf16[8,512,128]{2,1,0:T(8,128)(2,1)} %outer_other.1), calls=%async_computation.4 | async-start | bytes 2097152 | tf_op jit(solution)/shard_map/all_to_all | solution.py:303
  101.5 0.0 copy-done.11
  101.5 2.6 %collective-permute-start.5 = (bf16[128,1024]{1,0:T(8,128)(2,1)S(1)}, bf16[128,1024]{1,0:T(8,128)(2,1)S(1)}, u32[]{:S(2)}, u32[]{:S(2)}) collective-permute-start(bf16[128,1024]{1,0:T(8,128)(2,1)S(1)} %copy-done.11), channel_id=1, source_target_pairs={{0,504},{8,0},{16,8},{24,16},{32,24},{40,32},{48,40},{56,48},{64,5... | collective-permute-start | bytes 786440 | tf_op jit(solution)/shard_map/ppermute | solution.py:358
  104.1 29.3 %all-to-all-done.3 = bf16[8,512,128]{2,1,0:T(8,128)(2,1)S(1)} async-done(((bf16[8,512,128]{2,1,0:T(8,128)(2,1)}), bf16[8,512,128]{2,1,0:T(8,128)(2,1)S(1)}, u32[]{:S(2)}, u32[]{:S(2)}) %all-to-all-start.3) | async-done | bytes 1048608 | tf_op jit(solution)/shard_map/all_to_all | solution.py:303
  133.5 0.1 convert_reduce_fusion
  133.6 1.9 %collective-permute-start.7 = (bf16[512,128]{1,0:T(8,128)(2,1)S(1)}, bf16[512,128]{1,0:T(8,128)(2,1)S(1)}, u32[]{:S(2)}, u32[]{:S(2)}) collective-permute-start(bf16[512,128]{1,0:T(8,128)(2,1)S(1)} %fusion.4), channel_id=1, source_target_pairs={{0,8},{8,0},{1,9},{9,1},{2,10},{10,2},{3,11},{11,3},{4,12},{12,4},... | collective-permute-start | bytes 393224 | tf_op jit(solution)/shard_map/ppermute | solution.py:308
  135.6 0.0 collective-permute-done.5
  135.6 0.0 reduce-scatter.2.cloned.1.call-done
  135.6 1.9 %fusion.2 = bf16[128,1024]{1,0:T(8,128)(2,1)} fusion(bf16[128,1024]{1,0:T(8,128)(2,1)S(1)} %copy-done.4, bf16[128,1024]{1,0:T(8,128)(2,1)S(1)} %collective-permute-done.5, bf16[1,128,1024]{2,1,0:T(8,128)(2,1)} %reduce-scatter.2.cloned.1.call-done, f32[1024]{0:T(1024)S(1)} %bitcast.38, f32[128]{0:T(128)S(1)} %bitcast.33, pred[1024]{0:T(1024)(128)(4,1)S(1)} %compare_reduce_fusion), kind=kLoop, calls=%fused_computation.5 | loop fusion | flops 1572864 | bytes 1054208 | tf_op jit(solution)/shard_map/convert_element_type | solution.py:370
  137.6 10.1 %collective-permute-done.7 = bf16[512,128]{1,0:T(8,128)(2,1)S(1)} collective-permute-done((bf16[512,128]{1,0:T(8,128)(2,1)S(1)}, bf16[512,128]{1,0:T(8,128)(2,1)S(1)}, u32[]{:S(2)}, u32[]{:S(2)}) %collective-permute-start.7) | collective-permute-done | bytes 131104 | tf_op jit(solution)/shard_map/ppermute | solution.py:308
  147.6 0.7 fusion.3
  (18 shorter events, 0.1 us)
Async XLA Ops:
  7.2 49.7 %all-gather.3.cloned.1.call-start = ((), (), s32[]{:S(2)}) async-start(), calls=%async_computation.6 | async-start | bytes 1474560 | tf_op jit(solution)/shard_map/all_gather | solution.py:328
  7.8 7.2 %copy-start.4 = (bf16[128,1024]{1,0:T(8,128)(2,1)S(1)}, bf16[128,1024]{1,0:T(8,128)(2,1)}, u32[]{:S(2)}) copy-start(bf16[128,1024]{1,0:T(8,128)(2,1)} %x_ref.1) | copy-start | bytes 786436
  7.8 7.2 %copy-start.7 = (f32[1,1024]{1,0:T(1,128)S(1)}, f32[1,1024]{1,0:T(1,128)}, u32[]{:S(2)}) copy-start(f32[1,1024]{1,0:T(1,128)} %scale_ref.1) | copy-start | bytes 12292
  13.1 4.0 %collective-permute-start = (bf16[4,128,512]{2,1,0:T(8,128)(2,1)}, bf16[4,128,512]{2,1,0:T(8,128)(2,1)S(1)}, u32[]{:S(2)}, u32[]{:S(2)}) collective-permute-start(bf16[4,128,512]{2,1,0:T(8,128)(2,1)} %get-tuple-element.20), channel_id=1, source_target_pairs={{0,1},{1,0},{2,3},{3,2},{4,5},{5,4},{6,7},{7,6},{8,9},{9,8},{10,11... | collective-permute-start | bytes 1572872 | tf_op jit(solution)/shard_map/ppermute | solution.py:308
  19.1 22.8 %all-to-all-start = ((bf16[4,128,512]{2,1,0:T(8,128)(2,1)}), bf16[4,128,512]{2,1,0:T(8,128)(2,1)S(1)}, u32[]{:S(2)}, u32[]{:S(2)}) async-start(bf16[4,128,512]{2,1,0:T(8,128)(2,1)} %add_convert_fusion), calls=%async_computation | async-start | bytes 1048576 | tf_op jit(solution)/shard_map/all_to_all | solution.py:303
  24.7 24.6 %copy-start.12 = (s32[1,128]{1,0:T(1,128)S(1)}, s32[1,128]{1,0:T(1,128)}, u32[]{:S(2)}) copy-start(s32[1,128]{1,0:T(1,128)} %param.13) | copy-start | bytes 1540
  24.7 24.8 %copy-start = (bf16[8192,128]{1,0:T(8,128)(2,1)S(1)}, bf16[8192,128]{1,0:T(8,128)(2,1)}, u32[]{:S(2)}) copy-start(bf16[8192,128]{1,0:T(8,128)(2,1)} %w_ref.5) | copy-start | bytes 6291460
  24.7 24.8 %copy-start.5 = (bf16[128,128]{1,0:T(8,128)(2,1)S(1)}, bf16[128,128]{1,0:T(8,128)(2,1)}, u32[]{:S(2)}) copy-start(bf16[128,128]{1,0:T(8,128)(2,1)} %r2_ref.3) | copy-start | bytes 98308
  24.8 3.1 %collective-permute-start.1 = (f32[1,128]{1,0:T(1,128)S(1)}, f32[1,128]{1,0:T(1,128)S(1)}, u32[]{:S(2)}, u32[]{:S(2)}) collective-permute-start(f32[1,128]{1,0:T(1,128)S(1)} %bitcast.39), channel_id=1, source_target_pairs={{0,1},{1,0},{2,3},{3,2},{4,5},{5,4},{6,7},{7,6},{8,9},{9,8},{10,11... | collective-permute-start | bytes 1544 | tf_op jit(solution)/shard_map/ppermute | solution.py:308
  27.9 7.6 %collective-permute-start.2 = (f32[1,128]{1,0:T(1,128)S(1)}, f32[1,128]{1,0:T(1,128)S(1)}, u32[]{:S(2)}, u32[]{:S(2)}) collective-permute-start(f32[1,128]{1,0:T(1,128)S(1)} %bitcast_add_fusion), channel_id=1, source_target_pairs={{0,2},{2,0},{4,6},{6,4},{1,3},{3,1},{5,7},{7,5},{8,10},{10,8},{12,... | collective-permute-start | bytes 1544 | tf_op jit(solution)/shard_map/ppermute | solution.py:316
  35.5 6.3 %collective-permute-start.3 = (f32[1,128]{1,0:T(1,128)S(1)}, f32[1,128]{1,0:T(1,128)S(1)}, u32[]{:S(2)}, u32[]{:S(2)}) collective-permute-start(f32[1,128]{1,0:T(1,128)S(1)} %add.47), channel_id=1, source_target_pairs={{0,4},{2,6},{4,0},{6,2},{1,5},{3,7},{5,1},{7,3},{8,12},{10,14},{12... | collective-permute-start | bytes 1544 | tf_op jit(solution)/shard_map/ppermute | solution.py:316
  43.0 7.2 %copy-start.6 = (bf16[128,128]{1,0:T(8,128)(2,1)S(1)}, bf16[128,128]{1,0:T(8,128)(2,1)}, u32[]{:S(2)}) copy-start(bf16[128,128]{1,0:T(8,128)(2,1)} %dv_ref.5) | copy-start | bytes 98308
  43.0 7.2 %copy-start.9 = (f32[1,128]{1,0:T(1,128)S(1)}, f32[1,128]{1,0:T(1,128)}, u32[]{:S(2)}) copy-start(f32[1,128]{1,0:T(1,128)} %get-tuple-element.25.one_ref) | copy-start | bytes 1540
  43.0 20.4 %all-to-all-start.1 = ((bf16[8,128,512]{2,1,0:T(8,128)(2,1)}), bf16[8,128,512]{2,1,0:T(8,128)(2,1)S(1)}, u32[]{:S(2)}, u32[]{:S(2)}) async-start(bf16[8,128,512]{2,1,0:T(8,128)(2,1)} %broadcast_in_dim.20), calls=%async_computation.1 | async-start | bytes 2097152 | tf_op jit(solution)/shard_map/all_to_all | solution.py:303
  50.2 6.7 %copy-start.8 = (s32[2]{0:T(128)S(1)}, s32[2]{0:T(128)}, u32[]{:S(2)}) copy-start(s32[2]{0:T(128)} %pad_add_fusion.core_ref.place_ref) | copy-start | bytes 28
  55.6 1.3 copy-start.1
  56.9 1.3 copy-start.10
  60.7 1.0 copy-start.2
  63.4 19.5 %all-to-all-start.2 = ((bf16[8,128,512]{2,1,0:T(8,128)(2,1)}), bf16[8,128,512]{2,1,0:T(8,128)(2,1)}, u32[]{:S(2)}, u32[]{:S(2)}) async-start(bf16[8,128,512]{2,1,0:T(8,128)(2,1)} %copy-done.2), calls=%async_computation.2 | async-start | bytes 2097152 | tf_op jit(solution)/shard_map/all_to_all | solution.py:303
  67.7 67.9 %reduce-scatter.2.cloned.1.call-start = ((), (), s32[]{:S(2)}) async-start(), calls=%async_computation.5 | async-start | bytes 2359296 | tf_op jit(solution)/shard_map/reduce_scatter | solution.py:351
  68.4 4.8 %collective-permute-start.4 = (bf16[8,128,512]{2,1,0:T(8,128)(2,1)}, bf16[8,128,512]{2,1,0:T(8,128)(2,1)S(1)}, u32[]{:S(2)}, u32[]{:S(2)}) collective-permute-start(bf16[8,128,512]{2,1,0:T(8,128)(2,1)} %copy-done.2), channel_id=1, source_target_pairs={{0,1},{1,0},{2,3},{3,2},{4,5},{5,4},{6,7},{7,6},{8,9},{9,8},{10,11... | collective-permute-start | bytes 3145736 | tf_op jit(solution)/shard_map/ppermute | solution.py:308
  73.2 1.2 copy-start.3
  82.9 5.3 %collective-permute-start.6 = (bf16[8,128,512]{2,1,0:T(8,128)(2,1)}, bf16[8,128,512]{2,1,0:T(8,128)(2,1)S(1)}, u32[]{:S(2)}, u32[]{:S(2)}) collective-permute-start(bf16[8,128,512]{2,1,0:T(8,128)(2,1)} %all-to-all-done.2), channel_id=1, source_target_pairs={{0,1},{1,0},{2,3},{3,2},{4,5},{5,4},{6,7},{7,6},{8,9},{9,8},{10,11... | collective-permute-start | bytes 3145736 | tf_op jit(solution)/shard_map/ppermute | solution.py:308
  90.5 11.0 %copy-start.11 = (bf16[128,1024]{1,0:T(8,128)(2,1)S(1)}, bf16[128,1024]{1,0:T(8,128)(2,1)}, u32[]{:S(2)}) copy-start(bf16[128,1024]{1,0:T(8,128)(2,1)} %param.8) | copy-start | bytes 786436
  90.5 43.0 %all-to-all-start.3 = ((bf16[8,512,128]{2,1,0:T(8,128)(2,1)}), bf16[8,512,128]{2,1,0:T(8,128)(2,1)S(1)}, u32[]{:S(2)}, u32[]{:S(2)}) async-start(bf16[8,512,128]{2,1,0:T(8,128)(2,1)} %outer_other.1), calls=%async_computation.4 | async-start | bytes 2097152 | tf_op jit(solution)/shard_map/all_to_all | solution.py:303
  101.5 34.1 %collective-permute-start.5 = (bf16[128,1024]{1,0:T(8,128)(2,1)S(1)}, bf16[128,1024]{1,0:T(8,128)(2,1)S(1)}, u32[]{:S(2)}, u32[]{:S(2)}) collective-permute-start(bf16[128,1024]{1,0:T(8,128)(2,1)S(1)} %copy-done.11), channel_id=1, source_target_pairs={{0,504},{8,0},{16,8},{24,16},{32,24},{40,32},{48,40},{56,48},{64,5... | collective-permute-start | bytes 786440 | tf_op jit(solution)/shard_map/ppermute | solution.py:358
  133.6 14.0 %collective-permute-start.7 = (bf16[512,128]{1,0:T(8,128)(2,1)S(1)}, bf16[512,128]{1,0:T(8,128)(2,1)S(1)}, u32[]{:S(2)}, u32[]{:S(2)}) collective-permute-start(bf16[512,128]{1,0:T(8,128)(2,1)S(1)} %fusion.4), channel_id=1, source_target_pairs={{0,8},{8,0},{1,9},{9,1},{2,10},{10,2},{3,11},{11,3},{4,12},{12,4},... | collective-permute-start | bytes 393224 | tf_op jit(solution)/shard_map/ppermute | solution.py:308
Sparse Core Ops, SparseCore 0:
  16.0 40.2 all-gather.2
  71.4 55.8 reduce-scatter.1
